TPU v7x, 32 devices: a whole 2x2x4 slice. The times are simulated.
32 devices in a mesh: img: 32 (over z, y, x, core).
Axes of the slice: x: 2, y: 2, z: 4, core: 2. Of those that a mesh axis runs over, the one named last changes fastest.
Arguments:
- token_embeddings: bfloat16 [128, 576, 384], P('img')
- upstream_sensitivity: bfloat16 [128, 576, 384], P('img')
- tile_lattice_edges: int32 [128], P('img'), may hold values from 14 to 24, as said below
- opening_standardizer_factor: float32 [384], replicated, may hold values from 0.5 to 1.5
- opening_standardizer_offset: float32 [384], replicated, may hold values from -4 to 4
- projection_triple_matrix: bfloat16 [384, 1152], replicated, may hold values from -0.3125 to 0.3125
- projection_triple_offset: float32 [1152], replicated, may hold values from -4 to 4
- sharpness_factor: float32 [8], replicated, may hold values from 4 to 16
- mixing_exit_matrix: bfloat16 [384, 384], replicated, may hold values from -0.875 to 0.875
- mixing_exit_offset: float32 [384], replicated, may hold values from -4 to 4
- mixing_branch_factor: float32 [384], replicated, may hold values from 0.5 to 1.5
- middle_standardizer_factor: float32 [384], replicated, may hold values from 0.5 to 1.5
- middle_standardizer_offset: float32 [384], replicated, may hold values from -4 to 4
- early_perchannel_stencil: float32 [3, 3, 384], replicated, may hold values from -2 to 2
- early_perchannel_offset: float32 [384], replicated, may hold values from -4 to 4
- cohort_normalizer_factor: float32 [384], replicated, may hold values from 0.5 to 1.5
- cohort_normalizer_offset: float32 [384], replicated, may hold values from -4 to 4
- later_perchannel_stencil: float32 [3, 3, 384], replicated, may hold values from -2 to 2
- later_perchannel_offset: float32 [384], replicated, may hold values from -4 to 4
- neighbour_branch_factor: float32 [384], replicated, may hold values from 0.5 to 1.5
- closing_standardizer_factor: float32 [384], replicated, may hold values from 0.5 to 1.5
- closing_standardizer_offset: float32 [384], replicated, may hold values from -4 to 4
- perceptron_entry_matrix: bfloat16 [384, 1536], replicated, may hold values from -0.3125 to 0.3125
- perceptron_entry_offset: float32 [1536], replicated, may hold values from -4 to 4
- perceptron_exit_matrix: bfloat16 [1536, 384], replicated, may hold values from -0.15625 to 0.15625
- perceptron_exit_offset: float32 [384], replicated, may hold values from -4 to 4
- perceptron_branch_factor: float32 [384], replicated, may hold values from 0.5 to 1.5
Outputs:
- layer_out: bfloat16 [128, 576, 384], P('img')
- grad_input: bfloat16 [128, 576, 384], P('img')
- grad_norm1_gain: float32 [384], replicated
- grad_norm1_shift: float32 [384], replicated
- grad_qkv_weight: float32 [384, 1152], replicated
- grad_qkv_bias: float32 [1152], replicated
- sharpness_sensitivity: float32 [8], replicated
- grad_proj_weight: float32 [384, 384], replicated
- grad_proj_bias: float32 [384], replicated
- grad_scale_attn: float32 [384], replicated
- grad_norm2_gain: float32 [384], replicated
- grad_norm2_shift: float32 [384], replicated
- grad_conv1_kernel: float32 [3, 3, 384], replicated
- grad_conv1_bias: float32 [384], replicated
- grad_batch_gain: float32 [384], replicated
- grad_batch_shift: float32 [384], replicated
- grad_conv2_kernel: float32 [3, 3, 384], replicated
- grad_conv2_bias: float32 [384], replicated
- grad_scale_local: float32 [384], replicated
- grad_norm3_gain: float32 [384], replicated
- grad_norm3_shift: float32 [384], replicated
- grad_fc1_weight: float32 [384, 1536], replicated
- grad_fc1_bias: float32 [1536], replicated
- grad_fc2_weight: float32 [1536, 384], replicated
- grad_fc2_bias: float32 [384], replicated
- grad_scale_mlp: float32 [384], replicated
Inputs may be any that keep to these rules, and one draw needn't show every extreme that they name: `tile_lattice_edges`: each image's grid side is 24, 18 or (168) // 12; every draw has an image of each of the two extreme sides.
All inputs are finite; a program needn't handle non-finite values.
Results may differ from a plain program's by a relative error of at most 0.012.
Values sent between devices are 32-bit elements; how exact they have to be, the bound alone decides.
A program may use at most 192 MiB of HBM per device.

v0:
```python
import math

import jax
import jax.numpy as jnp
from jax import lax
from jax.sharding import PartitionSpec as P

EPS_NORM = 1e-06
EPS_BATCH = 1e-05
EPS_UNIT = 1e-06


def valid_tokens(tile_lattice_edges, grid):
    places = jnp.arange(grid * grid, dtype=jnp.int32)
    row_index = places // grid
    col_index = places % grid
    limits = tile_lattice_edges[:, None]
    inside = (row_index[None, :] < limits) & (col_index[None, :] < limits)
    return inside.astype(jnp.float32)[:, :, None]


def layer_norm(value, gain, shift):
    centre = value - jnp.mean(value, axis=-1, keepdims=True)
    spread = jnp.mean(centre * centre, axis=-1, keepdims=True)
    return centre * lax.rsqrt(spread + EPS_NORM) * gain + shift


def norm_back(value, gain, shift, grad):
    outcome, reverse_sweep = jax.vjp(layer_norm, value, gain, shift)
    return reverse_sweep(grad)


def depthwise(value, kernel):
    images, tokens, channels = value.shape
    grid = math.isqrt(tokens)
    plane = value.reshape(images, grid, grid, channels)
    padded = jnp.pad(plane, ((0, 0), (1, 1), (1, 1), (0, 0)))
    total = jnp.zeros_like(plane)
    for row_step in range(3):
        for col_step in range(3):
            total = (
                total
                + kernel[row_step, col_step]
                * padded[:, row_step : row_step + grid, col_step : col_step + grid, :]
            )
    return total.reshape(images, tokens, channels)


def unit_columns(value):
    return value * lax.rsqrt(jnp.sum(value * value, axis=1, keepdims=True) + EPS_UNIT)


def gelu_slope(value):
    return (
        0.5 * (1.0 + lax.erf(value * 0.7071067811865476))
        + value * jnp.exp(-0.5 * value * value) * 0.3989422804014327
    )


def on_device(
    token_embeddings,
    upstream_sensitivity,
    tile_lattice_edges,
    opening_standardizer_factor,
    opening_standardizer_offset,
    projection_triple_matrix,
    projection_triple_offset,
    sharpness_factor,
    mixing_exit_matrix,
    mixing_exit_offset,
    mixing_branch_factor,
    middle_standardizer_factor,
    middle_standardizer_offset,
    early_perchannel_stencil,
    early_perchannel_offset,
    cohort_normalizer_factor,
    cohort_normalizer_offset,
    later_perchannel_stencil,
    later_perchannel_offset,
    neighbour_branch_factor,
    closing_standardizer_factor,
    closing_standardizer_offset,
    perceptron_entry_matrix,
    perceptron_entry_offset,
    perceptron_exit_matrix,
    perceptron_exit_offset,
    perceptron_branch_factor,
):
    broadened_entries = jnp.float32
    reduced_precision_cast = jnp.bfloat16
    images, tokens, channels = token_embeddings.shape
    flat_rows = images * tokens
    channel_group_count = sharpness_factor.shape[0]
    head_size = channels // channel_group_count
    split_shape = (images, tokens, channel_group_count, head_size)
    inside = valid_tokens(tile_lattice_edges, math.isqrt(tokens))
    tokens_single_precise = token_embeddings.astype(broadened_entries)
    normed1 = (
        (
            inside
            * layer_norm(
                tokens_single_precise, opening_standardizer_factor, opening_standardizer_offset
            )
        )
        .astype(reduced_precision_cast)
        .reshape(flat_rows, channels)
    )
    qkv_rows = inside * (
        jnp.dot(
            normed1, projection_triple_matrix, preferred_element_type=broadened_entries
        ).reshape(images, tokens, 3 * channels)
        + projection_triple_offset
    )
    query_part = qkv_rows[:, :, :channels].reshape(split_shape)
    key_part = qkv_rows[:, :, channels : 2 * channels].reshape(split_shape)
    value_low = qkv_rows[:, :, 2 * channels :].reshape(split_shape).astype(reduced_precision_cast)
    query_unit = unit_columns(query_part).astype(reduced_precision_cast)
    key_unit = unit_columns(key_part).astype(reduced_precision_cast)
    channel_affinity_logits = jnp.einsum(
        "ithb,ithc->ihbc", query_unit, key_unit, preferred_element_type=broadened_entries
    )
    sharpness_entry = sharpness_factor[None, :, None, None]
    channel_affinity_softmaxed = jax.nn.softmax(sharpness_entry * channel_affinity_logits, axis=-1)
    attn_low = channel_affinity_softmaxed.astype(reduced_precision_cast)
    mixed_low = (
        jnp.einsum("ihbc,ithc->ithb", attn_low, value_low, preferred_element_type=broadened_entries)
        .astype(reduced_precision_cast)
        .reshape(flat_rows, channels)
    )
    attn_branch = inside * (
        jnp.dot(mixed_low, mixing_exit_matrix, preferred_element_type=broadened_entries).reshape(
            images, tokens, channels
        )
        + mixing_exit_offset
    )
    resid1 = tokens_single_precise + mixing_branch_factor * attn_branch
    normed2 = inside * layer_norm(resid1, middle_standardizer_factor, middle_standardizer_offset)
    conv_pre = depthwise(normed2, early_perchannel_stencil) + early_perchannel_offset
    activated = inside * jax.nn.gelu(conv_pre, approximate=False)
    local_count = jnp.sum(inside)
    sum_act = jnp.sum(activated, axis=(0, 1))
    sum_act_all, total_count = lax.psum((sum_act, local_count), "img")
    batch_mean = sum_act_all / total_count
    deviation = inside * (activated - batch_mean)
    variance = lax.psum(jnp.sum(deviation * deviation, axis=(0, 1)), "img") / total_count
    inv_spread = lax.rsqrt(variance + EPS_BATCH)
    centred = (activated - batch_mean) * inv_spread
    batch_normed = inside * (centred * cohort_normalizer_factor + cohort_normalizer_offset)
    local_branch = inside * (
        depthwise(batch_normed, later_perchannel_stencil) + later_perchannel_offset
    )
    resid2 = resid1 + neighbour_branch_factor * local_branch
    normed3 = (
        (inside * layer_norm(resid2, closing_standardizer_factor, closing_standardizer_offset))
        .astype(reduced_precision_cast)
        .reshape(flat_rows, channels)
    )
    hidden_pre = (
        jnp.dot(normed3, perceptron_entry_matrix, preferred_element_type=broadened_entries)
        + perceptron_entry_offset
    )
    hidden_low = jax.nn.gelu(hidden_pre, approximate=False).astype(reduced_precision_cast)
    mlp_branch = inside * (
        jnp.dot(
            hidden_low, perceptron_exit_matrix, preferred_element_type=broadened_entries
        ).reshape(images, tokens, channels)
        + perceptron_exit_offset
    )
    layer_out = (inside * (resid2 + perceptron_branch_factor * mlp_branch)).astype(
        reduced_precision_cast
    )
    out_grad = inside * upstream_sensitivity.astype(broadened_entries)
    grad_scale_mlp = jnp.sum(out_grad * mlp_branch, axis=(0, 1))
    fc2_err = perceptron_branch_factor * out_grad
    grad_fc2_bias = jnp.sum(fc2_err, axis=(0, 1))
    fc2_low = fc2_err.astype(reduced_precision_cast).reshape(flat_rows, channels)
    grad_fc2_weight = jnp.einsum(
        "tf,td->fd", hidden_low, fc2_low, preferred_element_type=broadened_entries
    )
    hidden_grad = jnp.einsum(
        "td,fd->tf", fc2_low, perceptron_exit_matrix, preferred_element_type=broadened_entries
    )
    fc1_err = hidden_grad * gelu_slope(hidden_pre)
    grad_fc1_bias = jnp.sum(fc1_err, axis=0)
    fc1_low = fc1_err.astype(reduced_precision_cast)
    grad_fc1_weight = jnp.einsum(
        "td,tf->df", normed3, fc1_low, preferred_element_type=broadened_entries
    )
    normed3_grad = jnp.einsum(
        "tf,df->td", fc1_low, perceptron_entry_matrix, preferred_element_type=broadened_entries
    ).reshape(images, tokens, channels)
    resid2_part, grad_norm3_gain, grad_norm3_shift = norm_back(
        resid2, closing_standardizer_factor, closing_standardizer_offset, inside * normed3_grad
    )
    resid2_grad = out_grad + resid2_part
    mlp_summed = (
        grad_norm3_gain,
        grad_norm3_shift,
        grad_fc1_weight,
        grad_fc1_bias,
        grad_fc2_weight,
        grad_fc2_bias,
        grad_scale_mlp,
    )
    grad_scale_local = jnp.sum(resid2_grad * local_branch, axis=(0, 1))
    local_err = inside * neighbour_branch_factor * resid2_grad
    grad_conv2_bias = jnp.sum(local_err, axis=(0, 1))
    unused, pull_second = jax.vjp(depthwise, batch_normed, later_perchannel_stencil)
    normed_back, grad_conv2_kernel = pull_second(local_err)
    batch_normed_grad = inside * normed_back
    grad_batch_gain = jnp.sum(batch_normed_grad * centred, axis=(0, 1))
    grad_batch_shift = jnp.sum(batch_normed_grad, axis=(0, 1))
    centred_grad = batch_normed_grad * cohort_normalizer_factor
    sum_grad_all, sum_cross_all = lax.psum(
        (jnp.sum(centred_grad, axis=(0, 1)), jnp.sum(centred_grad * centred, axis=(0, 1))), "img"
    )
    activated_grad = (
        inside
        * inv_spread
        * (centred_grad - sum_grad_all / total_count - centred * (sum_cross_all / total_count))
    )
    conv1_err = activated_grad * gelu_slope(conv_pre)
    grad_conv1_bias = jnp.sum(conv1_err, axis=(0, 1))
    unused, pull_first = jax.vjp(depthwise, normed2, early_perchannel_stencil)
    normed2_grad, grad_conv1_kernel = pull_first(conv1_err)
    resid1_part, grad_norm2_gain, grad_norm2_shift = norm_back(
        resid1, middle_standardizer_factor, middle_standardizer_offset, inside * normed2_grad
    )
    resid1_grad = resid2_grad + resid1_part
    grad_scale_attn = jnp.sum(resid1_grad * attn_branch, axis=(0, 1))
    proj_err = inside * mixing_branch_factor * resid1_grad
    grad_proj_bias = jnp.sum(proj_err, axis=(0, 1))
    proj_low = proj_err.astype(reduced_precision_cast).reshape(flat_rows, channels)
    grad_proj_weight = jnp.einsum(
        "td,te->de", mixed_low, proj_low, preferred_element_type=broadened_entries
    )
    mixed_grad = (
        jnp.einsum(
            "te,de->td", proj_low, mixing_exit_matrix, preferred_element_type=broadened_entries
        )
        .astype(reduced_precision_cast)
        .reshape(split_shape)
    )
    attn_grad = jnp.einsum(
        "ithb,ithc->ihbc", mixed_grad, value_low, preferred_element_type=broadened_entries
    )
    value_grad = jnp.einsum(
        "ihbc,ithb->ithc", attn_low, mixed_grad, preferred_element_type=broadened_entries
    )
    logit_sensitivity = channel_affinity_softmaxed * (
        attn_grad - jnp.sum(attn_grad * channel_affinity_softmaxed, axis=-1, keepdims=True)
    )
    sharpness_sensitivity = jnp.sum(logit_sensitivity * channel_affinity_logits, axis=(0, 2, 3))
    logit_reduced = (sharpness_entry * logit_sensitivity).astype(reduced_precision_cast)
    query_unit_grad = jnp.einsum(
        "ihbc,ithc->ithb", logit_reduced, key_unit, preferred_element_type=broadened_entries
    )
    key_unit_grad = jnp.einsum(
        "ihbc,ithb->ithc", logit_reduced, query_unit, preferred_element_type=broadened_entries
    )
    unused, pull_query = jax.vjp(unit_columns, query_part)
    query_grad = pull_query(query_unit_grad)[0]
    unused, pull_key = jax.vjp(unit_columns, key_part)
    key_grad = pull_key(key_unit_grad)[0]
    row_shape = (images, tokens, channels)
    qkv_grad = inside * jnp.concatenate(
        (query_grad.reshape(row_shape), key_grad.reshape(row_shape), value_grad.reshape(row_shape)),
        axis=-1,
    )
    grad_qkv_bias = jnp.sum(qkv_grad, axis=(0, 1))
    qkv_low = qkv_grad.astype(reduced_precision_cast).reshape(flat_rows, 3 * channels)
    grad_qkv_weight = jnp.einsum(
        "td,te->de", normed1, qkv_low, preferred_element_type=broadened_entries
    )
    normed1_grad = jnp.einsum(
        "te,de->td", qkv_low, projection_triple_matrix, preferred_element_type=broadened_entries
    ).reshape(row_shape)
    input_part, grad_norm1_gain, grad_norm1_shift = norm_back(
        tokens_single_precise,
        opening_standardizer_factor,
        opening_standardizer_offset,
        inside * normed1_grad,
    )
    grad_input = (resid1_grad + input_part).astype(reduced_precision_cast)
    every_summed = lax.psum(
        (
            grad_norm1_gain,
            grad_norm1_shift,
            grad_qkv_weight,
            grad_qkv_bias,
            sharpness_sensitivity,
            grad_proj_weight,
            grad_proj_bias,
            grad_scale_attn,
            grad_norm2_gain,
            grad_norm2_shift,
            grad_conv1_kernel,
            grad_conv1_bias,
            grad_batch_gain,
            grad_batch_shift,
            grad_conv2_kernel,
            grad_conv2_bias,
            grad_scale_local,
            grad_norm3_gain,
            grad_norm3_shift,
            grad_fc1_weight,
            grad_fc1_bias,
            grad_fc2_weight,
            grad_fc2_bias,
            grad_scale_mlp,
        ),
        "img",
    )
    other_summed = tuple(every_summed[:17])
    mlp_summed = tuple(every_summed[17:])
    return (layer_out, grad_input) + tuple(other_summed) + tuple(mlp_summed)


def solution(mesh):
    placed = (
        P("img", None, None),
        P("img", None, None),
        P("img"),
        P(),
        P(),
        P(),
        P(),
        P(),
        P(),
        P(),
        P(),
        P(),
        P(),
        P(),
        P(),
        P(),
        P(),
        P(),
        P(),
        P(),
        P(),
        P(),
        P(),
        P(),
        P(),
        P(),
        P(),
    )
    return jax.shard_map(
        on_device,
        mesh=mesh,
        in_specs=placed,
        out_specs=(
            P("img", None, None),
            P("img", None, None),
            P(),
            P(),
            P(),
            P(),
            P(),
            P(),
            P(),
            P(),
            P(),
            P(),
            P(),
            P(),
            P(),
            P(),
            P(),
            P(),
            P(),
            P(),
            P(),
            P(),
            P(),
            P(),
            P(),
            P(),
        ),
        check_vma=False,
    )
```

profile of v0, /device:TPU:0, one launch (start us, length us, event | category | flops | bytes accessed | tf_op | source)
XLA Modules:
  0.0 622.5 jit_solution(4497324052985042136)
XLA Ops:
  7.3 1.5 convert_reduce_fusion.1
  9.6 1.9 convert_reduce_fusion
  11.6 2.3 fusion.30
  14.0 3.7 add_multiply_fusion
  19.1 3.7 multiply_reduce_fusion.32
  26.0 4.1 copy.82
  30.1 5.3 copy.84
  35.4 5.3 copy.83
  40.7 4.1 fusion.71
  47.0 3.9 convolution_convert_fusion.1
  50.8 6.0 fusion.122
  59.1 13.1 %fusion.120 = (f32[384]{0:T(512)S(1)}, f32[4,24,24,384]{3,2,1,0:T(8,128)}, f32[4,24,24,384]{3,2,1,0:T(8,128)}) fusion(f32[4,24,24]{2,1,0:T(8,128)S(1)} %and_convert_fusion, f32[384]{0:T(512)S(1)} %copy-done.104, f32[384]{0:T(512)S(1)} %get-tuple-element.79, f32[384]{0:T(512)S(1)} %get-tuple-element.80, f32[384]{0:T(512)S(1)} %get-tuple-element.73, ...), kind=kLoop, calls=%fused_computation.301 | loop fusion | flops 74317440 | bytes 10642944 | tf_op jit(solution)/shard_map/reduce_sum | solution.py:141
  72.3 42.3 %all-reduce.40 = (f32[384]{0:T(512)S(1)}, f32[]{:T(128)}) all-reduce(f32[384]{0:T(512)S(1)} %get-tuple-element.122, f32[]{:T(128)} %convert_reduce_fusion.1), channel_id=1, replica_groups=mesh['img'=32] {'img'}, use_global_device_ids=true, to_apply=%region_9.10 | all-reduce | flops 385 | bytes 3080 | tf_op jit(solution)/shard_map/psum | solution.py:142
  115.2 2.5 multiply_reduce_fusion.30
  117.8 40.6 %psum.205 = f32[384]{0:T(512)S(1)} all-reduce(f32[384]{0:T(512)S(1)} %multiply_reduce_fusion.30), channel_id=1, replica_groups=mesh['img'=32] {'img'}, use_global_device_ids=true, to_apply=%region_13.14 | all-reduce | flops 384 | bytes 3072 | tf_op jit(solution)/shard_map/psum | solution.py:145
  159.1 2.6 add_multiply_fusion.2
  161.8 4.1 multiply_add_fusion.1
  165.9 1.8 copy-done.21
  167.7 2.3 multiply_add_fusion
  170.1 2.4 reduce_sum.533
  172.5 2.9 multiply_reduce_fusion.29
  176.8 36.3 %fusion.4 = (bf16[2304,1536]{1,0:T(8,128)(2,1)}, f32[2304,1536]{1,0:T(8,128)S(1)}) fusion(f32[1536]{0:T(1024)S(1)} %copy-done.109, bf16[2304,384]{1,0:T(8,128)(2,1)S(1)} %bitcast.102, bf16[384,1536]{1,0:T(8,128)(2,1)S(1)} %copy-done), kind=kOutput, calls=%fused_computation.7 | convolution fusion | flops 2951479296 | bytes 24188928 | tf_op jit(solution)/shard_map/dot_general | solution.py:159
  213.1 9.0 %fusion.128 = (f32[1536]{0:T(1024)}, bf16[2304,1536]{1,0:T(8,128)(2,1)S(1)}) fusion(f32[2304,1536]{1,0:T(8,128)S(1)} %get-tuple-element.153, bf16[2304,384]{1,0:T(8,128)(2,1)S(1)} %bitcast.109, bf16[1536,384]{1,0:T(8,128)(2,1)S(1)} %copy-done.106), kind=kOutput, calls=%fused_computation.304 | convolution fusion | flops 2756835840 | bytes 24188928 | tf_op jit(solution)/shard_map/td,fd->tf/dot_general | solution.py:180
  222.1 4.3 fusion.42
  226.4 3.9 multiply_reduce_fusion.1
  230.3 1.5 multiply_reduce_fusion.2
  231.8 2.0 fusion.119
  233.9 2.3 fusion.116
  238.4 12.3 %multiply_reduce_fusion.12 = (f32[384]{0:T(512)S(1)}, f32[384]{0:T(512)S(1)}, f32[384]{0:T(512)S(1)}, f32[384]{0:T(512)S(1)}, f32[384]{0:T(512)S(1)}, /*index=5*...) fusion(f32[4,24,24,384]{3,2,1,0:T(8,128)} %bitcast.99, ...), kind=kLoop, calls=%fused_computation.118 | loop fusion | flops 23884416 | bytes 38956032 | tf_op jit(solution)/shard_map/transpose(jvp())/reduce_sum | solution.py:43
  250.8 5.6 pad_add_fusion.1
  257.9 8.2 %multiply_reduce_fusion.13 = (f32[384]{0:T(512)S(1)}, f32[384]{0:T(512)S(1)}, f32[384]{0:T(512)S(1)}, f32[384]{0:T(512)S(1)}, f32[4,24,24,384]{3,2,1,0:T(8,128)}) fusion(f32[4,24,24,384]{3,2,1,0:T(8,128)S(1)} %copy-done.6, f32[384]{0:T(512)S(1)} %copy-done.63, f32[384]{0:T(512)S(1)} %copy-done.56, f32[384]{0:T(512)S(1)} %copy-done.84, ...), kind=kLoop, calls=%fused_computation.119 | loop fusion | flops 14154240 | bytes 31870464 | tf_op jit(solution)/shard_map/reduce_sum | solution.py:211
  266.1 40.0 %all-reduce.39 = (f32[384]{0:T(512)S(1)}, f32[384]{0:T(512)S(1)}) all-reduce(f32[384]{0:T(512)S(1)} %get-tuple-element.31, f32[384]{0:T(512)S(1)} %get-tuple-element.57), channel_id=1, replica_groups=mesh['img'=32] {'img'}, use_global_device_ids=true, to_apply=%region_21.22 | all-reduce | flops 768 | bytes 6144 | tf_op jit(solution)/shard_map/psum | solution.py:214
  307.5 20.6 %multiply_reduce_fusion.22 = (f32[384]{0:T(512)S(1)}, f32[384]{0:T(512)S(1)}, f32[384]{0:T(512)S(1)}, f32[384]{0:T(512)S(1)}, f32[384]{0:T(512)S(1)}, /*index=5*...) fusion(f32[4,24,24,384]{3,2,1,0:T(8,128)} %bitcast.93, ...), kind=kLoop, calls=%fused_computation.128 | loop fusion | flops 31846656 | bytes 17726976 | tf_op jit(solution)/shard_map/transpose(jvp())/reduce_sum | solution.py:43
  328.3 7.3 %broadcast_multiply_fusion.8 = (f32[4,24,24,384]{3,2,1,0:T(8,128)S(1)}, f32[4,24,24,384]{3,2,1,0:T(8,128)}, f32[4,24,24,384]{3,2,1,0:T(8,128)}, f32[4,24,24,384]...) fusion(f32[4,24,24,384]{3,2,1,0:T(8,128)S(1)} %get-tuple-elemen, ...), kind=kLoop, calls=%fused_computation.192 | loop fusion | flops 7962624 | bytes 35403264 | tf_op jit(solution)/shard_map/transpose(jvp())/mul | solution.py:43
  336.6 8.3 %multiply_reduce_fusion.23 = (f32[384]{0:T(512)S(1)}, f32[4,24,24,384]{3,2,1,0:T(8,128)S(1)}) fusion(f32[4,24,24]{2,1,0:T(8,128)S(1)} %copy-done.25, f32[4,24,24,384]{3,2,1,0:T(8,128)} %get-tuple-element.140, f32[4,24,24,384]{3,2,1,0:T(8,128)} %get-tuple-element.141, f32[4,24,24,384]{3,2,1,0:T(8,128)} %get-tuple-element.142, ...), kind=kLoop, calls=%fused_computation.129 | loop fusion | flops 7077504 | bytes 28322304 | tf_op jit(solution)/shard_map/transpose(jvp())/reduce_sum | solution.py:25
  345.4 1.6 copy-done.4
  348.2 2.3 multiply_reduce_fusion.24
  350.8 4.1 fusion.57
  354.9 2.5 convolution_convert_fusion
  357.3 3.8 copy.87
  361.2 5.5 reshape.570
  366.7 3.8 fusion.60
  370.5 4.3 fusion.58
  374.8 7.2 %fusion.24 = (f32[4,8,48]{2,1,0:T(8,128)S(1)}, f32[4,8,576,48]{2,3,1,0:T(8,128)}) fusion(f32[4,576,8,48]{1,3,2,0:T(8,128)} %bitcast.85, f32[4,576,8,48]{1,3,2,0:T(8,128)} %bitcast.89, f32[4,8,48]{2,1,0:T(8,128)S(1)} %copy-done.40, f32[8]{0:T(128)S(1)} %copy-done.93, f32[4,8,48,48]{2,3,1,0:T(8,128)} %fusion.60, f32[4,8,48,48]{2,3,1,0:T(8,128)} %get-tuple-element.150, ...), kind=kOutput, calls=%fused_computation.69 | convolution fusion | flops 88989744 | bytes 11225120 | tf_op jit(solution)/shard_map/ihbc,ithb->ithc/dot_general | solution.py:258
  381.9 7.2 %fusion.25 = (f32[4,8,48]{2,1,0:T(8,128)S(1)}, f32[4,8,576,48]{2,3,1,0:T(8,128)}) fusion(f32[4,576,8,48]{1,3,2,0:T(8,128)} %bitcast.90, f32[8]{0:T(128)S(1)} %copy-done.93, f32[4,8,48,48]{2,3,1,0:T(8,128)} %fusion.60, f32[4,8,48,48]{2,3,1,0:T(8,128)} %get-tuple-element.150, f32[4,8,48]{2,1,0:T(8,128)S(1)} %copy-done.36, f32[4,576,8,48]{1,3,2,0:T(8,128)} %bitcast.86, ...), kind=kOutput, calls=%fused_computation.72 | convolution fusion | flops 88989744 | bytes 11225120 | tf_op jit(solution)/shard_map/ihbc,ithc->ithb/dot_general | solution.py:255
  389.1 4.3 copy.94
  393.5 4.4 reshape.571
  397.9 8.9 %fusion.131 = f32[1536,384]{1,0:T(8,128)} fusion(bf16[2304,1536]{1,0:T(8,128)(2,1)} %get-tuple-element.152, bf16[2304,384]{1,0:T(8,128)(2,1)} %bitcast.108), kind=kOutput, calls=%fused_computation.307 | convolution fusion | flops 2717908992 | bytes 11206656 | tf_op jit(solution)/shard_map/tf,td->fd/dot_general | solution.py:177
  406.8 1.9 fusion.130
  408.7 5.4 copy.93
  414.2 5.0 add_add_fusion.1
  419.1 5.3 copy.91
  424.5 5.0 add_add_fusion
  429.5 5.6 copy.92
  435.1 8.1 %convolution_bitcast_fusion = f32[384,1152]{1,0:T(8,128)} fusion(bf16[4,576,384]{2,1,0:T(8,128)(2,1)S(1)} %copy-done.8, f32[384]{0:T(512)S(1)} %copy-done.111, f32[384]{0:T(512)S(1)} %copy-done.91, f32[4,576]{1,0:T(4,128)S(1)} %copy-done.50, f32[4,576]{1,0:T(4,128)S(1)} %copy-done.42, f32[4,576]{1,0:T(4,128)S(1)} %and_convert_fusion.2, ...), kind=kOutput, calls=%fused_computation.181 | convolution fusion | flops 2055241728 | bytes 14186496 | tf_op jit(solution)/shard_map/td,te->de/dot_general | solution.py:272
  443.3 9.0 %fusion.129 = f32[2304,384]{1,0:T(8,128)} fusion(bf16[2304,1536]{1,0:T(8,128)(2,1)} %get-tuple-element.152, bf16[1536,384]{1,0:T(8,128)(2,1)} %param.51), kind=kOutput, calls=%fused_computation.305 | convolution fusion | flops 2717908992 | bytes 11796480 | tf_op jit(solution)/shard_map/dot_general | solution.py:164
  452.6 17.0 %multiply_reduce_fusion = (f32[384]{0:T(512)S(1)}, f32[384]{0:T(512)S(1)}, f32[384]{0:T(512)S(1)}, f32[384]{0:T(512)S(1)}, f32[384]{0:T(512)S(1)}, /*index=5*/f3...) fusion(bf16[4,576,384]{2,1,0:T(8,128)(2,1)} %param.28, f32[4,576,384]{2,1,0:T(8,128)} %bitcast.110, ...), kind=kOutput, calls=%fused_computation.106 | convolution fusion | flops 2076471168 | bytes 41636352 | tf_op jit(solution)/shard_map/te,de->td/dot_general | solution.py:275
  469.7 2.5 multiply_reduce_fusion.36
  472.2 4.7 fusion.29
  478.1 42.8 %all-reduce.38 = (f32[384]{0:T(512)}, f32[384]{0:T(512)}, f32[1152]{0:T(1024)}, f32[8]{0:T(128)}, f32[384]{0:T(512)}, /*index=5*/f32[384]{0:T(512)}, f32[384]{0:...) all-reduce(f32[384]{0:T(512)S(1)} %get-tuple-element.50, ...), channel_id=1, replica_groups=mesh['img'=32] {'img'}, use_global_device_ids=true, to_apply=%region_30.31 | all-reduce | flops 15368 | bytes 122944 | tf_op jit(solution)/shard_map/psum | solution.py:285
  521.0 5.8 add_convert_fusion
  526.8 81.9 %all-reduce.44.cloned.1.call-done = (f32[384,1152]{1,0:T(8,128)}, f32[384,384]{1,0:T(8,128)}, f32[384,1536]{1,0:T(8,128)}, f32[1536,384]{1,0:T(8,128)}) async-done(((f32[384,1152]{1,0:T(8,128)}, f32[384,384]{1,0:T(8,128)}, f32[384,1536]{1,0:T(8,128)}, f32[1536,384]{1,0:T(8,128)}), (f32[384,1152]{1,0:T(8,128)}, f32[384,384]{1,0:T(8,128)}, f32[384,1536]{1,0:T(8,128)}, ...) | async-done | bytes 7077904 | tf_op jit(solution)/shard_map/psum | solution.py:285
  608.6 2.9 copy.106
  612.4 1.4 copy.108
  (294 shorter events, 23.8 us)
Async XLA Ops:
  7.2 169.6 %copy-start = (bf16[384,1536]{1,0:T(8,128)(2,1)S(1)}, bf16[384,1536]{1,0:T(8,128)(2,1)}, u32[]{:S(2)}) copy-start(bf16[384,1536]{1,0:T(8,128)(2,1)} %param.49) | copy-start | bytes 3538948
  7.2 6.7 %copy-start.7 = (bf16[4,576,384]{2,1,0:T(8,128)(2,1)S(1)}, bf16[4,576,384]{2,1,0:T(8,128)(2,1)}, u32[]{:S(2)}) copy-start(bf16[4,576,384]{2,1,0:T(8,128)(2,1)} %param.27) | copy-start | bytes 5308420
  7.2 6.7 %copy-start.90 = (f32[384]{0:T(512)S(1)}, f32[384]{0:T(512)}, u32[]{:S(2)}) copy-start(f32[384]{0:T(512)} %param.30) | copy-start | bytes 4612
  7.2 6.7 %copy-start.110 = (f32[384]{0:T(512)S(1)}, f32[384]{0:T(512)}, u32[]{:S(2)}) copy-start(f32[384]{0:T(512)} %param.31) | copy-start | bytes 4612
  7.3 6.7 %copy-start.108 = (f32[1152]{0:T(1024)S(1)}, f32[1152]{0:T(1024)}, u32[]{:S(2)}) copy-start(f32[1152]{0:T(1024)} %param.33) | copy-start | bytes 13828
  7.3 601.3 %all-reduce.44.cloned.1.call-start = ((), (), s32[]{:S(2)}) async-start(), calls=%async_computation | async-start | bytes 14155776 | tf_op jit(solution)/shard_map/psum | solution.py:285
  7.3 6.6 %copy-start.107 = (bf16[384,1152]{1,0:T(8,128)(2,1)S(1)}, bf16[384,1152]{1,0:T(8,128)(2,1)}, u32[]{:S(2)}) copy-start(bf16[384,1152]{1,0:T(8,128)(2,1)} %param.32) | copy-start | bytes 2654212
  11.5 6.1 copy-start.41
  19.1 5.8 copy-start.85
  19.1 5.9 copy-start.86
  25.0 34.1 %copy-start.65 = (f32[384]{0:T(512)}, f32[384]{0:T(512)S(1)}, u32[]{:S(2)}) copy-start(f32[384]{0:T(512)S(1)} %get-tuple-element.72) | copy-start | bytes 4612
  25.0 34.1 %copy-start.67 = (f32[384]{0:T(512)}, f32[384]{0:T(512)S(1)}, u32[]{:S(2)}) copy-start(f32[384]{0:T(512)S(1)} %get-tuple-element.73) | copy-start | bytes 4612
  25.0 34.0 %copy-start.69 = (f32[384]{0:T(512)}, f32[384]{0:T(512)S(1)}, u32[]{:S(2)}) copy-start(f32[384]{0:T(512)S(1)} %get-tuple-element.74) | copy-start | bytes 4612
  25.0 34.0 %copy-start.71 = (f32[384]{0:T(512)}, f32[384]{0:T(512)S(1)}, u32[]{:S(2)}) copy-start(f32[384]{0:T(512)S(1)} %get-tuple-element.75) | copy-start | bytes 4612
  25.0 34.0 %copy-start.73 = (f32[384]{0:T(512)}, f32[384]{0:T(512)S(1)}, u32[]{:S(2)}) copy-start(f32[384]{0:T(512)S(1)} %get-tuple-element.76) | copy-start | bytes 4612
  25.0 34.0 %copy-start.75 = (f32[384]{0:T(512)}, f32[384]{0:T(512)S(1)}, u32[]{:S(2)}) copy-start(f32[384]{0:T(512)S(1)} %get-tuple-element.77) | copy-start | bytes 4612
  25.0 34.0 %copy-start.77 = (f32[384]{0:T(512)}, f32[384]{0:T(512)S(1)}, u32[]{:S(2)}) copy-start(f32[384]{0:T(512)S(1)} %get-tuple-element.78) | copy-start | bytes 4612
  25.1 34.0 %copy-start.79 = (f32[384]{0:T(512)}, f32[384]{0:T(512)S(1)}, u32[]{:S(2)}) copy-start(f32[384]{0:T(512)S(1)} %get-tuple-element.79) | copy-start | bytes 4612
  25.1 34.0 %copy-start.81 = (f32[384]{0:T(512)}, f32[384]{0:T(512)S(1)}, u32[]{:S(2)}) copy-start(f32[384]{0:T(512)S(1)} %get-tuple-element.80) | copy-start | bytes 4612
  25.2 10.2 %copy-start.45 = (f32[4,8,48]{2,1,0:T(8,128)}, f32[4,8,48]{2,1,0:T(8,128)S(1)}, u32[]{:S(2)}) copy-start(f32[4,8,48]{2,1,0:T(8,128)S(1)} %add.405) | copy-start | bytes 18436
  25.9 14.8 %copy-start.37 = (f32[4,8,48]{2,1,0:T(8,128)}, f32[4,8,48]{2,1,0:T(8,128)S(1)}, u32[]{:S(2)}) copy-start(f32[4,8,48]{2,1,0:T(8,128)S(1)} %rsqrt.60) | copy-start | bytes 18436
  25.9 14.8 %copy-start.39 = (f32[4,8,48]{2,1,0:T(8,128)}, f32[4,8,48]{2,1,0:T(8,128)S(1)}, u32[]{:S(2)}) copy-start(f32[4,8,48]{2,1,0:T(8,128)S(1)} %rsqrt.59) | copy-start | bytes 18436
  47.0 9.8 %copy-start.35 = (f32[4,8,48]{2,1,0:T(8,128)}, f32[4,8,48]{2,1,0:T(8,128)S(1)}, u32[]{:S(2)}) copy-start(f32[4,8,48]{2,1,0:T(8,128)S(1)} %get-tuple-element.149) | copy-start | bytes 18436
  57.7 101.3 %copy-start.24 = (f32[4,24,24]{2,1,0:T(8,128)}, f32[4,24,24]{2,1,0:T(8,128)S(1)}, u32[]{:S(2)}) copy-start(f32[4,24,24]{2,1,0:T(8,128)S(1)} %and_convert_fusion) | copy-start | bytes 27652
  59.0 13.2 %copy-start.13 = (f32[4,576,384]{2,1,0:T(8,128)}, f32[4,576,384]{2,1,0:T(8,128)S(1)}, u32[]{:S(2)}) copy-start(f32[4,576,384]{2,1,0:T(8,128)S(1)} %add_multiply_fusion.3) | copy-start | bytes 10616836
  72.3 86.8 %copy-start.83 = (f32[384]{0:T(512)S(1)}, f32[384]{0:T(512)}, u32[]{:S(2)}) copy-start(f32[384]{0:T(512)} %param.42) | copy-start | bytes 4612
  72.3 86.8 %copy-start.105 = (f32[384]{0:T(512)S(1)}, f32[384]{0:T(512)}, u32[]{:S(2)}) copy-start(f32[384]{0:T(512)} %param.43) | copy-start | bytes 4612
  115.2 46.5 %copy-start.55 = (f32[384]{0:T(512)}, f32[384]{0:T(512)S(1)}, u32[]{:S(2)}) copy-start(f32[384]{0:T(512)S(1)} %broadcast_divide_fusion.3) | copy-start | bytes 4612
  161.7 6.0 copy-start.3
  161.8 6.0 copy-start.87
  161.8 6.0 copy-start.101
  176.8 36.3 %copy-start.29 = (bf16[4,576,384]{2,1,0:T(8,128)(2,1)S(1)}, bf16[4,576,384]{2,1,0:T(8,128)(2,1)}, u32[]{:S(2)}) copy-start(bf16[4,576,384]{2,1,0:T(8,128)(2,1)} %get-tuple-element.148) | copy-start | bytes 5308420
  176.8 36.3 %copy-start.106 = (bf16[1536,384]{1,0:T(8,128)(2,1)S(1)}, bf16[1536,384]{1,0:T(8,128)(2,1)}, u32[]{:S(2)}) copy-start(bf16[1536,384]{1,0:T(8,128)(2,1)} %param.51) | copy-start | bytes 3538948
  250.7 5.7 copy-start.6
  250.7 6.2 copy-start.19
  250.8 7.1 %copy-start.20 = (f32[4,24,24,384]{3,2,1,0:T(8,128)S(1)}, f32[4,24,24,384]{3,2,1,0:T(8,128)}, u32[]{:S(2)}) copy-start(f32[4,24,24,384]{3,2,1,0:T(8,128)} %get-tuple-element.131) | copy-start | bytes 10616836
  250.8 7.1 %copy-start.25 = (f32[4,24,24]{2,1,0:T(8,128)S(1)}, f32[4,24,24]{2,1,0:T(8,128)}, u32[]{:S(2)}) copy-start(f32[4,24,24]{2,1,0:T(8,128)} %copy-done.24) | copy-start | bytes 27652
  250.8 7.1 %copy-start.56 = (f32[384]{0:T(512)S(1)}, f32[384]{0:T(512)}, u32[]{:S(2)}) copy-start(f32[384]{0:T(512)} %copy-done.55) | copy-start | bytes 4612
  250.8 7.1 %copy-start.63 = (f32[384]{0:T(512)S(1)}, f32[384]{0:T(512)}, u32[]{:S(2)}) copy-start(f32[384]{0:T(512)} %copy-done.62) | copy-start | bytes 4612
  250.8 7.1 %copy-start.84 = (f32[384]{0:T(512)S(1)}, f32[384]{0:T(512)}, u32[]{:S(2)}) copy-start(f32[384]{0:T(512)} %param.42) | copy-start | bytes 4612
  307.4 20.8 %copy-start.66 = (f32[384]{0:T(512)S(1)}, f32[384]{0:T(512)}, u32[]{:S(2)}) copy-start(f32[384]{0:T(512)} %copy-done.65) | copy-start | bytes 4612
  307.4 20.7 %copy-start.68 = (f32[384]{0:T(512)S(1)}, f32[384]{0:T(512)}, u32[]{:S(2)}) copy-start(f32[384]{0:T(512)} %copy-done.67) | copy-start | bytes 4612
  307.5 20.7 %copy-start.70 = (f32[384]{0:T(512)S(1)}, f32[384]{0:T(512)}, u32[]{:S(2)}) copy-start(f32[384]{0:T(512)} %copy-done.69) | copy-start | bytes 4612
  307.5 20.7 %copy-start.72 = (f32[384]{0:T(512)S(1)}, f32[384]{0:T(512)}, u32[]{:S(2)}) copy-start(f32[384]{0:T(512)} %copy-done.71) | copy-start | bytes 4612
  307.5 20.7 %copy-start.74 = (f32[384]{0:T(512)S(1)}, f32[384]{0:T(512)}, u32[]{:S(2)}) copy-start(f32[384]{0:T(512)} %copy-done.73) | copy-start | bytes 4612
  307.5 20.7 %copy-start.76 = (f32[384]{0:T(512)S(1)}, f32[384]{0:T(512)}, u32[]{:S(2)}) copy-start(f32[384]{0:T(512)} %copy-done.75) | copy-start | bytes 4612
  307.5 20.7 %copy-start.78 = (f32[384]{0:T(512)S(1)}, f32[384]{0:T(512)}, u32[]{:S(2)}) copy-start(f32[384]{0:T(512)} %copy-done.77) | copy-start | bytes 4612
  307.5 20.7 %copy-start.80 = (f32[384]{0:T(512)S(1)}, f32[384]{0:T(512)}, u32[]{:S(2)}) copy-start(f32[384]{0:T(512)} %copy-done.79) | copy-start | bytes 4612
  307.5 20.7 %copy-start.82 = (f32[384]{0:T(512)S(1)}, f32[384]{0:T(512)}, u32[]{:S(2)}) copy-start(f32[384]{0:T(512)} %copy-done.81) | copy-start | bytes 4612
  361.2 9.3 %copy-start.23 = (f32[4,8,48,48]{2,3,1,0:T(8,128)S(1)}, f32[4,8,48,48]{2,3,1,0:T(8,128)}, u32[]{:S(2)}) copy-start(f32[4,8,48,48]{2,3,1,0:T(8,128)} %copy-done.22) | copy-start | bytes 884740
  361.2 9.3 %copy-start.36 = (f32[4,8,48]{2,1,0:T(8,128)S(1)}, f32[4,8,48]{2,1,0:T(8,128)}, u32[]{:S(2)}) copy-start(f32[4,8,48]{2,1,0:T(8,128)} %copy-done.35) | copy-start | bytes 18436
  361.2 9.3 %copy-start.93 = (f32[8]{0:T(128)S(1)}, f32[8]{0:T(128)}, u32[]{:S(2)}) copy-start(f32[8]{0:T(128)} %param.34) | copy-start | bytes 100
  374.8 7.2 %copy-start.38 = (f32[4,8,48]{2,1,0:T(8,128)S(1)}, f32[4,8,48]{2,1,0:T(8,128)}, u32[]{:S(2)}) copy-start(f32[4,8,48]{2,1,0:T(8,128)} %copy-done.37) | copy-start | bytes 18436
  397.9 8.9 %copy-start.28 = (bf16[2304,384]{0,1:T(8,128)(2,1)S(1)}, bf16[2304,384]{0,1:T(8,128)(2,1)}, u32[]{:S(2)}) copy-start(bf16[2304,384]{0,1:T(8,128)(2,1)} %reshape.571) | copy-start | bytes 5308420
  429.5 5.6 copy-start.42
  429.5 5.6 copy-start.50
  429.5 5.6 copy-start.91
  443.3 9.3 %copy-start.98 = (f32[384]{0:T(512)S(1)}, f32[384]{0:T(512)}, u32[]{:S(2)}) copy-start(f32[384]{0:T(512)} %param.36) | copy-start | bytes 4612
  443.3 9.3 %copy-start.100 = (f32[384]{0:T(512)S(1)}, f32[384]{0:T(512)}, u32[]{:S(2)}) copy-start(f32[384]{0:T(512)} %param.53) | copy-start | bytes 4612
  443.3 9.3 %copy-start.102 = (f32[384]{0:T(512)S(1)}, f32[384]{0:T(512)}, u32[]{:S(2)}) copy-start(f32[384]{0:T(512)} %param.45) | copy-start | bytes 4612
  443.3 9.3 %copy-start.112 = (f32[384]{0:T(512)S(1)}, f32[384]{0:T(512)}, u32[]{:S(2)}) copy-start(f32[384]{0:T(512)} %param.52) | copy-start | bytes 4612
  452.6 17.0 %copy-start.52 = (f32[4,576]{1,0:T(4,128)S(1)}, f32[4,576]{1,0:T(4,128)}, u32[]{:S(2)}) copy-start(f32[4,576]{1,0:T(4,128)} %copy-done.51) | copy-start | bytes 27652
  469.7 7.2 %copy-start.17 = (f32[4,576,384]{2,1,0:T(8,128)S(1)}, f32[4,576,384]{2,1,0:T(8,128)}, u32[]{:S(2)}) copy-start(f32[4,576,384]{2,1,0:T(8,128)} %copy.91) | copy-start | bytes 10616836
  469.7 7.2 %copy-start.18 = (f32[4,576,384]{2,1,0:T(8,128)S(1)}, f32[4,576,384]{2,1,0:T(8,128)}, u32[]{:S(2)}) copy-start(f32[4,576,384]{2,1,0:T(8,128)} %copy.92) | copy-start | bytes 10616836
  (50 other events, 160.7 us)
Sparse Core Ops, SparseCore 0:
  443.4 165.1 all-reduce.43
where the time goes:
time: 629 us; the launch traced here: 622 us
  blocking collectives  166 us (26%)
  other arithmetic  149 us (24%)
  matrix products  141 us (22%)
  waiting for transfers between devices  81.9 us (13%)
  local copies, waits for them, and re-layouts  69 us (11%)
  between operations  16.1 us (3%)
    psum x1, waiting for transfers between devices, on_device(): lax.psum((grad_norm1_gain, grad_norm1_shift, grad_qkv_weight, grad_qkv_bi...  81.9 us
    psum x1, blocking collectives, on_device(): lax.psum((grad_norm1_gain, grad_norm1_shift, grad_qkv_weight, grad_qkv_bi...  42.8 us
    psum x1, blocking collectives, on_device(): sum_act_all, total_count = lax.psum((sum_act, local_count), 'img')  42.3 us
    psum x1, blocking collectives, on_device(): lax.psum(jnp.sum(deviation * deviation, axis=(0, 1)), 'img') / total_count  40.6 us
    psum x1, blocking collectives, on_device(): lax.psum((jnp.sum(centred_grad, axis=(0, 1)), jnp.sum(centred_grad * cent...  40 us
    dot_general x1, matrix products, on_device(): jnp.dot(normed3, perceptron_entry_matrix, preferred_element_type=broadene...  36.3 us
    reduce_sum x2, other arithmetic, depthwise(): kernel[row_step, col_step]  33 us
    reduce_sum x5, other arithmetic, layer_norm(): return centre * lax.rsqrt(spread + EPS_NORM) * gain + shift  18 us
  transfers between devices with their start and end apart: 1, of which 1 were waited for; matrix products, arithmetic and copies ran while one was open for 6% of the time, Pallas kernels for 0%

commit v1 on v0

v1 whole, which is shorter than its diff:
```python
import math

import jax
import jax.numpy as jnp
from jax import lax
from jax.experimental import pallas as pl
from jax.experimental.pallas import tpu as pltpu
from jax.sharding import PartitionSpec as P

EPS_NORM = 1e-06
EPS_BATCH = 1e-05
EPS_UNIT = 1e-06
F32 = jnp.float32
BF16 = jnp.bfloat16
MESH = pl.DeviceIdType.MESH
G = 24
T = G * G
D = 384
FF = 1536
HEADS = 8
HD = 48
L = 128
PITCH = 32
PLANE = (G + 4) * PITCH
RC = 96
ROOT_HALF = 0.7071067811865476
ROOT_TWO_PI = 0.3989422804014327
NT = (((1,), (1,)), ((), ()))
TN = (((0,), (0,)), ((), ()))


def dot(a, b, dims=(((1,), (0,)), ((), ()))):
    return lax.dot_general(a, b, dims, preferred_element_type=F32)


def rows(start, size):
    return pl.ds(pl.multiple_of(start, 8), size)


def wide(v, times=3):
    return jnp.concatenate([v] * times, axis=1)


def fold8(v):
    return jnp.sum(v.reshape(v.shape[0] // 8, 8, v.shape[1]), axis=0)


def total(v):
    return jnp.sum(v, axis=0, keepdims=True)


def gelu_pair(u):
    phi = 0.5 + 0.5 * lax.erf(u * ROOT_HALF)
    bell = jnp.exp((u * u) * -0.5)
    return u * phi, phi + u * (bell * ROOT_TWO_PI)


def column_of(row):
    return jnp.broadcast_to(row, (L, D)).T


def write_mask(mask, edge):
    row_index = lax.broadcasted_iota(jnp.int32, (G, G, L), 0)
    col_index = lax.broadcasted_iota(jnp.int32, (G, G, L), 1)
    keep = (row_index < edge) & (col_index < edge)
    mask[...] = keep.astype(F32).reshape(T, L)


def write_sharp(sharp_mask, sharp):
    lane = lax.broadcasted_iota(jnp.int32, (HD, D), 1)
    for h in range(HEADS):
        own = (lane >= h * HD) & (lane < (h + 1) * HD)
        sharp_mask[h * HD : (h + 1) * HD, :] = jnp.where(own, sharp[h], 0.0)


def to_plane(plane, r, value):
    for g in range(RC // G):
        for c in range(3):
            plane[c, rows((r * (RC // G) + g + 2) * PITCH, G), :] = value[
                g * G : (g + 1) * G, c * L : (c + 1) * L
            ]


def row_count(n):
    return n // RC


def phase_a(i, edge, x, g1, b1, wqkv, bqkv, wm, bm, fm, g2, b2, st1, cb1,
            n1, ql, kl, vl, mixed, prob, score, sqk, m1, r1, resid1, vh2, r2, act, slope, stat,
            mask, sharp_mask, plane, plow):
    write_mask(mask, edge)

    def qkv_body(r, carry):
        sl = rows(r * RC, RC)
        xs = x[i, sl, :].astype(F32)
        mean = jnp.mean(xs, axis=1, keepdims=True)
        centre = xs - mean
        spread = lax.rsqrt(jnp.mean(centre * centre, axis=1, keepdims=True) + EPS_NORM)
        mk = wide(mask[sl, :])
        normed = ((centre * spread * g1[...] + b1[...]) * mk).astype(BF16)
        n1[i, sl, :] = normed
        m1[i, sl, :] = jnp.broadcast_to(mean, (RC, L))
        r1[i, sl, :] = jnp.broadcast_to(spread, (RC, L))
        sums = list(carry)
        for p, out in enumerate((ql, kl, vl)):
            cols = slice(p * D, (p + 1) * D)
            part = (dot(normed, wqkv[:, cols]) + bqkv[:, cols]) * mk
            if p < 2:
                sums[p] = sums[p] + fold8(part * part)
            out[i, sl, :] = part.astype(BF16)
        return tuple(sums)

    zero = jnp.zeros((8, D), F32)
    sums = lax.fori_loop(0, T // RC, qkv_body, (zero, zero))
    sq = lax.rsqrt(total(sums[0]) + EPS_UNIT)
    sk = lax.rsqrt(total(sums[1]) + EPS_UNIT)
    sqk[i, 0] = jnp.broadcast_to(sq, (8, D))
    sqk[i, 1] = jnp.broadcast_to(sk, (8, D))
    sqcol = column_of(sq)
    raw = dot(ql[i], kl[i], TN)
    for h in range(HEADS):
        band = slice(h * HD, (h + 1) * HD)
        sc = raw[band] * wide(sqcol[band]) * sk
        sh = sharp_mask[band, :]
        ex = jnp.where(sh > 0.0, jnp.exp(sc * sh), 0.0)
        pr = ex / jnp.sum(ex, axis=1, keepdims=True)
        score[i, band, :] = sc
        prob[i, band, :] = pr
        plow[band, :] = pr.astype(BF16)

    def mix_body(r, _):
        sl = rows(r * RC, RC)
        mk = wide(mask[sl, :])
        mx = dot(vl[i, sl, :], plow[...], NT).astype(BF16)
        mixed[i, sl, :] = mx
        branch = (dot(mx, wm[...]) + bm[...]) * mk
        res = x[i, sl, :].astype(F32) + fm[...] * branch
        resid1[i, sl, :] = res
        mean = jnp.mean(res, axis=1, keepdims=True)
        centre = res - mean
        spread = lax.rsqrt(jnp.mean(centre * centre, axis=1, keepdims=True) + EPS_NORM)
        vhat = centre * spread
        vh2[i, sl, :] = vhat
        r2[i, sl, :] = jnp.broadcast_to(spread, (RC, L))
        to_plane(plane, r, (vhat * g2[...] + b2[...]) * mk)
        return 0

    lax.fori_loop(0, T // RC, mix_body, 0)

    sums = []
    for c in range(3):
        cs = slice(c * L, (c + 1) * L)
        taps = [jnp.broadcast_to(st1[a, b : b + 1, cs], (G, L)) for a in range(3) for b in range(3)]

        def conv_body(r, carry):
            base = r * (4 * PITCH)
            outs = [None] * 4
            for a in range(6):
                for b in range(3):
                    v = plane[c, pl.ds(base + (a + 1) * PITCH - 1 + b, G), :]
                    for o in range(4):
                        if 0 <= a - o < 3:
                            t = v * taps[(a - o) * 3 + b]
                            outs[o] = t if outs[o] is None else outs[o] + t
            for o in range(4):
                sl = rows(r * (4 * G) + o * G, G)
                value, diff = gelu_pair(outs[o] + cb1[:, cs])
                value = value * mask[sl, :]
                act[i, sl, cs] = value
                slope[i, sl, cs] = diff.astype(slope.dtype)
                carry = carry + fold8(value)
            return carry

        sums.append(total(lax.fori_loop(0, G // 4, conv_body, jnp.zeros((8, L), F32))))
    count = (edge * edge).astype(F32)
    summed = jnp.concatenate(sums, axis=1)
    mean = summed / count

    def spread_body(r, carry):
        sl = rows(r * RC, RC)
        dev = (act[i, sl, :] - mean) * wide(mask[sl, :])
        return carry + fold8(dev * dev)

    square = total(lax.fori_loop(0, T // RC, spread_body, zero))
    stat[i, 0:1, :] = summed
    stat[i, 1:2, :] = square
    stat[i, 2:3, :] = jnp.full((1, D), count, F32)


def merge_stats(parts):
    summed = sum(p[0] for p in parts)
    count = sum(p[2] for p in parts)
    mean = summed / count
    square = sum(p[1] + p[2] * (p[0] / p[2] - mean) * (p[0] / p[2] - mean) for p in parts)
    return summed, square, count


def phase_b(i, edge, sens, resid1, act, bstat, bg, bo, st2, cb2, fl, g3, b3, w1, bb1, w2, bb2, fp,
            lout, rg, bng, dw1, dw2, sm_b, smf,
            mask, plane, plane2, res2, vh3, r3, n3, f2, hl, e1):
    write_mask(mask, edge)
    mean, inv, _ = bstat
    scale = inv * bg[...]
    shift = bo[...] - mean * scale

    def bn_body(r, _):
        sl = rows(r * RC, RC)
        to_plane(plane, r, (act[i, sl, :] * scale + shift) * wide(mask[sl, :]))
        return 0

    lax.fori_loop(0, T // RC, bn_body, 0)

    for c in range(3):
        cs = slice(c * L, (c + 1) * L)
        taps = [jnp.broadcast_to(st2[a, b : b + 1, cs], (G, L)) for a in range(3) for b in range(3)]

        def conv_body(r, _):
            base = r * (4 * PITCH)
            outs = [None] * 4
            for a in range(6):
                for b in range(3):
                    v = plane[c, pl.ds(base + (a + 1) * PITCH - 1 + b, G), :]
                    for o in range(4):
                        if 0 <= a - o < 3:
                            t = v * taps[(a - o) * 3 + b]
                            outs[o] = t if outs[o] is None else outs[o] + t
            for o in range(4):
                sl = rows(r * (4 * G) + o * G, G)
                local = (outs[o] + cb2[:, cs]) * mask[sl, :]
                res2[sl, cs] = resid1[i, sl, cs] + fl[:, cs] * local
            return 0

        lax.fori_loop(0, G // 4, conv_body, 0)

    def mlp_body(r, carry):
        gain_sum, shift_sum, bias_sum, local_sum, hidden_sum = carry
        sl = rows(r * RC, RC)
        mk = wide(mask[sl, :])
        res = res2[sl, :]
        mean = jnp.mean(res, axis=1, keepdims=True)
        centre = res - mean
        spread = lax.rsqrt(jnp.mean(centre * centre, axis=1, keepdims=True) + EPS_NORM)
        vhat = centre * spread
        vh3[sl, :] = vhat
        normed = ((vhat * g3[...] + b3[...]) * mk).astype(BF16)
        n3[sl, :] = normed
        og = sens[i, sl, :].astype(F32) * mk
        err = og * fp[...]
        bias_sum = bias_sum + fold8(err)
        low = err.astype(BF16)
        f2[sl, :] = low
        hidden_parts = []
        branch = None
        back = None
        for j in range(FF // 256):
            cols = slice(j * 256, (j + 1) * 256)
            pre = dot(normed, w1[:, cols]) + bb1[:, cols]
            value, diff = gelu_pair(pre)
            value = value.astype(BF16)
            hl[sl, cols] = value
            t = dot(value, w2[cols, :])
            branch = t if branch is None else branch + t
            he = dot(low, w2[cols, :], NT) * diff
            hidden_parts.append(fold8(he))
            he = he.astype(BF16)
            e1[sl, cols] = he
            t = dot(he, w1[:, cols], NT)
            back = t if back is None else back + t
        hidden_sum = hidden_sum + jnp.concatenate(hidden_parts, axis=1)
        lout[i, sl, :] = ((res + fp[...] * (branch + bb2[...])) * mk).astype(BF16)
        err = back * mk
        shift_sum = shift_sum + fold8(err)
        gain_sum = gain_sum + fold8(err * vhat)
        eg = err * g3[...]
        mean1 = jnp.mean(eg, axis=1, keepdims=True)
        mean2 = jnp.mean(eg * vhat, axis=1, keepdims=True)
        grad = og + spread * (eg - mean1 - vhat * mean2)
        rg[i, sl, :] = grad
        local = grad * mk * fl[...]
        local_sum = local_sum + fold8(local)
        to_plane(plane2, r, local)
        return gain_sum, shift_sum, bias_sum, local_sum, hidden_sum

    zero = jnp.zeros((8, D), F32)
    sums = lax.fori_loop(0, T // RC, mlp_body, (zero, zero, zero, zero, jnp.zeros((8, FF), F32)))
    for k in range(4):
        sm_b[k] += sums[k]
    smf[...] += sums[4]
    dw1[...] += dot(n3[...], e1[...], TN)
    dw2[...] += dot(hl[...], f2[...], TN)

    for c in range(3):
        cs = slice(c * L, (c + 1) * L)
        taps = [jnp.broadcast_to(st2[a, b : b + 1, cs], (G, L)) for a in range(3) for b in range(3)]

        def back_body(r, carry):
            kernel, gain, shift_s = list(carry[:9]), carry[9], carry[10]
            base = r * (3 * PITCH)
            outs = [None] * 3
            vs = [plane[c, rows(base + (o + 2) * PITCH, G), :] for o in range(3)]
            for a in range(5):
                for b in range(3):
                    v = plane2[c, pl.ds(base + (a + 1) * PITCH - 1 + b, G), :]
                    for o in range(3):
                        if 0 <= a - o < 3:
                            k = (2 - (a - o)) * 3 + (2 - b)
                            t = v * taps[k]
                            outs[o] = t if outs[o] is None else outs[o] + t
                            kernel[k] = kernel[k] + fold8(v * vs[o])
            for o in range(3):
                sl = rows(r * (3 * G) + o * G, G)
                grad = outs[o] * mask[sl, :]
                bng[i, sl, cs] = grad
                centred = (act[i, sl, cs] - mean[:, cs]) * inv[:, cs]
                gain = gain + fold8(grad * centred)
                shift_s = shift_s + fold8(grad)
            return tuple(kernel) + (gain, shift_s)

        init = tuple(jnp.zeros((8, L), F32) for _ in range(11))
        found = lax.fori_loop(0, G // 3, back_body, init)
        for k in range(11):
            sm_b[4 + k, :, cs] += found[k]


def phase_c(i, edge, x, n1, ql, kl, vl, mixed, prob, score, sqk, m1, r1, rg, vh2, r2, act, slope, bng,
            bstat, bsum, bg, st1, fm, g2, b2, wm, g1, wqkv,
            gin, dwm, dwqkv, sm_c, smq, srow,
            mask, sharp_mask, back, plane2, plow, mgrad, alow, qkvl, rg1):
    write_mask(mask, edge)
    mean, inv, count = bstat
    gain_all, shift_all = bsum
    zero = jnp.zeros((8, D), F32)
    coef = inv * bg[...]
    by_centred = gain_all / count * inv
    const = shift_all / count - mean * by_centred

    def bn_body(r, carry):
        sl = rows(r * RC, RC)
        mk = wide(mask[sl, :])
        grad = (bng[i, sl, :] - const - act[i, sl, :] * by_centred) * coef
        err = grad * mk * slope[i, sl, :].astype(F32)
        to_plane(plane2, r, err)
        return carry + fold8(err)

    sm_c[14] += lax.fori_loop(0, T // RC, bn_body, zero)

    for c in range(3):
        cs = slice(c * L, (c + 1) * L)
        taps = [jnp.broadcast_to(st1[a, b : b + 1, cs], (G, L)) for a in range(3) for b in range(3)]

        def back_body(r, carry):
            kernel = list(carry)
            base = r * (3 * PITCH)
            outs = [None] * 3
            vs = []
            for o in range(3):
                sl = rows(r * (3 * G) + o * G, G)
                vs.append((vh2[i, sl, cs] * g2[:, cs] + b2[:, cs]) * mask[sl, :])
            for a in range(5):
                for b in range(3):
                    v = plane2[c, pl.ds(base + (a + 1) * PITCH - 1 + b, G), :]
                    for o in range(3):
                        if 0 <= a - o < 3:
                            k = (2 - (a - o)) * 3 + (2 - b)
                            t = v * taps[k]
                            outs[o] = t if outs[o] is None else outs[o] + t
                            kernel[k] = kernel[k] + fold8(v * vs[o])
            for o in range(3):
                sl = rows(r * (3 * G) + o * G, G)
                back[sl, cs] = outs[o] * mask[sl, :]
            return tuple(kernel)

        init = tuple(jnp.zeros((8, L), F32) for _ in range(9))
        found = lax.fori_loop(0, G // 3, back_body, init)
        for k in range(9):
            sm_c[5 + k, :, cs] += found[k]

    def norm_body(r, carry):
        gain_sum, shift_sum, bias_sum = carry
        sl = rows(r * RC, RC)
        mk = wide(mask[sl, :])
        err = back[sl, :]
        vhat = vh2[i, sl, :]
        shift_sum = shift_sum + fold8(err)
        gain_sum = gain_sum + fold8(err * vhat)
        eg = err * g2[...]
        mean1 = jnp.mean(eg, axis=1, keepdims=True)
        mean2 = jnp.mean(eg * vhat, axis=1, keepdims=True)
        grad = rg[i, sl, :] + wide(r2[i, sl, :]) * (eg - mean1 - vhat * mean2)
        rg1[sl, :] = grad
        err = grad * mk * fm[...]
        bias_sum = bias_sum + fold8(err)
        low = err.astype(BF16)
        plow[sl, :] = low
        mgrad[sl, :] = dot(low, wm[...], NT).astype(BF16)
        return gain_sum, shift_sum, bias_sum

    sums = lax.fori_loop(0, T // RC, norm_body, (zero, zero, zero))
    for k in range(3):
        sm_c[2 + k] += sums[k]
    dwm[...] += dot(mixed[i], plow[...], TN)

    raw = dot(mgrad[...], vl[i], TN)
    sq, sk = sqk[i, 0, 0:1, :], sqk[i, 1, 0:1, :]
    sqcol = column_of(sq)
    colsum = zero
    rowsums = []
    for h in range(HEADS):
        band = slice(h * HD, (h + 1) * HD)
        pr = prob[i, band, :]
        weighted = raw[band] * pr
        logit = weighted - pr * jnp.sum(weighted, axis=1, keepdims=True)
        sc = score[i, band, :]
        sh = sharp_mask[band, :]
        lg = logit * sh
        cross = lg * sc
        rowsums.append(jnp.sum(cross, axis=1, keepdims=True))
        colsum = colsum + fold8(cross)
        alow[band, :] = (lg * wide(sqcol[band]) * sk).astype(BF16)
        plow[band, :] = pr.astype(BF16)
    rowcol = jnp.concatenate(rowsums, axis=0)
    rowrow = jnp.broadcast_to(rowcol, (D, L)).T[0:1, :]
    srow[...] += rowrow
    cq = sq * sq * rowrow
    ck = sk * sk * total(colsum)

    def qkv_body(r, carry):
        sums = list(carry)
        sl = rows(r * RC, RC)
        qv, kv = ql[i, sl, :], kl[i, sl, :]
        grads = (
            dot(kv, alow[...], NT) - qv.astype(F32) * cq,
            dot(qv, alow[...]) - kv.astype(F32) * ck,
            dot(mgrad[sl, :], plow[0:D, :]),
        )
        for p in range(3):
            sums[p] = sums[p] + fold8(grads[p])
            qkvl[sl, p * D : (p + 1) * D] = grads[p].astype(BF16)
        return tuple(sums)

    sums = lax.fori_loop(0, T // RC, qkv_body, (zero, zero, zero))
    for p in range(3):
        smq[:, p * D : (p + 1) * D] += sums[p]
    dwqkv[...] += dot(n1[i], qkvl[...], TN)

    def in_body(r, carry):
        gain_sum, shift_sum = carry
        sl = rows(r * RC, RC)
        err = dot(qkvl[sl, :], wqkv[...], NT) * wide(mask[sl, :])
        spread = wide(r1[i, sl, :])
        vhat = (x[i, sl, :].astype(F32) - wide(m1[i, sl, :])) * spread
        shift_sum = shift_sum + fold8(err)
        gain_sum = gain_sum + fold8(err * vhat)
        eg = err * g1[...]
        mean1 = jnp.mean(eg, axis=1, keepdims=True)
        mean2 = jnp.mean(eg * vhat, axis=1, keepdims=True)
        gin[i, sl, :] = (rg1[sl, :] + spread * (eg - mean1 - vhat * mean2)).astype(BF16)
        return gain_sum, shift_sum

    sums = lax.fori_loop(0, T // RC, in_body, (zero, zero))
    for k in range(2):
        sm_c[k] += sums[k]


def exchange_kernel(n, payload, gathered, buf, send_sem, recv_sem):
    me = lax.axis_index("img")
    barrier = pltpu.get_barrier_semaphore()

    def other(k):
        return (lax.rem(me + k, n),)

    def signal(k, _):
        pl.semaphore_signal(barrier, inc=1, device_id=other(k), device_id_type=MESH)
        return 0

    lax.fori_loop(1, n, signal, 0)
    pl.semaphore_wait(barrier, n - 1)

    def copy(k):
        return pltpu.make_async_remote_copy(
            src_ref=payload,
            dst_ref=buf.at[me],
            send_sem=send_sem,
            recv_sem=recv_sem,
            device_id=other(k),
            device_id_type=MESH,
        )

    def start(k, _):
        copy(k).start()
        return 0

    lax.fori_loop(1, n, start, 0)
    buf[me] = payload[...]
    most = buf.at[pl.ds(0, n - 1)]
    pltpu.make_async_copy(most, most, send_sem).wait()
    pltpu.make_async_copy(most, most, recv_sem).wait()
    gathered[...] = buf[...]


def exchange(n, payload, ident):
    return pl.pallas_call(
        lambda *refs: exchange_kernel(n, *refs),
        out_shape=jax.ShapeDtypeStruct((n,) + payload.shape, F32),
        in_specs=[pl.BlockSpec(memory_space=pltpu.VMEM)],
        out_specs=pl.BlockSpec(memory_space=pltpu.VMEM),
        scratch_shapes=[
            pltpu.VMEM((n,) + payload.shape, F32),
            pltpu.SemaphoreType.DMA,
            pltpu.SemaphoreType.DMA,
        ],
        compiler_params=pltpu.CompilerParams(collective_id=ident, has_side_effects=True),
    )(payload)


def stack_rows(row):
    return [row[:, c * L : (c + 1) * L] for c in range(3)]


def unstack_rows(ref, k, first):
    return jnp.concatenate([ref[k, first + c : first + c + 1, :] for c in range(3)], axis=1)


def on_device(n, x, sens, edges, g1, b1, wqkv, bqkv, sharp, wm, bm, fm, g2, b2, st1, cb1, bg, bo, st2, cb2, fl, g3, b3,
              w1, bb1, w2, bb2, fp):
    images = x.shape[0]
    sharp_in = sharp
    g1, b1, bqkv, bm, fm, g2, b2, cb1, bg, bo, cb2, fl, g3, b3, bb1, bb2, fp = (
        v.reshape(1, v.shape[0]) for v in (g1, b1, bqkv, bm, fm, g2, b2, cb1, bg, bo, cb2, fl, g3, b3, bb1, bb2, fp)
    )
    S = jax.ShapeDtypeStruct
    vm = pl.BlockSpec(memory_space=pltpu.VMEM)
    sm = pl.BlockSpec(memory_space=pltpu.SMEM)
    cp = pltpu.CompilerParams(vmem_limit_bytes=60 * 1024 * 1024)
    full = lambda t: S((images, T, D), t)
    lanes = S((images, T, L), F32)
    square = S((images, D, D), F32)

    def kernel_a(edges, sharp, x, g1, b1, wqkv, bqkv, wm, bm, fm, g2, b2, st1, cb1,
                 n1, ql, kl, vl, mixed, prob, score, sqk, m1, r1, resid1, vh2, r2, act, slope, payload,
                 mask, sharp_mask, plane, plow, stat):
        write_sharp(sharp_mask, sharp)
        plane[...] = jnp.zeros_like(plane)

        def body(i, _):
            phase_a(i, edges[i], x, g1, b1, wqkv, bqkv, wm, bm, fm, g2, b2, st1, cb1,
                    n1, ql, kl, vl, mixed, prob, score, sqk, m1, r1, resid1, vh2, r2, act, slope, stat,
                    mask, sharp_mask, plane, plow)
            return 0

        lax.fori_loop(0, images, body, 0)
        merged = merge_stats([tuple(stat[i, k : k + 1, :] for k in range(3)) for i in range(images)])
        out = stack_rows(merged[0]) + stack_rows(merged[1]) + [merged[2][:, 0:L], jnp.zeros((1, L), F32)]
        payload[...] = jnp.concatenate(out, axis=0)

    (n1, ql, kl, vl, mixed, prob, score, sqk, m1, r1, resid1, vh2, r2, act, slope, payload) = pl.pallas_call(
        kernel_a,
        in_specs=[sm, sm] + [vm] * 12,
        out_specs=[vm] * 16,
        out_shape=[full(BF16)] * 5 + [square, square, S((images, 2, 8, D), F32), lanes, lanes, full(F32), full(F32), lanes,
                   full(F32), full(BF16), S((8, L), F32)],
        scratch_shapes=[pltpu.VMEM((T, L), F32), pltpu.VMEM((D, D), F32), pltpu.VMEM((3, PLANE, L), F32),
                        pltpu.VMEM((D, D), BF16), pltpu.VMEM((images, 8, D), F32)],
        compiler_params=cp,
    )(edges, sharp, x, g1, b1, wqkv, bqkv, wm, bm, fm, g2, b2, st1, cb1)

    gathered = exchange(n, payload, 0)

    def kernel_b(edges, gathered, sens, resid1, act, bg, bo, st2, cb2, fl, g3, b3, w1, bb1, w2, bb2, fp,
                 lout, rg, bng, dw1, dw2, small, hidden_bias, stats, payload,
                 mask, plane, plane2, res2, vh3, r3, n3, f2, hl, e1, sm_b, smf):
        merged = merge_stats([
            (unstack_rows(gathered, k, 0), unstack_rows(gathered, k, 3), wide(gathered[k, 6:7, :])) for k in range(n)
        ])
        count = merged[2]
        mean = merged[0] / count
        inv = lax.rsqrt(merged[1] / count + EPS_BATCH)
        stats[...] = jnp.concatenate([mean, inv, count, jnp.zeros((5, D), F32)], axis=0)
        plane[...] = jnp.zeros_like(plane)
        plane2[...] = jnp.zeros_like(plane2)
        sm_b[...] = jnp.zeros_like(sm_b)
        smf[...] = jnp.zeros_like(smf)
        dw1[...] = jnp.zeros_like(dw1)
        dw2[...] = jnp.zeros_like(dw2)

        def body(i, _):
            bstat = (stats[0:1, :], stats[1:2, :], stats[2:3, :])
            phase_b(i, edges[i], sens, resid1, act, bstat, bg, bo, st2, cb2, fl, g3, b3, w1, bb1, w2, bb2, fp,
                    lout, rg, bng, dw1, dw2, sm_b, smf,
                    mask, plane, plane2, res2, vh3, r3, n3, f2, hl, e1)
            return 0

        lax.fori_loop(0, images, body, 0)
        sums = [total(sm_b[k]) for k in range(15)]
        small[...] = jnp.concatenate(sums + [jnp.zeros((1, D), F32)], axis=0)
        hidden_bias[...] = total(smf[...])
        payload[...] = jnp.concatenate(stack_rows(sums[13]) + stack_rows(sums[14]) + [jnp.zeros((2, L), F32)], axis=0)

    lout, rg, bng, dw1, dw2, small_b, hidden_bias, stats, payload2 = pl.pallas_call(
        kernel_b,
        in_specs=[sm] + [vm] * 16,
        out_specs=[vm] * 9,
        out_shape=[full(BF16), full(F32), full(F32), S((D, FF), F32), S((FF, D), F32), S((16, D), F32), S((1, FF), F32),
                   S((8, D), F32), S((8, L), F32)],
        scratch_shapes=[pltpu.VMEM((T, L), F32), pltpu.VMEM((3, PLANE, L), F32), pltpu.VMEM((3, PLANE, L), F32),
                        pltpu.VMEM((T, D), F32), pltpu.VMEM((T, D), F32), pltpu.VMEM((T, L), F32),
                        pltpu.VMEM((T, D), BF16), pltpu.VMEM((T, D), BF16), pltpu.VMEM((T, FF), BF16),
                        pltpu.VMEM((T, FF), BF16), pltpu.VMEM((15, 8, D), F32), pltpu.VMEM((8, FF), F32)],
        compiler_params=cp,
    )(edges, gathered, sens, resid1, act, bg, bo, st2, cb2, fl, g3, b3, w1, bb1, w2, bb2, fp)

    gathered2 = exchange(n, payload2, 1)

    def kernel_c(edges, sharp, gathered, stats, x, n1, ql, kl, vl, mixed, prob, score, sqk, m1, r1, rg, vh2, r2, act, slope,
                 bng, bg, st1, fm, g2, b2, wm, g1, wqkv,
                 gin, dwm, dwqkv, small, qkv_bias, srow,
                 mask, sharp_mask, back, plane2, plow, mgrad, alow, qkvl, rg1, sm_c, smq, bsums):
        summed = gathered[0]
        for k in range(1, n):
            summed = summed + gathered[k]
        bsums[0:1, :] = jnp.concatenate([summed[c : c + 1] for c in range(3)], axis=1)
        bsums[1:2, :] = jnp.concatenate([summed[c : c + 1] for c in range(3, 6)], axis=1)
        write_sharp(sharp_mask, sharp)
        plane2[...] = jnp.zeros_like(plane2)
        sm_c[...] = jnp.zeros_like(sm_c)
        smq[...] = jnp.zeros_like(smq)
        srow[...] = jnp.zeros_like(srow)
        dwm[...] = jnp.zeros_like(dwm)
        dwqkv[...] = jnp.zeros_like(dwqkv)

        def body(i, _):
            bstat = (stats[0:1, :], stats[1:2, :], stats[2:3, :])
            bsum = (bsums[0:1, :], bsums[1:2, :])
            phase_c(i, edges[i], x, n1, ql, kl, vl, mixed, prob, score, sqk, m1, r1, rg, vh2, r2, act, slope, bng,
                    bstat, bsum, bg, st1, fm, g2, b2, wm, g1, wqkv,
                    gin, dwm, dwqkv, sm_c, smq, srow,
                    mask, sharp_mask, back, plane2, plow, mgrad, alow, qkvl, rg1)
            return 0

        lax.fori_loop(0, images, body, 0)
        small[...] = jnp.concatenate([total(sm_c[k]) for k in range(15)] + [jnp.zeros((1, D), F32)], axis=0)
        qkv_bias[...] = total(smq[...])

    gin, dwm, dwqkv, small_c, qkv_bias, srow = pl.pallas_call(
        kernel_c,
        in_specs=[sm, sm] + [vm] * 27,
        out_specs=[vm] * 6,
        out_shape=[full(BF16), S((D, D), F32), S((D, 3 * D), F32), S((16, D), F32), S((1, 3 * D), F32), S((1, D), F32)],
        scratch_shapes=[pltpu.VMEM((T, L), F32), pltpu.VMEM((D, D), F32), pltpu.VMEM((T, D), F32),
                        pltpu.VMEM((3, PLANE, L), F32), pltpu.VMEM((T, D), BF16), pltpu.VMEM((T, D), BF16),
                        pltpu.VMEM((D, D), BF16), pltpu.VMEM((T, 3 * D), BF16), pltpu.VMEM((T, D), F32),
                        pltpu.VMEM((15, 8, D), F32), pltpu.VMEM((8, 3 * D), F32), pltpu.VMEM((8, D), F32)],
        compiler_params=cp,
    )(edges, sharp, gathered2, stats, x, n1, ql, kl, vl, mixed, prob, score, sqk, m1, r1, rg, vh2, r2, act, slope, bng,
      bg, st1, fm, g2, b2, wm, g1, wqkv)

    small_b, small_c, hidden_bias, qkv_bias, srow, dwm, dwqkv, dw1, dw2 = lax.psum(
        (small_b, small_c, hidden_bias, qkv_bias, srow, dwm, dwqkv, dw1, dw2), "img"
    )
    proj_bias = small_c[4]
    scale_attn = (jnp.sum(dwm * wm.astype(F32), axis=0) + bm[0] * proj_bias) / fm[0]
    conv2_kernel = small_b[4:13].reshape(3, 3, D)
    conv2_bias = small_b[3]
    scale_local = (jnp.sum(conv2_kernel * st2, axis=(0, 1)) + cb2[0] * conv2_bias) / fl[0]
    fc2_bias = small_b[2]
    scale_mlp = (jnp.sum(dw2 * w2.astype(F32), axis=0) + bb2[0] * fc2_bias) / fp[0]
    sharp_grad = jnp.sum(srow.reshape(HEADS, HD), axis=1) / sharp_in
    return (lout, gin, small_c[0], small_c[1], dwqkv, qkv_bias[0], sharp_grad, dwm, proj_bias, scale_attn,
            small_c[2], small_c[3], small_c[5:14].reshape(3, 3, D), small_c[14], small_b[13], small_b[14],
            conv2_kernel, conv2_bias, scale_local, small_b[0], small_b[1], dw1, hidden_bias[0], dw2, fc2_bias, scale_mlp)


def solution(mesh):
    n = mesh.shape["img"]
    split = P("img", None, None)
    return jax.shard_map(
        lambda *args: on_device(n, *args),
        mesh=mesh,
        in_specs=(split, split, P("img")) + (P(),) * 24,
        out_specs=(split, split) + (P(),) * 24,
        check_vma=False,
    )
```

time: 629 us -> 406 us (0.65)
  Pallas kernels: 0 us -> 198 us
  other arithmetic: 149 us -> 4.73 us
  matrix products: 141 us -> 0 us
  blocking collectives: 166 us -> 43.9 us
  local copies, waits for them, and re-layouts: 69 us -> 23.6 us
  waiting for transfers between devices: 81.9 us -> 121 us
    pallas_call x0 -> x5, Pallas kernels: none -> 198 us  [the longest x1 74.3 us: on_device(): pl.pallas_call(kernel_b, in_specs=[sm] + [vm] * 16, out_specs=[vm] * 9, o...]
    dot_general x18 -> x0, matrix products: 141 us -> none  [the longest x1 36.3 us: on_device(): jnp.dot(normed3, perceptron_entry_matrix, preferred_element_type=broadene...]
    psum x4 -> x1, blocking collectives: 166 us -> 43.9 us  [on_device(): lax.psum((small_b, small_c, hidden_bias, qkv_bias, srow, dwm, dwqkv, dw1,...]
    reduce_sum x20 -> x4, other arithmetic: 95.9 us -> 2.38 us  [the longest x1 2.14 us: on_device(): jnp.sum(dw2 * w2.astype(F32), axis=0) + bb2[0] * fc2_bias]
    psum x1, waiting for transfers between devices: 81.9 us -> 120 us  [on_device(): lax.psum((small_b, small_c, hidden_bias, qkv_bias, srow, dwm, dwqkv, dw1,...]
    add_any x6 -> x0, other arithmetic: 16.6 us -> none  [the longest x2 9.96 us: unit_columns(): value * value]
    concatenate x3 -> x0, local copies, waits for them, and re-layouts: 16.4 us -> none  [on_device(): jnp.concatenate((query_grad.reshape(row_shape), key_grad.reshape(row_shap...]
    slice x6 -> x3, local copies, waits for them, and re-layouts: 16.3 us -> 0.66 us  [the longest x1 0.65 us: on_device(): fc2_bias = small_b[2]]
  transfers between devices with their start and end apart: 1 -> 1, of which waited for: 1 -> 1; matrix products, arithmetic and copies ran while one was open for 6% -> 1% of each run, Pallas kernels for 0% -> 0%
where the time goes in v1:
time: 406 us; the launch traced here: 405 us
  Pallas kernels  198 us (49%)
  waiting for transfers between devices  121 us (30%)
  blocking collectives  43.9 us (11%)
  local copies, waits for them, and re-layouts  23.6 us (6%)
  between operations  14.4 us (4%)
  other arithmetic  4.73 us (1%)
    psum x1, waiting for transfers between devices, on_device(): lax.psum((small_b, small_c, hidden_bias, qkv_bias, srow, dwm, dwqkv, dw1,...  120 us
    pallas_call x1, Pallas kernels, on_device(): pl.pallas_call(kernel_b, in_specs=[sm] + [vm] * 16, out_specs=[vm] * 9, o...  74.3 us
    pallas_call x1, Pallas kernels, on_device(): pl.pallas_call(kernel_c, in_specs=[sm, sm] + [vm] * 27, out_specs=[vm] *...  56.7 us
    pallas_call x1, Pallas kernels, on_device(): pl.pallas_call(kernel_a, in_specs=[sm, sm] + [vm] * 12, out_specs=[vm] *...  45.9 us
    psum x1, blocking collectives, on_device(): lax.psum((small_b, small_c, hidden_bias, qkv_bias, srow, dwm, dwqkv, dw1,...  43.9 us
    pallas_call x2, Pallas kernels, exchange(): pl.pallas_call(lambda *refs: exchange_kernel(n, *refs), out_shape=jax.Sha...  21.4 us
    reshape x17, local copies, waits for them, and re-layouts, on_device(): v.reshape(1, v.shape[0])  15.1 us
  transfers between devices with their start and end apart: 1, of which 1 were waited for; matrix products, arithmetic and copies ran while one was open for 1% of the time, Pallas kernels for 0%

profile of v1, /device:TPU:0, one launch (start us, length us, event | category | flops | bytes accessed | tf_op | source)
XLA Modules:
  0.0 405.4 jit_solution(14556537313985357768)
XLA Ops:
  7.2 0.0 copy-start.22
  7.2 0.0 copy-start.16
  7.2 0.0 copy-start.23
  7.2 0.0 copy-start.10
  7.2 0.0 copy-start.11
  7.3 0.0 copy-start.24
  7.3 0.0 copy-start.25
  7.3 0.0 copy-start.12
  7.3 0.0 copy-start.13
  7.3 0.0 all-reduce.4.cloned.1.call-start
  7.3 1.3 reshape.112.g1
  8.6 1.2 reshape.116.fm
  9.8 1.2 reshape.117.g2
  11.1 1.2 reshape.118.b2
  12.3 1.3 reshape.114.bqkv
  13.6 1.2 reshape.113.b1
  14.9 1.2 reshape.115.bm
  16.1 1.2 reshape.119.cb1
  17.4 45.9 %shard_map.458 = (bf16[4,576,384]{2,1,0:T(8,128)(2,1)}, bf16[4,576,384]{2,1,0:T(8,128)(2,1)}, bf16[4,576,384]{2,1,0:T(8,128)(2,1)}, bf16[4,576,384]{2,1,0:T(8,12...) custom-call(s32[4]{0:T(128)} %edges.5, f32[8]{0:T(128)} %sharp.3, ...), custom_call_target="tpu_custom_call" | custom-call | tf_op jit(solution)/shard_map/pallas_call | solution.py:556
  63.2 11.3 %shard_map.459.gathered = f32[32,8,128]{2,1,0:T(8,128)} custom-call(f32[8,128]{1,0:T(8,128)} %get-tuple-element.57.refs_0_), custom_call_target="tpu_custom_call" | custom-call | tf_op jit(solution)/shard_map/pallas_call | solution.py:502
  74.5 0.6 reshape.120.bg
  75.1 0.6 reshape.126.bb1
  75.7 0.6 reshape.121.bo
  76.3 0.6 reshape.122.cb2
  76.8 0.6 reshape.123.fl
  77.4 0.6 reshape.124.g3
  78.0 0.6 reshape.125.b3
  78.5 0.6 reshape.127.bb2
  79.1 0.0 copy-done.13
  79.1 0.6 reshape.128.fp
  79.7 74.3 %shard_map.460 = (bf16[4,576,384]{2,1,0:T(8,128)(2,1)}, f32[4,576,384]{2,1,0:T(8,128)}, f32[4,576,384]{2,1,0:T(8,128)}, f32[384,1536]{1,0:T(8,128)}, f32[1536,38...) custom-call(s32[4]{0:T(128)} %edges.5, ...), custom_call_target="tpu_custom_call" | custom-call | tf_op jit(solution)/shard_map/pallas_call | solution.py:599
  154.0 10.1 %shard_map.461.gathered = f32[32,8,128]{2,1,0:T(8,128)} custom-call(f32[8,128]{1,0:T(8,128)} %get-tuple-element.61.refs_0_), custom_call_target="tpu_custom_call" | custom-call | tf_op jit(solution)/shard_map/pallas_call | solution.py:502
  164.1 56.7 %shard_map.462 = (bf16[4,576,384]{2,1,0:T(8,128)(2,1)}, f32[384,384]{1,0:T(8,128)}, f32[384,1152]{1,0:T(8,128)}, f32[16,384]{1,0:T(8,128)}, f32[1,1152]{1,0:T(1,128)}, /*index=5*/f32[1,384]{1,0:T(1,128)}) custom-call(s32[4]{0:T(128)} %edges.5, f32[8]{0:T(128)} %sharp.3, f32[32,8,128]{2,1,0:T(8,128)} %shard_map.461.gathered, ...), custom_call_target="tpu_custom_call" | custom-call | tf_op jit(solution)/shard_map/pallas_call | solution.py:644
  220.8 0.0 copy-start.21
  220.8 0.0 copy-start.27
  220.9 0.0 copy-start.20
  220.9 0.0 copy-start.26
  220.9 0.0 copy-start.7
  220.9 0.0 copy-start.1
  220.9 0.0 all-reduce.4.cloned.1.call-update
  220.9 0.6 copy-done.21
  221.6 0.1 reshape.129
  221.7 43.9 %all-reduce = (f32[16,384]{1,0:T(8,128)S(1)}, f32[1152]{0:T(1024)}, f32[8,48]{1,0:T(8,128)S(1)}, f32[16,384]{1,0:T(8,128)S(1)}, f32[1536]{0:T(1024)}) all-reduce(f32[16,384]{1,0:T(8,128)S(1)} %copy-done.9, f32[1152]{0:T(1024)S(1)} %reduce.2, f32[8,48]{1,0:T(8,128)S(1)} %reshape.129, ...), channel_id=1, replica_groups=mesh['img'=32] {'img'}, use_global_device_ids=true, to_apply=%region_0.0 | all-reduce | flops 15360 | bytes 122880 | tf_op jit(solution)/shard_map/psum | solution.py:657
  265.6 0.6 reshape.130
  266.2 0.1 reduce_sum.36
  266.3 0.0 copy-done.26
  266.3 0.5 div.12
  266.9 0.0 copy-done.7
  266.9 0.6 slice_reduce_fusion
  267.5 0.6 add_divide_fusion.1
  268.1 120.5 %all-reduce.4.cloned.1.call-done = (f32[384,1152]{1,0:T(8,128)}, f32[384,384]{1,0:T(8,128)}, f32[384,1536]{1,0:T(8,128)}, f32[1536,384]{1,0:T(8,128)}) async-done(((f32[384,1152]{1,0:T(8,128)}, f32[384,384]{1,0:T(8,128)}, f32[384,1536]{1,0:T(8,128)}, f32[1536,384]{1,0:T(8,128)}), (f32[384,1152]{1,0:T(8,128)}, f32[384,384]{1,0:T(8,128)}, f32[384,1536]{1,0:T(8,128)}, ...) | async-done | bytes 7077904 | tf_op jit(solution)/shard_map/psum | solution.py:657
  388.6 0.0 copy-start.15
  388.7 2.1 multiply_reduce_fusion
  390.8 0.1 multiply_reduce_fusion.1
  390.9 0.0 copy-done.17
  390.9 0.6 add_divide_fusion
  391.5 0.0 copy-done.14
  391.5 0.6 add_divide_fusion.2
  392.1 1.2 copy.57
  393.3 0.8 copy.58
  394.1 0.5 copy-done.3
  394.6 1.4 copy.59
  396.0 1.1 copy-done
  397.2 1.4 copy.60
  (39 shorter events, 0.2 us)
Async XLA Ops:
  7.2 67.3 %copy-start.22 = (f32[384]{0:T(512)S(1)}, f32[384]{0:T(512)}, u32[]{:S(2)}) copy-start(f32[384]{0:T(512)} %param.42) | copy-start | bytes 4612
  7.2 67.9 %copy-start.16 = (f32[1536]{0:T(1024)S(1)}, f32[1536]{0:T(1024)}, u32[]{:S(2)}) copy-start(f32[1536]{0:T(1024)} %param.50) | copy-start | bytes 18436
  7.2 68.5 %copy-start.23 = (f32[384]{0:T(512)S(1)}, f32[384]{0:T(512)}, u32[]{:S(2)}) copy-start(f32[384]{0:T(512)} %param.43) | copy-start | bytes 4612
  7.2 69.0 %copy-start.10 = (f32[384]{0:T(512)S(1)}, f32[384]{0:T(512)}, u32[]{:S(2)}) copy-start(f32[384]{0:T(512)} %param.45) | copy-start | bytes 4612
  7.2 69.6 %copy-start.11 = (f32[384]{0:T(512)S(1)}, f32[384]{0:T(512)}, u32[]{:S(2)}) copy-start(f32[384]{0:T(512)} %param.46) | copy-start | bytes 4612
  7.3 70.2 %copy-start.24 = (f32[384]{0:T(512)S(1)}, f32[384]{0:T(512)}, u32[]{:S(2)}) copy-start(f32[384]{0:T(512)} %param.47) | copy-start | bytes 4612
  7.3 70.7 %copy-start.25 = (f32[384]{0:T(512)S(1)}, f32[384]{0:T(512)}, u32[]{:S(2)}) copy-start(f32[384]{0:T(512)} %param.48) | copy-start | bytes 4612
  7.3 71.3 %copy-start.12 = (f32[384]{0:T(512)S(1)}, f32[384]{0:T(512)}, u32[]{:S(2)}) copy-start(f32[384]{0:T(512)} %param.52) | copy-start | bytes 4612
  7.3 71.8 %copy-start.13 = (f32[384]{0:T(512)S(1)}, f32[384]{0:T(512)}, u32[]{:S(2)}) copy-start(f32[384]{0:T(512)} %param.53) | copy-start | bytes 4612
  7.3 381.3 %all-reduce.4.cloned.1.call-start = ((), (), s32[]{:S(2)}) async-start(), calls=%async_computation | async-start | bytes 14155776 | tf_op jit(solution)/shard_map/psum | solution.py:657
  220.8 0.7 copy-start.21
  220.8 0.7 copy-start.27
  220.9 0.8 copy-start.20
  220.9 0.8 copy-start.8
  220.9 0.8 copy-start.9
  220.9 45.5 %copy-start.26 = (f32[8]{0:T(128)S(1)}, f32[8]{0:T(128)}, u32[]{:S(2)}) copy-start(f32[8]{0:T(128)} %sharp.3) | copy-start | bytes 100
  220.9 46.0 %copy-start.7 = (f32[3,3,384]{2,1,0:T(4,128)S(1)}, f32[3,3,384]{2,1,0:T(4,128)}, u32[]{:S(2)}) copy-start(f32[3,3,384]{2,1,0:T(4,128)} %st2.1) | copy-start | bytes 41476
  220.9 167.7 %copy-start.1 = (bf16[1536,384]{1,0:T(8,128)(2,1)S(1)}, bf16[1536,384]{1,0:T(8,128)(2,1)}, u32[]{:S(2)}) copy-start(bf16[1536,384]{1,0:T(8,128)(2,1)} %w2.1) | copy-start | bytes 3538948
  265.6 125.2 %copy-start.6 = (f32[3,3,384]{2,1,0:T(4,128)}, f32[3,3,384]{2,1,0:T(4,128)S(1)}, u32[]{:S(2)}) copy-start(f32[3,3,384]{2,1,0:T(4,128)S(1)} %reshape.131) | copy-start | bytes 41476
  267.5 123.3 %copy-start.18 = (f32[384]{0:T(512)}, f32[384]{0:T(512)S(1)}, u32[]{:S(2)}) copy-start(f32[384]{0:T(512)S(1)} %get-tuple-element.132) | copy-start | bytes 4612
  267.5 123.4 %copy-start.17 = (f32[384]{0:T(512)}, f32[384]{0:T(512)S(1)}, u32[]{:S(2)}) copy-start(f32[384]{0:T(512)S(1)} %get-tuple-element.139) | copy-start | bytes 4612
  267.5 124.0 %copy-start.19 = (f32[384]{0:T(512)}, f32[384]{0:T(512)S(1)}, u32[]{:S(2)}) copy-start(f32[384]{0:T(512)S(1)} %get-tuple-element.123) | copy-start | bytes 4612
  388.6 2.2 copy-start.2
  388.6 2.2 copy-start.4
  388.6 2.9 copy-start.14
  388.6 2.9 copy-start.15
  388.6 3.5 copy-start.5
  392.1 2.5 copy-start.3
  394.6 2.5 copy-start
Sparse Core Ops, SparseCore 0:
  221.1 167.5 all-reduce.3

commit v2 on v1

v2 whole, which is shorter than its diff:
```python
import math

import jax
import jax.numpy as jnp
from jax import lax
from jax.experimental import pallas as pl
from jax.experimental.pallas import tpu as pltpu
from jax.sharding import PartitionSpec as P

EPS_NORM = 1e-06
EPS_BATCH = 1e-05
EPS_UNIT = 1e-06
F32 = jnp.float32
BF16 = jnp.bfloat16
MESH = pl.DeviceIdType.MESH
G = 24
T = G * G
D = 384
FF = 1536
HEADS = 8
HD = 48
L = 128
PITCH = 32
PLANE = (G + 4) * PITCH
RC = T
RM = T
RF = T // 2
ROOT_HALF = 0.7071067811865476
ROOT_TWO_PI = 0.3989422804014327
NT = (((1,), (1,)), ((), ()))
TN = (((0,), (0,)), ((), ()))


def dot(a, b, dims=(((1,), (0,)), ((), ()))):
    return lax.dot_general(a, b, dims, preferred_element_type=F32)


def rows(start, size):
    return pl.ds(pl.multiple_of(start, 8), size)


def wide(v, times=3):
    return jnp.concatenate([v] * times, axis=1)


def fold8(v):
    return jnp.sum(v.reshape(v.shape[0] // 8, 8, v.shape[1]), axis=0)


def total(v):
    return jnp.sum(v, axis=0, keepdims=True)


def zeros(*shape):
    return jnp.zeros(shape, F32)


def lane_mean(v):
    return jnp.mean(v, axis=1, keepdims=True)


def gelu_pair(u):
    phi = 0.5 + 0.5 * lax.erf(u * ROOT_HALF)
    bell = jnp.exp((u * u) * -0.5)
    return u * phi, phi + u * (bell * ROOT_TWO_PI)


def column_of(row):
    return jnp.broadcast_to(row, (L, D)).T


def write_mask(edge, mask):
    row_index = lax.broadcasted_iota(jnp.int32, (G, G, L), 0)
    col_index = lax.broadcasted_iota(jnp.int32, (G, G, L), 1)
    keep = (row_index < edge) & (col_index < edge)
    mask[...] = keep.astype(F32).reshape(T, L)


def write_sharp(sharp_mask, sharp):
    lane = lax.broadcasted_iota(jnp.int32, (HD, D), 1)
    for h in range(HEADS):
        own = (lane >= h * HD) & (lane < (h + 1) * HD)
        sharp_mask[h * HD : (h + 1) * HD, :] = jnp.where(own, sharp[h], 0.0)


def to_plane(plane, r, value):
    count = value.shape[0] // G
    for g in range(count):
        for c in range(3):
            plane[c, rows((r * count + g + 2) * PITCH, G), :] = value[g * G : (g + 1) * G, c * L : (c + 1) * L]


def taps_of(st, cs):
    return [jnp.broadcast_to(st[a, b : b + 1, cs], (G, L)) for a in range(3) for b in range(3)]


def stencil(plane, c, r, taps, count):
    base = r * (count * PITCH)
    outs = [None] * count
    for a in range(count + 2):
        for b in range(3):
            v = plane[c, pl.ds(base + (a + 1) * PITCH - 1 + b, G), :]
            for o in range(count):
                if 0 <= a - o < 3:
                    t = v * taps[(a - o) * 3 + b]
                    outs[o] = t if outs[o] is None else outs[o] + t
    return outs


def stencil_back(plane, c, r, taps, vs, kernel):
    count = len(vs)
    base = r * (count * PITCH)
    outs = [None] * count
    for a in range(count + 2):
        for b in range(3):
            v = plane[c, pl.ds(base + (a + 1) * PITCH - 1 + b, G), :]
            for o in range(count):
                if 0 <= a - o < 3:
                    k = (2 - (a - o)) * 3 + (2 - b)
                    t = v * taps[k]
                    outs[o] = t if outs[o] is None else outs[o] + t
                    kernel[k] = kernel[k] + fold8(v * vs[o])
    return outs


def chunks(body, init, size):
    if size == T:
        return body(0, pl.ds(0, T), init)
    return lax.fori_loop(0, T // size, lambda r, c: body(r, rows(r * size, size), c), init)


def stage_a1(i, x, g1, b1, n1, mask):
    def body(r, sl, carry):
        xs = x[i, sl, :].astype(F32)
        mean = lane_mean(xs)
        centre = xs - mean
        spread = lax.rsqrt(lane_mean(centre * centre) + EPS_NORM)
        n1[i, sl, :] = ((centre * spread * g1[...] + b1[...]) * wide(mask[sl, :])).astype(BF16)
        return carry

    chunks(body, 0, RC)


def stage_a2(i, wqkv, bqkv, n1, qkv, sqk, mask):
    def body(r, sl, carry):
        sums = list(carry)
        mk = wide(mask[sl, :])
        normed = n1[i, sl, :]
        for p in range(3):
            cols = slice(p * D, (p + 1) * D)
            part = (dot(normed, wqkv[:, cols]) + bqkv[:, cols]) * mk
            if p < 2:
                sums[p] = sums[p] + fold8(part * part)
            qkv[i, sl, cols] = part.astype(BF16)
        return tuple(sums)

    sums = chunks(body, (zeros(8, D), zeros(8, D)), RM)
    for p in range(2):
        sqk[i, p] = jnp.broadcast_to(lax.rsqrt(total(sums[p]) + EPS_UNIT), (8, D))


def softmax_band(sc, sh):
    ex = jnp.where(sh > 0.0, jnp.exp(sc * sh), 0.0)
    return ex / jnp.sum(ex, axis=1, keepdims=True)


def stage_a3(i, qkv, sqk, score, sharp_mask, pmat):
    sq, sk = sqk[i, 0, 0:1, :], sqk[i, 1, 0:1, :]
    sqcol = column_of(sq)
    raw = dot(qkv[i, :, :D], qkv[i, :, D : 2 * D], TN)
    for h in range(HEADS):
        band = slice(h * HD, (h + 1) * HD)
        sc = raw[band] * wide(sqcol[band]) * sk
        score[i, band, :] = sc
        pmat[band, :] = softmax_band(sc, sharp_mask[band, :]).astype(BF16)


def stage_a4(i, x, wm, bm, fm, g2, b2, qkv, mixed, resid, vh2, r2, mask, plane, pmat):
    def body(r, sl, carry):
        mk = wide(mask[sl, :])
        mx = dot(qkv[i, sl, 2 * D :], pmat[...], NT).astype(BF16)
        mixed[i, sl, :] = mx
        branch = (dot(mx, wm[...]) + bm[...]) * mk
        res = x[i, sl, :].astype(F32) + fm[...] * branch
        resid[i, sl, :] = res
        mean = lane_mean(res)
        centre = res - mean
        spread = lax.rsqrt(lane_mean(centre * centre) + EPS_NORM)
        vhat = centre * spread
        vh2[i, sl, :] = vhat
        r2[i, sl, :] = jnp.broadcast_to(spread, (RM, L))
        to_plane(plane, r, (vhat * g2[...] + b2[...]) * mk)
        return carry

    chunks(body, 0, RM)


def stage_a5(i, st1, cb1, act, slope, stat, mask, plane):
    for c in range(3):
        cs = slice(c * L, (c + 1) * L)
        taps = taps_of(st1, cs)

        def conv_body(r, carry):
            outs = stencil(plane, c, r, taps, 4)
            diffs = []
            for o in range(4):
                sl = rows((r * 4 + o) * G, G)
                value, diff = gelu_pair(outs[o] + cb1[:, cs])
                value = value * mask[sl, :]
                act[i, sl, cs] = value
                diffs.append(diff)
                carry = carry + fold8(value)
            slope[i, pl.ds(pl.multiple_of(r * (4 * G), 32), 4 * G), cs] = jnp.concatenate(diffs, axis=0).astype(BF16)
            return carry

        stat[i, 0:1, cs] = total(lax.fori_loop(0, G // 4, conv_body, zeros(8, L)))


def stage_a6(i, edge, act, stat, mask):
    count = (edge * edge).astype(F32)
    mean = stat[i, 0:1, :] / count

    def body(r, sl, carry):
        dev = (act[i, sl, :] - mean) * wide(mask[sl, :])
        return carry + fold8(dev * dev)

    stat[i, 1:2, :] = total(chunks(body, zeros(8, D), RC))
    stat[i, 2:3, :] = jnp.full((1, D), count, F32)


def merge_stats(parts):
    summed = sum(p[0] for p in parts)
    count = sum(p[2] for p in parts)
    mean = summed / count
    square = sum(p[1] + p[2] * (p[0] / p[2] - mean) * (p[0] / p[2] - mean) for p in parts)
    return summed, square, count


def stage_b1(i, act, stats, bg, bo, mask, plane):
    mean, inv = stats[0:1, :], stats[1:2, :]
    scale = inv * bg[...]
    shift = bo[...] - mean * scale

    def body(r, sl, carry):
        to_plane(plane, r, (act[i, sl, :] * scale + shift) * wide(mask[sl, :]))
        return carry

    chunks(body, 0, RC)


def stage_b2(i, st2, cb2, fl, resid, mask, plane):
    for c in range(3):
        cs = slice(c * L, (c + 1) * L)
        taps = taps_of(st2, cs)

        def conv_body(r, carry):
            outs = stencil(plane, c, r, taps, 4)
            for o in range(4):
                sl = rows((r * 4 + o) * G, G)
                resid[i, sl, cs] = resid[i, sl, cs] + fl[:, cs] * ((outs[o] + cb2[:, cs]) * mask[sl, :])
            return carry

        lax.fori_loop(0, G // 4, conv_body, 0)


def stage_b3(i, sens, g3, b3, fp, sm_b, mask, resid, vh3, r3, n3, f2):
    def body(r, sl, carry):
        mk = wide(mask[sl, :])
        res = resid[i, sl, :]
        centre = res - lane_mean(res)
        spread = lax.rsqrt(lane_mean(centre * centre) + EPS_NORM)
        vhat = centre * spread
        vh3[i, sl, :] = vhat
        r3[sl, :] = jnp.broadcast_to(spread, (RC, L))
        n3[sl, :] = ((vhat * g3[...] + b3[...]) * mk).astype(BF16)
        err = sens[i, sl, :].astype(F32) * mk * fp[...]
        f2[sl, :] = err.astype(BF16)
        return carry + fold8(err)

    sm_b[2] += chunks(body, zeros(8, D), RC)


def stage_b4(w1, bb1, w2, smf, n3, f2, hl, e1, branch, back):
    def body(r, sl, hidden_sum):
        normed = n3[sl, :]
        low = f2[sl, :]
        parts = []
        for j in range(FF // 256):
            cols = slice(j * 256, (j + 1) * 256)
            value, diff = gelu_pair(dot(normed, w1[:, cols]) + bb1[:, cols])
            hl[sl, cols] = value.astype(BF16)
            err = dot(low, w2[cols, :], NT) * diff
            parts.append(fold8(err))
            e1[sl, cols] = err.astype(BF16)
        branch[sl, :] = dot(hl[sl, :], w2[...])
        back[sl, :] = dot(e1[sl, :], w1[...], NT)
        return hidden_sum + jnp.concatenate(parts, axis=1)

    smf[...] += chunks(body, zeros(8, FF), RF)


def stage_b5(i, sens, bb2, fp, g3, fl, resid, sm_b, mask, vh3, r3, branch, back):
    def body(r, sl, carry):
        gain_sum, shift_sum, local_sum = carry
        mk = wide(mask[sl, :])
        upstream = sens[i, sl, :].astype(F32) * mk
        sens[i, sl, :] = ((resid[i, sl, :] + fp[...] * (branch[sl, :] + bb2[...])) * mk).astype(BF16)
        err = back[sl, :] * mk
        vhat = vh3[i, sl, :]
        shift_sum = shift_sum + fold8(err)
        gain_sum = gain_sum + fold8(err * vhat)
        eg = err * g3[...]
        mean1 = lane_mean(eg)
        mean2 = lane_mean(eg * vhat)
        grad = upstream + wide(r3[sl, :]) * (eg - mean1 - vhat * mean2)
        resid[i, sl, :] = grad
        local_sum = local_sum + fold8(grad * mk)
        return gain_sum, shift_sum, local_sum

    sums = chunks(body, (zeros(8, D),) * 3, RC)
    sm_b[0] += sums[0]
    sm_b[1] += sums[1]
    sm_b[3] += sums[2] * fl[...]


def stage_b6(dw1, n3, e1):
    left = n3[...].T
    for j in range(FF // 512):
        part = dot(left, e1[:, j * 512 : (j + 1) * 512])
        for k in range(4):
            block, col = divmod(j * 512 + k * L, D)
            dw1[block * D : (block + 1) * D, col : col + L] += part[:, k * L : (k + 1) * L]


def stage_b7(dw2, hl, f2):
    dw2[...] += dot(hl[...], f2[...], TN)


def stage_b8(i, act, stats, bg, bo, fl, st2, resid, bng, sm_b, mask, plane, plane2):
    stage_b1(i, act, stats, bg, bo, mask, plane)

    def local_body(r, sl, carry):
        to_plane(plane2, r, resid[i, sl, :] * wide(mask[sl, :]) * fl[...])
        return carry

    chunks(local_body, 0, RC)
    mean, inv = stats[0:1, :], stats[1:2, :]
    for c in range(3):
        cs = slice(c * L, (c + 1) * L)
        taps = taps_of(st2, cs)

        def back_body(r, carry):
            kernel = list(carry)
            vs = [plane[c, rows((r * 4 + o + 2) * PITCH, G), :] for o in range(4)]
            outs = stencil_back(plane2, c, r, taps, vs, kernel)
            for o in range(4):
                sl = rows((r * 4 + o) * G, G)
                bng[i, sl, cs] = outs[o] * mask[sl, :]
            return tuple(kernel)

        found = lax.fori_loop(0, G // 4, back_body, (zeros(8, L),) * 9)
        for k in range(9):
            sm_b[4 + k, :, cs] += found[k]

    def sum_body(r, sl, carry):
        grad = bng[i, sl, :]
        centred = (act[i, sl, :] - mean) * inv
        return carry[0] + fold8(grad * centred), carry[1] + fold8(grad)

    sums = chunks(sum_body, (zeros(8, D),) * 2, RC)
    sm_b[13] += sums[0]
    sm_b[14] += sums[1]


def stage_c1(i, act, slope, bng, stats, bsums, bg, sm_c, mask, plane2):
    mean, inv, count = (stats[k : k + 1, :] for k in range(3))
    coef = inv * bg[...]
    by_centred = bsums[0:1, :] / count * inv
    const = bsums[1:2, :] / count - mean * by_centred

    def body(r, sl, carry):
        grad = (bng[i, sl, :] - const - act[i, sl, :] * by_centred) * coef
        err = grad * wide(mask[sl, :]) * slope[i, sl, :].astype(F32)
        to_plane(plane2, r, err)
        return carry + fold8(err)

    sm_c[14] += chunks(body, zeros(8, D), RC)


def stage_c2(i, vh2, g2, b2, st1, sm_c, mask, plane2, back):
    for c in range(3):
        cs = slice(c * L, (c + 1) * L)
        taps = taps_of(st1, cs)

        def back_body(r, carry):
            kernel = list(carry)
            sls = [rows((r * 4 + o) * G, G) for o in range(4)]
            vs = [(vh2[i, sl, cs] * g2[:, cs] + b2[:, cs]) * mask[sl, :] for sl in sls]
            outs = stencil_back(plane2, c, r, taps, vs, kernel)
            for o in range(4):
                back[sls[o], cs] = outs[o] * mask[sls[o], :]
            return tuple(kernel)

        found = lax.fori_loop(0, G // 4, back_body, (zeros(8, L),) * 9)
        for k in range(9):
            sm_c[5 + k, :, cs] += found[k]


def stage_c3(i, resid, vh2, r2, fm, g2, sm_c, mask, back, plow):
    def body(r, sl, carry):
        gain_sum, shift_sum, bias_sum = carry
        mk = wide(mask[sl, :])
        err = back[sl, :]
        vhat = vh2[i, sl, :]
        shift_sum = shift_sum + fold8(err)
        gain_sum = gain_sum + fold8(err * vhat)
        eg = err * g2[...]
        mean1 = lane_mean(eg)
        mean2 = lane_mean(eg * vhat)
        grad = resid[i, sl, :] + wide(r2[i, sl, :]) * (eg - mean1 - vhat * mean2)
        resid[i, sl, :] = grad
        err = grad * mk * fm[...]
        bias_sum = bias_sum + fold8(err)
        plow[i, sl, :] = err.astype(BF16)
        return gain_sum, shift_sum, bias_sum

    sums = chunks(body, (zeros(8, D),) * 3, RC)
    for k in range(3):
        sm_c[2 + k] += sums[k]


def stage_c4(mixed, dwm, plow):
    images = mixed.shape[0]
    dwm[...] = dot(mixed[...].reshape(images * T, D), plow[...].reshape(images * T, D), TN)


def stage_c4b(i, wm, plow):
    plow[i] = dot(plow[i], wm[...], NT).astype(BF16)


def stage_c5(i, qkv, score, sqk, srow, sharp_mask, plow, pmat, alow, cqk):
    raw = dot(plow[i], qkv[i, :, 2 * D :], TN)
    sq, sk = sqk[i, 0, 0:1, :], sqk[i, 1, 0:1, :]
    sqcol = column_of(sq)
    colsum = zeros(8, D)
    rowsums = []
    for h in range(HEADS):
        band = slice(h * HD, (h + 1) * HD)
        sc = score[i, band, :]
        sh = sharp_mask[band, :]
        pr = softmax_band(sc, sh)
        pmat[band, :] = pr.astype(BF16)
        weighted = raw[band] * pr
        logit = weighted - pr * jnp.sum(weighted, axis=1, keepdims=True)
        lg = logit * sh
        cross = lg * sc
        rowsums.append(jnp.sum(cross, axis=1, keepdims=True))
        colsum = colsum + fold8(cross)
        alow[band, :] = (lg * wide(sqcol[band]) * sk).astype(BF16)
    rowcol = jnp.concatenate(rowsums, axis=0)
    rowrow = jnp.broadcast_to(rowcol, (D, L)).T[0:1, :]
    srow[...] += rowrow
    cqk[0:1, :] = sq * sq * rowrow
    cqk[1:2, :] = sk * sk * total(colsum)


def stage_c6(i, qkv, smq, plow, pmat, alow, cqk):
    cq, ck = cqk[0:1, :], cqk[1:2, :]
    qv, kv = qkv[i, :, :D], qkv[i, :, D : 2 * D]
    grads = (
        dot(kv, alow[...], NT) - qv.astype(F32) * cq,
        dot(qv, alow[...]) - kv.astype(F32) * ck,
        dot(plow[i], pmat[...]),
    )
    for p in range(3):
        cols = slice(p * D, (p + 1) * D)
        smq[:, cols] += fold8(grads[p])
        qkv[i, :, cols] = grads[p].astype(BF16)


def stage_c7(n1, qkv, dwq, dwk, dwv):
    images = n1.shape[0]
    left = n1[...].reshape(images * T, D).T
    for p, out in enumerate((dwq, dwk, dwv)):
        out[...] = dot(left, qkv[:, :, p * D : (p + 1) * D].reshape(images * T, D))


def stage_c8(i, x, g1, wqkv, resid, sm_c, mask, qkv):
    err = dot(qkv[i], wqkv[...], NT) * wide(mask[...])
    xs = x[i].astype(F32)
    centre = xs - lane_mean(xs)
    spread = lax.rsqrt(lane_mean(centre * centre) + EPS_NORM)
    vhat = centre * spread
    sm_c[1] += fold8(err)
    sm_c[0] += fold8(err * vhat)
    eg = err * g1[...]
    mean1 = lane_mean(eg)
    mean2 = lane_mean(eg * vhat)
    x[i] = (resid[i] + spread * (eg - mean1 - vhat * mean2)).astype(BF16)


def geometry(n):
    chips = n // 2
    side = 2 if chips < 64 else 4
    return side, side, chips // (side * side)


class Place:
    def __init__(self, n):
        self.n = n
        self.me = lax.axis_index("img")
        x, y, z = geometry(n)
        self.axes = {}
        stride = 1
        for name, size in (("core", 2), ("x", x), ("y", y), ("z", z)):
            self.axes[name] = (size, stride, lax.rem(self.me // stride, size))
            stride *= size

    def other(self, k):
        return lax.rem(self.me + k, self.n)


def stream_steps(n, first):
    if n == 32:
        order = ("x", "y") if first else ("y", "x")
        return [("core", True), (order[0], True), (order[1], True), ("z", True)]
    order = ("x", "z") if first else ("z", "x")
    return [("core", True), (order[0], True), (order[1], True), ("y", False)]


STREAMS = (FF // 2,) * 6


def stream_shape(n, steps, size):
    axes = dict(zip(("core", "x", "y", "z"), (2,) + geometry(n)))
    received, copies, length = 0, 0, size
    for axis, split in steps:
        s = axes[axis]
        piece = length // s if split else length
        received += (s - 1) * piece
        copies += s - 1
        length = piece
    return received, copies


class Stream:
    def __init__(self, place, steps, buf, start, size, recv, sems, credits):
        self.place, self.buf, self.recv, self.sems, self.credits = place, buf, recv, sems, credits
        off, length, slot, sem = start, size, 0, 0
        self.down = []
        for axis, split in steps:
            s, stride, k = place.axes[axis]
            piece = length // s if split else length
            self.down.append((axis, split, off, piece, slot, sem))
            slot += (s - 1) * piece
            sem += s - 1
            if split:
                off = off + k * piece
            length = piece
        self.flying = []
        self.done = 0
        self.last = 2 * len(steps)

    def peers(self, axis):
        s, stride, k = self.place.axes[axis]
        for j in range(1, s):
            p = lax.rem(k + j, s)
            yield j, p, self.place.me + (p - k) * stride

    def send(self, src, dst, side, sem, device):
        copy = pltpu.make_async_remote_copy(
            src_ref=src,
            dst_ref=dst,
            send_sem=self.sems.at[side, sem],
            recv_sem=self.sems.at[side + 1, sem],
            device_id=(device,),
            device_id_type=MESH,
        )
        copy.start()
        self.flying.append(copy)

    def land(self):
        for copy in self.flying:
            copy.wait()
        self.flying = []

    def start_sum(self, step):
        axis, split, off, piece, slot, sem = self.down[step]
        for j, p, device in self.peers(axis):
            src = self.buf.at[rows(off + p * piece if split else off, piece), :]
            dst = self.recv.at[pl.ds(slot + (j - 1) * piece, piece), :]
            self.send(src, dst, 0, sem + j - 1, device)

    def finish_sum(self, step):
        axis, split, off, piece, slot, sem = self.down[step]
        s, stride, k = self.place.axes[axis]
        self.land()
        if split:
            for j, p, device in self.peers(axis):
                pl.semaphore_signal(self.credits.at[step], inc=1, device_id=(device,), device_id_type=MESH)
            own = off + k * piece
            size = math.gcd(piece, 96)

            def add(r, _):
                sl = rows(own + r * size, size)
                summed = self.buf[sl, :]
                for j in range(1, s):
                    summed = summed + self.recv[rows(slot + (j - 1) * piece + r * size, size), :]
                self.buf[sl, :] = summed
                return 0

            lax.fori_loop(0, piece // size, add, 0)
        else:
            sl = rows(off, piece)
            own = self.buf[sl, :]
            summed = None
            for q in range(s):
                j = lax.rem(k - q + s, s)
                at = slot + jnp.maximum(j - 1, 0) * piece
                term = jnp.where(k == q, own, self.recv[rows(at, piece), :])
                summed = term if summed is None else summed + term
            self.buf[sl, :] = summed

    def start_gather(self, step):
        axis, split, off, piece, slot, sem = self.down[step]
        if split:
            s, stride, k = self.place.axes[axis]
            pl.semaphore_wait(self.credits.at[step], s - 1)
            part = self.buf.at[rows(off + k * piece, piece), :]
            for j, p, device in self.peers(axis):
                self.send(part, part, 2, sem + j - 1, device)

    def advance(self):
        count, k = self.last // 2, self.done
        if 0 < k <= self.last:
            if k <= count:
                self.finish_sum(k - 1)
            else:
                self.land()
        if k < self.last:
            if k < count:
                self.start_sum(k)
            else:
                self.start_gather(self.last - 1 - k)
        self.done += 1


def stream_rows(n, sizes):
    return [stream_shape(n, stream_steps(n, k % 2 == 0), size)[0] for k, size in enumerate(sizes)]


def push_all(place, source, target, sems):
    def start(k, _):
        device = place.other(k)
        pltpu.make_async_remote_copy(
            src_ref=source(device),
            dst_ref=target,
            send_sem=sems.at[0],
            recv_sem=sems.at[1],
            device_id=(device,),
            device_id_type=MESH,
        ).start()
        return 0

    lax.fori_loop(1, place.n, start, 0)


def land_all(most, sems):
    for k in range(2):
        pltpu.make_async_copy(most, most, sems.at[k]).wait()


def put_small(small, k, row):
    for c in range(3):
        small[3 * k + c : 3 * k + c + 1, :] = row[:, c * L : (c + 1) * L]


def get_small(small, k):
    return jnp.concatenate([small[3 * k + c : 3 * k + c + 1, :] for c in range(3)], axis=1)


def mega_kernel(n, images, refs):
    (edges, sharp, x_in, sens_in, wqkv, wm, w1_in, w2_in, st1, st2,
     g1_in, b1_in, bqkv_in, bm_in, fm_in, g2_in, b2_in, cb1_in, bg_in, bo_in, cb2_in, fl_in, g3_in, b3_in, bb1_in, bb2_in, fp_in,
     lout, gin, dwqkv_out, dwm_out, dw1_out, dw2_out, small_out,
     vecs, x, sens, w1, w2, n1, qkv, mixed, score, sqk, r2, resid, vh2, act, vh3, slope, stat, stats, bsums, cqk,
     mask, sharp_mask, pmat, alow, plane, plane2, r3, n3, f2, hl, e1,
     sm_b, smf, sm_c, smq, srow, grads, recv, small, payload, gathered,
     in_sems, out_sems, group_sems, credits, push_sems) = refs
    place = Place(n)
    me = place.me
    barrier = pltpu.get_barrier_semaphore()

    def greet(k, _):
        pl.semaphore_signal(barrier, inc=1, device_id=(place.other(k),), device_id_type=MESH)
        return 0

    lax.fori_loop(1, n, greet, 0)

    x_copies = [pltpu.make_async_copy(x_in.at[k], x.at[k], in_sems.at[k]) for k in range(images)]
    later = [(w1_in, w1), (w2_in, w2), (sens_in, sens)]
    later_copies = [pltpu.make_async_copy(a, b, in_sems.at[images + k]) for k, (a, b) in enumerate(later)]
    for copy in x_copies + later_copies:
        copy.start()

    names = {}
    at = 0
    vectors = (("g1", g1_in), ("b1", b1_in), ("bm", bm_in), ("fm", fm_in), ("g2", g2_in), ("b2", b2_in), ("cb1", cb1_in),
               ("bg", bg_in), ("bo", bo_in), ("cb2", cb2_in), ("fl", fl_in), ("g3", g3_in), ("b3", b3_in), ("bb2", bb2_in),
               ("fp", fp_in))
    for name, ref in vectors:
        vecs[at : at + 1, 0:D] = ref[...].reshape(1, D)
        names[name] = vecs.at[at : at + 1, 0:D]
        at += 1
    vecs[at : at + 1, 0 : 3 * D] = bqkv_in[...].reshape(1, 3 * D)
    bqkv = vecs.at[at : at + 1, 0 : 3 * D]
    vecs[at + 1 : at + 2, :] = bb1_in[...].reshape(1, FF)
    bb1 = vecs.at[at + 1 : at + 2, :]
    g1, b1, bm, fm, g2, b2, cb1, bg, bo, cb2, fl, g3, b3, bb2, fp = (names[name] for name, ref in vectors)

    write_sharp(sharp_mask, sharp)
    for ref in (plane, plane2, sm_b, smf, sm_c, smq, srow, small):
        ref[...] = jnp.zeros_like(ref)
    dwq, dwk, dwv, dwm = (grads.at[k * D : (k + 1) * D, :] for k in range(4))
    branch, back = grads.at[0:T, :], grads.at[T : 2 * T, :]
    dw2 = grads.at[4 * D + FF : 4 * D + 2 * FF, :]
    dw1 = grads.at[4 * D : 4 * D + FF, :]
    grads[4 * D :, :] = zeros(2 * FF, D)

    for copy in x_copies:
        copy.wait()

    def front(i, _):
        edge = edges[i]
        write_mask(edge, mask)
        stage_a1(i, x, g1, b1, n1, mask)
        stage_a2(i, wqkv, bqkv, n1, qkv, sqk, mask)
        stage_a3(i, qkv, sqk, score, sharp_mask, pmat)
        stage_a4(i, x, wm, bm, fm, g2, b2, qkv, mixed, resid, vh2, r2, mask, plane, pmat)
        stage_a5(i, st1, cb1, act, slope, stat, mask, plane)
        stage_a6(i, edge, act, stat, mask)
        return 0

    lax.fori_loop(0, images, front, 0)

    merged = merge_stats([tuple(stat[i, k : k + 1, :] for k in range(3)) for i in range(images)])
    for k in range(2):
        put_small(payload.at[0], k, merged[k])
    payload[0, 6:7, :] = merged[2][:, 0:L]
    pl.semaphore_wait(barrier, n - 1)
    push_all(place, lambda device: payload.at[0], gathered.at[0, me], push_sems.at[0])
    gathered[0, me] = payload[0]
    for copy in later_copies:
        copy.wait()
    land_all(gathered.at[0, pl.ds(0, n - 1)], push_sems.at[0])

    def sum_both(k, carry):
        return carry + gathered[0, k]

    summed = lax.fori_loop(0, n, sum_both, zeros(8, L))
    count = summed[6:7, :]
    mean = summed[0:3, :] / count

    def sum_squares(k, carry):
        part = gathered[0, k]
        own = part[6:7, :]
        gap = part[0:3, :] / own - mean
        return carry + part[3:6, :] + own * gap * gap

    square = lax.fori_loop(0, n, sum_squares, zeros(3, L))
    inv = lax.rsqrt(square / count + EPS_BATCH)
    for c in range(3):
        stats[0:1, c * L : (c + 1) * L] = mean[c : c + 1, :]
        stats[1:2, c * L : (c + 1) * L] = inv[c : c + 1, :]
        stats[2:3, c * L : (c + 1) * L] = count

    def middle(i, _):
        write_mask(edges[i], mask)
        stage_b1(i, act, stats, bg, bo, mask, plane)
        stage_b2(i, st2, cb2, fl, resid, mask, plane)
        stage_b3(i, sens, g3, b3, fp, sm_b, mask, resid, vh3, r3, n3, f2)
        stage_b4(w1, bb1, w2, smf, n3, f2, hl, e1, branch, back)
        stage_b5(i, sens, bb2, fp, g3, fl, resid, sm_b, mask, vh3, r3, branch, back)
        stage_b6(dw1, n3, e1)
        stage_b7(dw2, hl, f2)
        return 0

    lax.fori_loop(0, images, middle, 0)
    out_copies = [pltpu.make_async_copy(sens, lout, out_sems.at[0])]
    out_copies[0].start()

    def conv_back(i, _):
        write_mask(edges[i], mask)
        stage_b8(i, act, stats, bg, bo, fl, st2, resid, vh3, sm_b, mask, plane, plane2)
        return 0

    lax.fori_loop(0, images, conv_back, 0)
    for k in range(15):
        put_small(small, k, total(sm_b[k]))
    for j in range(4):
        put_small(small, 15 + j, total(smf[:, j * D : (j + 1) * D]))
    for k in range(2):
        put_small(payload.at[1], k, total(sm_b[13 + k]))
    payload[1, 6:8, :] = zeros(2, L)
    push_all(place, lambda device: payload.at[1], gathered.at[1, me], push_sems.at[1])
    gathered[1, me] = payload[1]
    land_all(gathered.at[1, pl.ds(0, n - 1)], push_sems.at[1])
    summed = lax.fori_loop(0, n, lambda k, carry: carry + gathered[1, k], zeros(8, L))
    for k in range(2):
        bsums[k : k + 1, :] = jnp.concatenate([summed[3 * k + c : 3 * k + c + 1] for c in range(3)], axis=1)

    def rear1(i, _):
        write_mask(edges[i], mask)
        stage_c1(i, act, slope, vh3, stats, bsums, bg, sm_c, mask, plane2)
        stage_c2(i, vh2, g2, b2, st1, sm_c, mask, plane2, back)
        stage_c3(i, resid, vh2, r2, fm, g2, sm_c, mask, back, slope)
        return 0

    lax.fori_loop(0, images, rear1, 0)
    stage_c4(mixed, dwm, slope)

    def rear2(i, _):
        stage_c4b(i, wm, slope)
        stage_c5(i, qkv, score, sqk, srow, sharp_mask, slope, pmat, alow, cqk)
        stage_c6(i, qkv, smq, slope, pmat, alow, cqk)
        return 0

    lax.fori_loop(0, images, rear2, 0)
    stage_c7(n1, qkv, dwq, dwk, dwv)

    def rear3(i, _):
        write_mask(edges[i], mask)
        stage_c8(i, x, g1, wqkv, resid, sm_c, mask, qkv)
        return 0

    lax.fori_loop(0, images, rear3, 0)
    out_copies.append(pltpu.make_async_copy(x, gin, out_sems.at[1]))
    out_copies[1].start()
    for k in range(15):
        put_small(small, 19 + k, total(sm_c[k]))
    for p in range(3):
        put_small(small, 34 + p, total(smq[:, p * D : (p + 1) * D]))
    put_small(small, 37, srow[...])

    push_all(place, lambda device: small.at[rows(device * 8, 8), :], gathered.at[0, me], push_sems.at[2])
    gathered[0, me] = small[rows(me * 8, 8), :]
    streams = []
    at, start = 0, 0
    for k, (size, received) in enumerate(zip(STREAMS, stream_rows(n, STREAMS))):
        piece = recv.at[pl.ds(at, received), :]
        steps = stream_steps(n, k % 2 == 0)
        streams.append(Stream(place, steps, grads, start, size, piece, group_sems.at[k], credits.at[k]))
        at, start = at + received, start + size
    for stream in streams:
        stream.advance()
    land_all(gathered.at[0, pl.ds(0, n - 1)], push_sems.at[2])
    gathered[1, me] = lax.fori_loop(0, n, lambda k, carry: carry + gathered[0, k], zeros(8, L))
    push_all(place, lambda device: gathered.at[1, me], gathered.at[1, me], push_sems.at[3])
    for k in range(streams[0].last):
        for stream in streams:
            stream.advance()
    land_all(gathered.at[1, pl.ds(0, n - 1)], push_sems.at[3])
    for k in range(16):
        small[8 * k : 8 * k + 8, :] = gathered[1, k]

    weights = [(grads.at[p * D : (p + 1) * D, :], dwqkv_out.at[:, p * D : (p + 1) * D]) for p in range(3)]
    weights.append((dwm, dwm_out))
    weights += [(grads.at[(4 + j) * D : (5 + j) * D, :], dw1_out.at[:, j * D : (j + 1) * D]) for j in range(4)]
    weights.append((dw2, dw2_out))
    for k, (a, b) in enumerate(weights):
        out_copies.append(pltpu.make_async_copy(a, b, out_sems.at[2 + k]))
        out_copies[-1].start()

    def branch_factor(weight, grad, bias, bias_grad, factor):
        return (total(weight.astype(F32) * grad) + bias * bias_grad) / factor

    picked = [get_small(small, k) for k in range(38)]
    picked.append(branch_factor(wm[...], dwm[...], bm[...], picked[19 + 4], fm[...]))
    local = sum(st2[a, b : b + 1, :] * picked[4 + 3 * a + b] for a in range(3) for b in range(3))
    picked.append((local + cb2[...] * picked[3]) / fl[...])
    picked.append(branch_factor(w2[...], dw2[...], bb2[...], picked[2], fp[...]))
    for k, row in enumerate(picked):
        small_out[k : k + 1, :] = row
    for copy in out_copies:
        copy.wait()


def on_device(n, x, sens, edges, g1, b1, wqkv, bqkv, sharp, wm, bm, fm, g2, b2, st1, cb1, bg, bo, st2, cb2, fl, g3, b3,
              w1, bb1, w2, bb2, fp):
    images = x.shape[0]
    S = jax.ShapeDtypeStruct
    V = pltpu.VMEM
    vm = pl.BlockSpec(memory_space=pltpu.VMEM)
    sm = pl.BlockSpec(memory_space=pltpu.SMEM)
    hbm = pl.BlockSpec(memory_space=pl.ANY)
    full = (images, T, D)
    small_rows = max(16 * 8, 8 * n)
    dma = pltpu.SemaphoreType.DMA
    copies = stream_shape(n, stream_steps(n, True), FF)[1]
    lout, gin, dwqkv, dwm, dw1, dw2, small = pl.pallas_call(
        lambda *refs: mega_kernel(n, images, refs),
        in_specs=[sm, sm, hbm, hbm, vm, vm, hbm, hbm, vm, vm] + [vm] * 17,
        out_specs=[hbm] * 6 + [vm],
        out_shape=[S(full, BF16), S(full, BF16), S((D, 3 * D), F32), S((D, D), F32), S((D, FF), F32), S((FF, D), F32),
                   S((48, D), F32)],
        scratch_shapes=[
            V((24, FF), F32), V(full, BF16), V(full, BF16), V((D, FF), BF16), V((FF, D), BF16),
            V(full, BF16), V((images, T, 3 * D), BF16), V(full, BF16),
            V((images, D, D), F32), V((images, 2, 8, D), F32),
            V((images, T, L), F32), V(full, F32), V(full, F32), V(full, F32), V(full, F32),
            V(full, BF16), V((images, 8, D), F32), V((8, D), F32), V((8, D), F32), V((8, D), F32),
            V((T, L), F32), V((D, D), F32), V((D, D), BF16), V((D, D), BF16), V((3, PLANE, L), F32), V((3, PLANE, L), F32),
            V((T, L), F32), V((T, D), BF16), V((T, D), BF16), V((T, FF), BF16), V((T, FF), BF16),
            V((15, 8, D), F32), V((8, FF), F32), V((15, 8, D), F32), V((8, 3 * D), F32), V((1, D), F32),
            V((4 * D + 2 * FF, D), F32), V((sum(stream_rows(n, STREAMS)), D), F32),
            V((small_rows, L), F32), V((2, 8, L), F32), V((2, n, 8, L), F32),
            dma((images + 3,)), dma((11,)), dma((len(STREAMS), 4, copies)),
            pltpu.SemaphoreType.REGULAR((len(STREAMS), 4)), dma((4, 2)),
        ],
        compiler_params=pltpu.CompilerParams(
            collective_id=0, has_side_effects=True, vmem_limit_bytes=64 * 1024 * 1024
        ),
    )(edges, sharp, x, sens, wqkv, wm, w1, w2, st1, st2, g1, b1, bqkv, bm, fm, g2, b2, cb1, bg, bo, cb2, fl, g3, b3, bb1, bb2, fp)

    sharp_grad = jnp.sum(small[37].reshape(HEADS, HD), axis=1) / sharp
    c = 19
    return (lout, gin, small[c], small[c + 1], dwqkv, small[34:37].reshape(3 * D), sharp_grad, dwm, small[c + 4], small[38],
            small[c + 2], small[c + 3], small[c + 5 : c + 14].reshape(3, 3, D), small[c + 14], small[13], small[14],
            small[4:13].reshape(3, 3, D), small[3], small[39], small[0], small[1], dw1, small[15:19].reshape(FF), dw2,
            small[2], small[40])


def solution(mesh):
    n = mesh.shape["img"]
    split = P("img", None, None)
    return jax.shard_map(
        lambda *args: on_device(n, *args),
        mesh=mesh,
        in_specs=(split, split, P("img")) + (P(),) * 24,
        out_specs=(split, split) + (P(),) * 24,
        check_vma=False,
    )
```

time: 406 us -> 226 us (0.56)
  waiting for transfers between devices: 121 us -> 0 us
  blocking collectives: 43.9 us -> 0 us
  between operations: 14.4 us -> 0.7 us
  Pallas kernels: 198 us -> 205 us
  local copies, waits for them, and re-layouts: 23.6 us -> 18.1 us
    psum x1 -> x0, waiting for transfers between devices: 120 us -> none  [on_device(): lax.psum((small_b, small_c, hidden_bias, qkv_bias, srow, dwm, dwqkv, dw1,...]
    psum x1 -> x0, blocking collectives: 43.9 us -> none  [on_device(): lax.psum((small_b, small_c, hidden_bias, qkv_bias, srow, dwm, dwqkv, dw1,...]
    reshape x20 -> x4, local copies, waits for them, and re-layouts: 15.8 us -> 2.45 us  [the longest x1 0.62 us: on_device(): small[4:13].reshape(3, 3, D)]
    pallas_call x5 -> x1, Pallas kernels: 198 us -> 205 us  [on_device(): pl.pallas_call(lambda *refs: mega_kernel(n, images, refs), in_specs=[sm,...]
    unnamed x60 -> x16, local copies, waits for them, and re-layouts: 7.13 us -> 11.7 us
  transfers between devices with their start and end apart: 1 -> 0, of which waited for: 1 -> 0; matrix products, arithmetic and copies ran while one was open for 1% -> 0% of each run, Pallas kernels for 0% -> 0%
where the time goes in v2:
time: 226 us; the launch traced here: 225 us
  Pallas kernels  205 us (91%)
  local copies, waits for them, and re-layouts  18.1 us (8%)
    pallas_call x1, Pallas kernels, on_device(): pl.pallas_call(lambda *refs: mega_kernel(n, images, refs), in_specs=[sm,...  205 us
    unnamed x16, local copies, waits for them, and re-layouts  11.7 us

profile of v2, /device:TPU:0, one launch (start us, length us, event | category | flops | bytes accessed | tf_op | source)
XLA Modules:
  0.0 225.1 jit_solution(7466406934630980195)
XLA Ops:
  0.7 205.0 %shard_map.458 = (bf16[4,576,384]{2,1,0:T(8,128)(2,1)}, bf16[4,576,384]{2,1,0:T(8,128)(2,1)}, f32[384,1152]{1,0:T(8,128)}, f32[384,384]{1,0:T(8,128)}, f32[384,1...) custom-call(s32[4]{0:T(128)} %refs_0_.1, f32[8]{0:T(128)} %refs_1_.1, bf16[4,576,384]{2,1,0:T(8,128)(2,1)} %refs_2_.1, ...), custom_call_target="tpu_custom_call" | custom-call | tf_op jit(solution)/shard_map/pallas_call | solution.py:900
  205.7 0.7 slice.62
  206.4 0.6 reshape.64
  207.0 0.7 slice.77
  207.7 0.6 reshape.67
  208.3 1.7 slice_reduce_fusion
  210.0 0.8 fusion
  210.8 0.6 reshape.66
  211.4 0.1 reshape_squeeze.3
  211.5 0.1 reduce_sum.9
  211.6 1.2 div.3
  212.8 0.6 reshape.65
  213.4 0.0 copy-start.3
  213.4 3.0 %copy.59 = bf16[4,576,384]{2,1,0:T(8,128)(2,1)} copy(bf16[4,576,384]{2,1,0:T(8,128)(2,1)} %get-tuple-element.84) | data formatting | bytes 3538944
  216.4 0.0 copy-done.3
  216.4 0.0 copy-start.2
  216.4 1.2 copy.60
  217.6 0.9 copy-done.2
  218.5 0.0 copy-start.4
  218.5 0.0 copy-start.1
  218.5 1.2 copy.61
  219.7 0.2 copy-done.4
  220.0 0.8 copy.62
  220.8 0.4 copy-done.1
  221.2 0.0 copy-start
  221.2 1.4 copy.63
  222.6 1.1 copy-done
  223.7 1.4 copy.64
Async XLA Ops:
  213.4 3.0 %copy-start.3 = (bf16[4,576,384]{2,1,0:T(8,128)(2,1)S(1)}, bf16[4,576,384]{2,1,0:T(8,128)(2,1)}, u32[]{:S(2)}) copy-start(bf16[4,576,384]{2,1,0:T(8,128)(2,1)} %get-tuple-element.85) | copy-start | bytes 5308420
  216.4 2.1 copy-start.2
  218.5 1.4 copy-start.4
  218.5 2.7 %copy-start.1 = (f32[384,1536]{1,0:T(8,128)S(1)}, f32[384,1536]{1,0:T(8,128)}, u32[]{:S(2)}) copy-start(f32[384,1536]{1,0:T(8,128)} %get-tuple-element.105) | copy-start | bytes 7077892
  221.2 2.5 %copy-start = (f32[1536,384]{1,0:T(8,128)S(1)}, f32[1536,384]{1,0:T(8,128)}, u32[]{:S(2)}) copy-start(f32[1536,384]{1,0:T(8,128)} %get-tuple-element.107) | copy-start | bytes 7077892

commit v3 on v2

--- a/solution.py
+++ b/solution.py
@@ -786,6 +786,21 @@
         return 0
 
     lax.fori_loop(0, images, middle, 0)
+
+    streams = []
+    at, start = 0, 0
+    for k, (size, received) in enumerate(zip(STREAMS, stream_rows(n, STREAMS))):
+        piece = recv.at[pl.ds(at, received), :]
+        steps = stream_steps(n, k % 2 == 0)
+        streams.append(Stream(place, steps, grads, start, size, piece, group_sems.at[k], credits.at[k]))
+        at, start = at + received, start + size
+
+    def tick(*which):
+        for k in which:
+            if streams[k].done <= streams[k].last:
+                streams[k].advance()
+
+    tick(4, 5, 2, 3)
     out_copies = [pltpu.make_async_copy(sens, lout, out_sems.at[0])]
     out_copies[0].start()
 
@@ -794,7 +809,9 @@
         stage_b8(i, act, stats, bg, bo, fl, st2, resid, vh3, sm_b, mask, plane, plane2)
         return 0
 
-    lax.fori_loop(0, images, conv_back, 0)
+    lax.fori_loop(0, images // 2, conv_back, 0)
+    tick(4, 5)
+    lax.fori_loop(images // 2, images, conv_back, 0)
     for k in range(15):
         put_small(small, k, total(sm_b[k]))
     for j in range(4):
@@ -816,7 +833,10 @@
         stage_c3(i, resid, vh2, r2, fm, g2, sm_c, mask, back, slope)
         return 0
 
-    lax.fori_loop(0, images, rear1, 0)
+    tick(4, 5)
+    lax.fori_loop(0, images // 2, rear1, 0)
+    tick(4, 5, 2, 3)
+    lax.fori_loop(images // 2, images, rear1, 0)
     stage_c4(mixed, dwm, slope)
 
     def rear2(i, _):
@@ -825,8 +845,14 @@
         stage_c6(i, qkv, smq, slope, pmat, alow, cqk)
         return 0
 
-    lax.fori_loop(0, images, rear2, 0)
+    lax.fori_loop(0, images // 4, rear2, 0)
+    tick(4, 5, 2, 3)
+    lax.fori_loop(images // 4, images // 2, rear2, 0)
+    tick(2, 3)
+    lax.fori_loop(images // 2, images, rear2, 0)
+    tick(4, 5)
     stage_c7(n1, qkv, dwq, dwk, dwv)
+    tick(4, 5, 2, 3, 0, 1)
 
     def rear3(i, _):
         write_mask(edges[i], mask)
@@ -844,21 +870,12 @@
 
     push_all(place, lambda device: small.at[rows(device * 8, 8), :], gathered.at[0, me], push_sems.at[2])
     gathered[0, me] = small[rows(me * 8, 8), :]
-    streams = []
-    at, start = 0, 0
-    for k, (size, received) in enumerate(zip(STREAMS, stream_rows(n, STREAMS))):
-        piece = recv.at[pl.ds(at, received), :]
-        steps = stream_steps(n, k % 2 == 0)
-        streams.append(Stream(place, steps, grads, start, size, piece, group_sems.at[k], credits.at[k]))
-        at, start = at + received, start + size
-    for stream in streams:
-        stream.advance()
+    tick(0, 1, 4, 5, 2, 3)
     land_all(gathered.at[0, pl.ds(0, n - 1)], push_sems.at[2])
     gathered[1, me] = lax.fori_loop(0, n, lambda k, carry: carry + gathered[0, k], zeros(8, L))
     push_all(place, lambda device: gathered.at[1, me], gathered.at[1, me], push_sems.at[3])
     for k in range(streams[0].last):
-        for stream in streams:
-            stream.advance()
+        tick(0, 1, 4, 5, 2, 3)
     land_all(gathered.at[1, pl.ds(0, n - 1)], push_sems.at[3])
     for k in range(16):
         small[8 * k : 8 * k + 8, :] = gathered[1, k]
@@ -879,9 +896,43 @@
     local = sum(st2[a, b : b + 1, :] * picked[4 + 3 * a + b] for a in range(3) for b in range(3))
     picked.append((local + cb2[...] * picked[3]) / fl[...])
     picked.append(branch_factor(w2[...], dw2[...], bb2[...], picked[2], fp[...]))
+    lane = lax.broadcasted_iota(jnp.int32, (1, D), 1)
+    by_head = zeros(1, D)
+    for h in range(HEADS):
+        own = jnp.where((lane >= h * HD) & (lane < (h + 1) * HD), picked[37], 0.0)
+        by_head = jnp.where(lane == h, jnp.sum(own, axis=1, keepdims=True) / sharp[h], by_head)
+    picked.append(by_head)
     for k, row in enumerate(picked):
         small_out[k : k + 1, :] = row
     for copy in out_copies:
+        copy.wait()
+
+
+SINGLES = (0, 1, 2, 3, 13, 14, 19, 20, 21, 22, 23, 33, 38, 39, 40)
+
+
+def deliver_kernel(*refs):
+    small, outs, stage, sems = refs[6], refs[7:-7], refs[-7:-1], refs[-1]
+    loads = [pltpu.make_async_copy(refs[k], stage[k], sems.at[0, k]) for k in range(6)]
+    copies = [pltpu.make_async_copy(stage[k], outs[k], sems.at[1, k]) for k in range(6)]
+    for load in loads:
+        load.start()
+    qkv_bias, hidden_bias, sharp_grad, conv1, conv2 = outs[6:11]
+    for p in range(3):
+        qkv_bias[p * D : (p + 1) * D] = small[34 + p : 35 + p, :].reshape(D)
+    for j in range(4):
+        hidden_bias[j * D : (j + 1) * D] = small[15 + j : 16 + j, :].reshape(D)
+    sharp_grad[...] = small[41:42, :].reshape(D)[0:HEADS]
+    for a in range(3):
+        for b in range(3):
+            conv2[a, b : b + 1, :] = small[4 + 3 * a + b : 5 + 3 * a + b, :]
+            conv1[a, b : b + 1, :] = small[24 + 3 * a + b : 25 + 3 * a + b, :]
+    for k, out in zip(SINGLES, outs[11:]):
+        out[...] = small[k : k + 1, :].reshape(D)
+    for load, copy in zip(loads, copies):
+        load.wait()
+        copy.start()
+    for copy in copies:
         copy.wait()
 
 
@@ -922,12 +973,21 @@
         ),
     )(edges, sharp, x, sens, wqkv, wm, w1, w2, st1, st2, g1, b1, bqkv, bm, fm, g2, b2, cb1, bg, bo, cb2, fl, g3, b3, bb1, bb2, fp)
 
-    sharp_grad = jnp.sum(small[37].reshape(HEADS, HD), axis=1) / sharp
-    c = 19
-    return (lout, gin, small[c], small[c + 1], dwqkv, small[34:37].reshape(3 * D), sharp_grad, dwm, small[c + 4], small[38],
-            small[c + 2], small[c + 3], small[c + 5 : c + 14].reshape(3, 3, D), small[c + 14], small[13], small[14],
-            small[4:13].reshape(3, 3, D), small[3], small[39], small[0], small[1], dw1, small[15:19].reshape(FF), dw2,
-            small[2], small[40])
+    vector = S((D,), F32)
+    stencil_shape = S((3, 3, D), F32)
+    (lout, gin, dwqkv, dwm, dw1, dw2, qkv_bias, hidden_bias, sharp_grad, conv1, conv2, *singles) = pl.pallas_call(
+        deliver_kernel,
+        in_specs=[hbm] * 6 + [vm],
+        out_specs=[hbm] * 6 + [vm] * (5 + len(SINGLES)),
+        out_shape=[S(v.shape, v.dtype) for v in (lout, gin, dwqkv, dwm, dw1, dw2)]
+        + [S((3 * D,), F32), S((FF,), F32), S((HEADS,), F32), stencil_shape, stencil_shape]
+        + [vector] * len(SINGLES),
+        scratch_shapes=[V(v.shape, v.dtype) for v in (lout, gin, dwqkv, dwm, dw1, dw2)] + [dma((2, 6))],
+        compiler_params=pltpu.CompilerParams(vmem_limit_bytes=62 * 1024 * 1024),
+    )(lout, gin, dwqkv, dwm, dw1, dw2, small)
+    one = dict(zip(SINGLES, singles))
+    return (lout, gin, one[19], one[20], dwqkv, qkv_bias, sharp_grad, dwm, one[23], one[38], one[21], one[22], conv1, one[33],
+            one[13], one[14], conv2, one[3], one[39], one[0], one[1], dw1, hidden_bias, dw2, one[2], one[40])
 
 
 def solution(mesh):

time: 226 us -> 175 us (0.77)
  Pallas kernels: 205 us -> 173 us
  local copies, waits for them, and re-layouts: 18.1 us -> 0 us
    pallas_call x1, Pallas kernels: 205 us -> 164 us  [on_device(): pl.pallas_call(lambda *refs: mega_kernel(n, images, refs), in_specs=[sm,...]
    unnamed x16 -> x0, local copies, waits for them, and re-layouts: 11.7 us -> none
    pallas_call x0 -> x1, Pallas kernels: none -> 9.44 us  [on_device(): pl.pallas_call(deliver_kernel, in_specs=[hbm] * 6 + [vm], out_specs=[hbm]...]
    slice x4 -> x0, local copies, waits for them, and re-layouts: 3.9 us -> none  [the longest x1 1.68 us: on_device(): small[40]]
    reshape x4 -> x0, local copies, waits for them, and re-layouts: 2.45 us -> none  [the longest x1 0.62 us: on_device(): small[4:13].reshape(3, 3, D)]
where the time goes in v3:
time: 175 us; the launch traced here: 174 us
  Pallas kernels  173 us (99%)
    pallas_call x1, Pallas kernels, on_device(): pl.pallas_call(lambda *refs: mega_kernel(n, images, refs), in_specs=[sm,...  164 us
    pallas_call x1, Pallas kernels, on_device(): pl.pallas_call(deliver_kernel, in_specs=[hbm] * 6 + [vm], out_specs=[hbm]...  9.44 us

profile of v3, /device:TPU:0, one launch (start us, length us, event | category | flops | bytes accessed | tf_op | source)
XLA Modules:
  0.0 174.3 jit_solution(880347663675097505)
XLA Ops:
  0.7 164.0 %shard_map.458 = (bf16[4,576,384]{2,1,0:T(8,128)(2,1)}, bf16[4,576,384]{2,1,0:T(8,128)(2,1)}, f32[384,1152]{1,0:T(8,128)}, f32[384,384]{1,0:T(8,128)}, f32[384,1...) custom-call(s32[4]{0:T(128)} %refs_0_.1, f32[8]{0:T(128)} %refs_1_.1, bf16[4,576,384]{2,1,0:T(8,128)(2,1)} %refs_2_.1, ...), custom_call_target="tpu_custom_call" | custom-call | tf_op jit(solution)/shard_map/pallas_call | solution.py:951
  164.7 9.4 %shard_map.459 = (bf16[4,576,384]{2,1,0:T(8,128)(2,1)}, bf16[4,576,384]{2,1,0:T(8,128)(2,1)}, f32[384,1152]{1,0:T(8,128)}, f32[384,384]{1,0:T(8,128)}, f32[384,1...) custom-call(bf16[4,576,384]{2,1,0:T(8,128)(2,1)} %get-tuple-element., ...), custom_call_target="tpu_custom_call" | custom-call | tf_op jit(solution)/shard_map/pallas_call | solution.py:978

commit v4 on v3

--- a/solution.py
+++ b/solution.py
@@ -24,7 +24,8 @@
 PLANE = (G + 4) * PITCH
 RC = T
 RM = T
-RF = T // 2
+RF = T
+FP = 512
 ROOT_HALF = 0.7071067811865476
 ROOT_TWO_PI = 0.3989422804014327
 NT = (((1,), (1,)), ((), ()))
@@ -263,77 +264,66 @@
         lax.fori_loop(0, G // 4, conv_body, 0)
 
 
-def stage_b3(i, sens, g3, b3, fp, sm_b, mask, resid, vh3, r3, n3, f2):
-    def body(r, sl, carry):
-        mk = wide(mask[sl, :])
-        res = resid[i, sl, :]
-        centre = res - lane_mean(res)
-        spread = lax.rsqrt(lane_mean(centre * centre) + EPS_NORM)
-        vhat = centre * spread
-        vh3[i, sl, :] = vhat
-        r3[sl, :] = jnp.broadcast_to(spread, (RC, L))
-        n3[sl, :] = ((vhat * g3[...] + b3[...]) * mk).astype(BF16)
-        err = sens[i, sl, :].astype(F32) * mk * fp[...]
-        f2[sl, :] = err.astype(BF16)
-        return carry + fold8(err)
-
-    sm_b[2] += chunks(body, zeros(8, D), RC)
-
-
-def stage_b4(w1, bb1, w2, smf, n3, f2, hl, e1, branch, back):
+def stage_b3(i, sens, g3, b3, fp, resid, sm_b, mask, n3, f2):
+    mk = wide(mask[...])
+    res = resid[i]
+    centre = res - lane_mean(res)
+    spread = lax.rsqrt(lane_mean(centre * centre) + EPS_NORM)
+    n3[i] = ((centre * spread * g3[...] + b3[...]) * mk).astype(BF16)
+    err = sens[i].astype(F32) * mk * fp[...]
+    f2[i] = err.astype(BF16)
+    sm_b[2] += fold8(err)
+
+
+def stage_b4(i, part, w1, bb1, w2, smf, n3, f2, hl, e1, branch, back):
     def body(r, sl, hidden_sum):
-        normed = n3[sl, :]
-        low = f2[sl, :]
-        parts = []
-        for j in range(FF // 256):
+        normed = n3[i, sl, :]
+        low = f2[i, sl, :]
+        sums = []
+        for j in range(FP // 256):
             cols = slice(j * 256, (j + 1) * 256)
-            value, diff = gelu_pair(dot(normed, w1[:, cols]) + bb1[:, cols])
-            hl[sl, cols] = value.astype(BF16)
-            err = dot(low, w2[cols, :], NT) * diff
-            parts.append(fold8(err))
-            e1[sl, cols] = err.astype(BF16)
-        branch[sl, :] = dot(hl[sl, :], w2[...])
-        back[sl, :] = dot(e1[sl, :], w1[...], NT)
-        return hidden_sum + jnp.concatenate(parts, axis=1)
-
-    smf[...] += chunks(body, zeros(8, FF), RF)
-
-
-def stage_b5(i, sens, bb2, fp, g3, fl, resid, sm_b, mask, vh3, r3, branch, back):
-    def body(r, sl, carry):
-        gain_sum, shift_sum, local_sum = carry
-        mk = wide(mask[sl, :])
-        upstream = sens[i, sl, :].astype(F32) * mk
-        sens[i, sl, :] = ((resid[i, sl, :] + fp[...] * (branch[sl, :] + bb2[...])) * mk).astype(BF16)
-        err = back[sl, :] * mk
-        vhat = vh3[i, sl, :]
-        shift_sum = shift_sum + fold8(err)
-        gain_sum = gain_sum + fold8(err * vhat)
-        eg = err * g3[...]
-        mean1 = lane_mean(eg)
-        mean2 = lane_mean(eg * vhat)
-        grad = upstream + wide(r3[sl, :]) * (eg - mean1 - vhat * mean2)
-        resid[i, sl, :] = grad
-        local_sum = local_sum + fold8(grad * mk)
-        return gain_sum, shift_sum, local_sum
-
-    sums = chunks(body, (zeros(8, D),) * 3, RC)
-    sm_b[0] += sums[0]
-    sm_b[1] += sums[1]
-    sm_b[3] += sums[2] * fl[...]
-
-
-def stage_b6(dw1, n3, e1):
-    left = n3[...].T
-    for j in range(FF // 512):
-        part = dot(left, e1[:, j * 512 : (j + 1) * 512])
-        for k in range(4):
-            block, col = divmod(j * 512 + k * L, D)
-            dw1[block * D : (block + 1) * D, col : col + L] += part[:, k * L : (k + 1) * L]
-
-
-def stage_b7(dw2, hl, f2):
-    dw2[...] += dot(hl[...], f2[...], TN)
+            units = slice(part * FP + j * 256, part * FP + (j + 1) * 256)
+            value, diff = gelu_pair(dot(normed, w1[:, units]) + bb1[:, units])
+            hl[i, sl, cols] = value.astype(BF16)
+            err = dot(low, w2[units, :], NT) * diff
+            sums.append(fold8(err))
+            e1[i, sl, cols] = err.astype(BF16)
+        units = slice(part * FP, (part + 1) * FP)
+        forward = dot(hl[i, sl, :], w2[units, :])
+        backward = dot(e1[i, sl, :], w1[:, units], NT)
+        if part == 0:
+            branch[i, sl, :] = forward
+            back[i, sl, :] = backward
+        else:
+            branch[i, sl, :] += forward
+            back[i, sl, :] += backward
+        return hidden_sum + jnp.concatenate(sums, axis=1)
+
+    smf[:, part * FP : (part + 1) * FP] += chunks(body, zeros(8, FP), RF)
+
+
+def stage_b5(i, sens, bb2, fp, g3, fl, resid, sm_b, mask, branch, back):
+    mk = wide(mask[...])
+    res = resid[i]
+    centre = res - lane_mean(res)
+    spread = lax.rsqrt(lane_mean(centre * centre) + EPS_NORM)
+    vhat = centre * spread
+    upstream = sens[i].astype(F32) * mk
+    sens[i] = ((res + fp[...] * (branch[i] + bb2[...])) * mk).astype(BF16)
+    err = back[i] * mk
+    sm_b[1] += fold8(err)
+    sm_b[0] += fold8(err * vhat)
+    eg = err * g3[...]
+    mean1 = lane_mean(eg)
+    mean2 = lane_mean(eg * vhat)
+    grad = upstream + spread * (eg - mean1 - vhat * mean2)
+    resid[i] = grad
+    sm_b[3] += fold8(grad * mk) * fl[...]
+
+
+def stage_b6(out, left, right):
+    images, _, width = left.shape
+    out[...] = dot(right[...].reshape(images * T, D), left[...].reshape(images * T, width), TN).T
 
 
 def stage_b8(i, act, stats, bg, bo, fl, st2, resid, bng, sm_b, mask, plane, plane2):
@@ -434,12 +424,21 @@
     dwm[...] = dot(mixed[...].reshape(images * T, D), plow[...].reshape(images * T, D), TN)
 
 
-def stage_c4b(i, wm, plow):
-    plow[i] = dot(plow[i], wm[...], NT).astype(BF16)
-
-
-def stage_c5(i, qkv, score, sqk, srow, sharp_mask, plow, pmat, alow, cqk):
-    raw = dot(plow[i], qkv[i, :, 2 * D :], TN)
+def stage_c5a(i, wm, qkv, score, smq, sharp_mask, plow, pmat, attn_grad):
+    mixed_grad = dot(plow[i], wm[...], NT).astype(BF16)
+    for h in range(HEADS):
+        band = slice(h * HD, (h + 1) * HD)
+        pmat[band, :] = softmax_band(score[i, band, :], sharp_mask[band, :]).astype(BF16)
+    raw = dot(mixed_grad, qkv[i, :, 2 * D :], TN)
+    for h in range(HEADS):
+        band = slice(h * HD, (h + 1) * HD)
+        attn_grad[i, band, :] = jnp.where(sharp_mask[band, :] > 0.0, raw[band], 0.0)
+    value_grad = dot(mixed_grad, pmat[...])
+    smq[:, 2 * D :] += fold8(value_grad)
+    qkv[i, :, 2 * D :] = value_grad.astype(BF16)
+
+
+def stage_c5b(i, score, sqk, srow, sharp_mask, attn_grad, alow, cqk):
     sq, sk = sqk[i, 0, 0:1, :], sqk[i, 1, 0:1, :]
     sqcol = column_of(sq)
     colsum = zeros(8, D)
@@ -449,8 +448,7 @@
         sc = score[i, band, :]
         sh = sharp_mask[band, :]
         pr = softmax_band(sc, sh)
-        pmat[band, :] = pr.astype(BF16)
-        weighted = raw[band] * pr
+        weighted = attn_grad[i, band, :] * pr
         logit = weighted - pr * jnp.sum(weighted, axis=1, keepdims=True)
         lg = logit * sh
         cross = lg * sc
@@ -464,25 +462,20 @@
     cqk[1:2, :] = sk * sk * total(colsum)
 
 
-def stage_c6(i, qkv, smq, plow, pmat, alow, cqk):
+def stage_c6(i, qkv, smq, pmat, alow, cqk):
     cq, ck = cqk[0:1, :], cqk[1:2, :]
     qv, kv = qkv[i, :, :D], qkv[i, :, D : 2 * D]
-    grads = (
-        dot(kv, alow[...], NT) - qv.astype(F32) * cq,
-        dot(qv, alow[...]) - kv.astype(F32) * ck,
-        dot(plow[i], pmat[...]),
-    )
-    for p in range(3):
+    grads = (dot(kv, alow[...], NT) - qv.astype(F32) * cq, dot(qv, alow[...]) - kv.astype(F32) * ck)
+    for p in range(2):
         cols = slice(p * D, (p + 1) * D)
         smq[:, cols] += fold8(grads[p])
         qkv[i, :, cols] = grads[p].astype(BF16)
 
 
-def stage_c7(n1, qkv, dwq, dwk, dwv):
+def stage_c7(part, n1, qkv, out):
     images = n1.shape[0]
-    left = n1[...].reshape(images * T, D).T
-    for p, out in enumerate((dwq, dwk, dwv)):
-        out[...] = dot(left, qkv[:, :, p * D : (p + 1) * D].reshape(images * T, D))
+    left = n1[...].reshape(images * T, D)
+    out[...] = dot(left, qkv[:, :, part * D : (part + 1) * D].reshape(images * T, D), TN)
 
 
 def stage_c8(i, x, g1, wqkv, resid, sm_c, mask, qkv):
@@ -515,6 +508,7 @@
         for name, size in (("core", 2), ("x", x), ("y", y), ("z", z)):
             self.axes[name] = (size, stride, lax.rem(self.me // stride, size))
             stride *= size
+        self.axes["plane"] = (x * y, 2, lax.rem(self.me // 2, x * y))
 
     def other(self, k):
         return lax.rem(self.me + k, self.n)
@@ -522,17 +516,19 @@
 
 def stream_steps(n, first):
     if n == 32:
-        order = ("x", "y") if first else ("y", "x")
-        return [("core", True), (order[0], True), (order[1], True), ("z", True)]
+        order = ("plane", "z") if first else ("z", "plane")
+        return [("core", True), (order[0], True), (order[1], True)]
     order = ("x", "z") if first else ("z", "x")
     return [("core", True), (order[0], True), (order[1], True), ("y", False)]
 
 
-STREAMS = (FF // 2,) * 6
+STREAMS = ((512, True), (512, False), (512, True), (512, True), (512, True), (512, True), (512, False), (512, True), (512, True))
+TAIL, PART0, PART1, PART2 = (0, 1, 2), (3, 4), (5, 6), (7, 8)
 
 
 def stream_shape(n, steps, size):
-    axes = dict(zip(("core", "x", "y", "z"), (2,) + geometry(n)))
+    x, y, z = geometry(n)
+    axes = {"core": 2, "x": x, "y": y, "z": z, "plane": x * y}
     received, copies, length = 0, 0, size
     for axis, split in steps:
         s = axes[axis]
@@ -541,6 +537,25 @@
         copies += s - 1
         length = piece
     return received, copies
+
+
+PLAN = {
+    "part0": (PART0,),
+    "mlp1": {2: (PART0,)},
+    "part1": (PART1,),
+    "mlp2": {2: (PART1,), 3: (PART0,)},
+    "part2": (PART2,),
+    "conv_back": {1: (PART2,), 2: (PART1,), 3: (PART0,)},
+    "exchange": (PART0, PART1, PART2,),
+    "rear1": {},
+    "rear2": {0: (PART2,), 1: (PART0,), 2: (PART1,)},
+    "value": (PART0, PART2,),
+    "rear3": {},
+    "query": (TAIL, PART1,),
+    "rear4": {0: (PART2,), 2: (TAIL,), 3: (PART1,)},
+    "small": (PART2,),
+    "end": (PART0, PART1, PART2, TAIL),
+}
 
 
 class Stream:
@@ -557,7 +572,6 @@
             if split:
                 off = off + k * piece
             length = piece
-        self.flying = []
         self.done = 0
         self.last = 2 * len(steps)
 
@@ -567,39 +581,35 @@
             p = lax.rem(k + j, s)
             yield j, p, self.place.me + (p - k) * stride
 
-    def send(self, src, dst, side, sem, device):
-        copy = pltpu.make_async_remote_copy(
-            src_ref=src,
-            dst_ref=dst,
-            send_sem=self.sems.at[side, sem],
-            recv_sem=self.sems.at[side + 1, sem],
-            device_id=(device,),
-            device_id_type=MESH,
-        )
-        copy.start()
-        self.flying.append(copy)
-
-    def land(self):
-        for copy in self.flying:
-            copy.wait()
-        self.flying = []
-
-    def start_sum(self, step):
+    def copies(self, step, gather):
         axis, split, off, piece, slot, sem = self.down[step]
+        s, stride, k = self.place.axes[axis]
+        side = 2 if gather else 0
         for j, p, device in self.peers(axis):
-            src = self.buf.at[rows(off + p * piece if split else off, piece), :]
-            dst = self.recv.at[pl.ds(slot + (j - 1) * piece, piece), :]
-            self.send(src, dst, 0, sem + j - 1, device)
+            if gather:
+                src = dst = self.buf.at[rows(off + k * piece, piece), :]
+            else:
+                src = self.buf.at[rows(off + p * piece if split else off, piece), :]
+                dst = self.recv.at[pl.ds(slot + (j - 1) * piece, piece), :]
+            yield pltpu.make_async_remote_copy(
+                src_ref=src,
+                dst_ref=dst,
+                send_sem=self.sems.at[side, sem + j - 1],
+                recv_sem=self.sems.at[side + 1, sem + j - 1],
+                device_id=(device,),
+                device_id_type=MESH,
+            )
 
     def finish_sum(self, step):
         axis, split, off, piece, slot, sem = self.down[step]
         s, stride, k = self.place.axes[axis]
-        self.land()
+        for copy in self.copies(step, False):
+            copy.wait()
         if split:
             for j, p, device in self.peers(axis):
                 pl.semaphore_signal(self.credits.at[step], inc=1, device_id=(device,), device_id_type=MESH)
             own = off + k * piece
-            size = math.gcd(piece, 96)
+            size = next(s_ for s_ in (128, 96, 64, 32, 24, 16, 8) if piece % s_ == 0)
 
             def add(r, _):
                 sl = rows(own + r * size, size)
@@ -609,7 +619,10 @@
                 self.buf[sl, :] = summed
                 return 0
 
-            lax.fori_loop(0, piece // size, add, 0)
+            if piece == size:
+                add(0, 0)
+            else:
+                lax.fori_loop(0, piece // size, add, 0)
         else:
             sl = rows(off, piece)
             own = self.buf[sl, :]
@@ -621,32 +634,25 @@
                 summed = term if summed is None else summed + term
             self.buf[sl, :] = summed
 
-    def start_gather(self, step):
-        axis, split, off, piece, slot, sem = self.down[step]
-        if split:
-            s, stride, k = self.place.axes[axis]
-            pl.semaphore_wait(self.credits.at[step], s - 1)
-            part = self.buf.at[rows(off + k * piece, piece), :]
-            for j, p, device in self.peers(axis):
-                self.send(part, part, 2, sem + j - 1, device)
-
-    def advance(self):
-        count, k = self.last // 2, self.done
-        if 0 < k <= self.last:
-            if k <= count:
-                self.finish_sum(k - 1)
-            else:
-                self.land()
-        if k < self.last:
-            if k < count:
-                self.start_sum(k)
-            else:
-                self.start_gather(self.last - 1 - k)
-        self.done += 1
-
-
-def stream_rows(n, sizes):
-    return [stream_shape(n, stream_steps(n, k % 2 == 0), size)[0] for k, size in enumerate(sizes)]
+    def advance(self, k):
+        count = self.last // 2
+        if 0 < k <= count:
+            self.finish_sum(k - 1)
+        elif count < k <= self.last and self.down[self.last - k][1]:
+            for copy in self.copies(self.last - k, True):
+                copy.wait()
+        if k < count:
+            for copy in self.copies(k, False):
+                copy.start()
+        elif k < self.last and self.down[self.last - 1 - k][1]:
+            step = self.last - 1 - k
+            pl.semaphore_wait(self.credits.at[step], self.place.axes[self.down[step][0]][0] - 1)
+            for copy in self.copies(step, True):
+                copy.start()
+
+
+def stream_rows(n):
+    return [stream_shape(n, stream_steps(n, first), size)[0] for size, first in STREAMS]
 
 
 def push_all(place, source, target, sems):
@@ -680,13 +686,13 @@
 
 
 def mega_kernel(n, images, refs):
-    (edges, sharp, x_in, sens_in, wqkv, wm, w1_in, w2_in, st1, st2,
+    (edges, sharp, x_in, sens_in, wqkv_in, wm_in, w1_in, w2_in, st1_in, st2_in,
      g1_in, b1_in, bqkv_in, bm_in, fm_in, g2_in, b2_in, cb1_in, bg_in, bo_in, cb2_in, fl_in, g3_in, b3_in, bb1_in, bb2_in, fp_in,
-     lout, gin, dwqkv_out, dwm_out, dw1_out, dw2_out, small_out,
-     vecs, x, sens, w1, w2, n1, qkv, mixed, score, sqk, r2, resid, vh2, act, vh3, slope, stat, stats, bsums, cqk,
-     mask, sharp_mask, pmat, alow, plane, plane2, r3, n3, f2, hl, e1,
+     lout, gin, dwqkv_out, dwm_out, dw1_out, dw2_out, small_out, n1_away, mixed_away, vh2_away,
+     vecs, x, sens, wqkv, wm, w1, w2, st1, st2, n1, qkv, mixed, score, sqk, r2, resid, vh2, act, vh3, slope, stat, stats, bsums, cqk,
+     mask, sharp_mask, pmat, alow, plane, plane2, hl, e1,
      sm_b, smf, sm_c, smq, srow, grads, recv, small, payload, gathered,
-     in_sems, out_sems, group_sems, credits, push_sems) = refs
+     in_sems, out_sems, away_sems, group_sems, credits, push_sems) = refs
     place = Place(n)
     me = place.me
     barrier = pltpu.get_barrier_semaphore()
@@ -695,39 +701,34 @@
         pl.semaphore_signal(barrier, inc=1, device_id=(place.other(k),), device_id_type=MESH)
         return 0
 
-    lax.fori_loop(1, n, greet, 0)
-
-    x_copies = [pltpu.make_async_copy(x_in.at[k], x.at[k], in_sems.at[k]) for k in range(images)]
-    later = [(w1_in, w1), (w2_in, w2), (sens_in, sens)]
-    later_copies = [pltpu.make_async_copy(a, b, in_sems.at[images + k]) for k, (a, b) in enumerate(later)]
-    for copy in x_copies + later_copies:
-        copy.start()
-
-    names = {}
-    at = 0
     vectors = (("g1", g1_in), ("b1", b1_in), ("bm", bm_in), ("fm", fm_in), ("g2", g2_in), ("b2", b2_in), ("cb1", cb1_in),
                ("bg", bg_in), ("bo", bo_in), ("cb2", cb2_in), ("fl", fl_in), ("g3", g3_in), ("b3", b3_in), ("bb2", bb2_in),
-               ("fp", fp_in))
-    for name, ref in vectors:
-        vecs[at : at + 1, 0:D] = ref[...].reshape(1, D)
-        names[name] = vecs.at[at : at + 1, 0:D]
-        at += 1
-    vecs[at : at + 1, 0 : 3 * D] = bqkv_in[...].reshape(1, 3 * D)
-    bqkv = vecs.at[at : at + 1, 0 : 3 * D]
-    vecs[at + 1 : at + 2, :] = bb1_in[...].reshape(1, FF)
-    bb1 = vecs.at[at + 1 : at + 2, :]
-    g1, b1, bm, fm, g2, b2, cb1, bg, bo, cb2, fl, g3, b3, bb2, fp = (names[name] for name, ref in vectors)
+               ("fp", fp_in), ("bqkv", bqkv_in), ("bb1", bb1_in))
+    pairs = [(ref, vecs.at[k, pl.ds(0, ref.shape[0])]) for k, (name, ref) in enumerate(vectors)]
+    pairs += [(wqkv_in, wqkv), (wm_in, wm), (st1_in, st1), (st2_in, st2)]
+    pairs += [(x_in.at[k], x.at[k]) for k in range(images)]
+    early = len(pairs)
+    pairs += [(w1_in, w1), (w2_in, w2), (sens_in, sens)]
+    in_copies = [pltpu.make_async_copy(a, b, in_sems.at[k]) for k, (a, b) in enumerate(pairs)]
+    for copy in in_copies:
+        copy.start()
+    lax.fori_loop(1, n, greet, 0)
+    (g1, b1, bm, fm, g2, b2, cb1, bg, bo, cb2, fl, g3, b3, bb2, fp, bqkv, bb1) = (
+        vecs.at[k : k + 1, 0 : ref.shape[0]] for k, (name, ref) in enumerate(vectors)
+    )
 
     write_sharp(sharp_mask, sharp)
     for ref in (plane, plane2, sm_b, smf, sm_c, smq, srow, small):
         ref[...] = jnp.zeros_like(ref)
     dwq, dwk, dwv, dwm = (grads.at[k * D : (k + 1) * D, :] for k in range(4))
-    branch, back = grads.at[0:T, :], grads.at[T : 2 * T, :]
-    dw2 = grads.at[4 * D + FF : 4 * D + 2 * FF, :]
-    dw1 = grads.at[4 * D : 4 * D + FF, :]
-    grads[4 * D :, :] = zeros(2 * FF, D)
-
-    for copy in x_copies:
+    back = grads.at[0:T, :]
+    starts = [4 * D + part * 2 * FP for part in range(FF // FP)]
+    first = [grads.at[at : at + FP, :] for at in starts]
+    second = [grads.at[at + FP : at + 2 * FP, :] for at in starts]
+    n3, f2, branch, rear = n1, mixed, vh2, vh3
+    away = [(n1, n1_away), (mixed, mixed_away), (vh2, vh2_away)]
+
+    for copy in in_copies[:early]:
         copy.wait()
 
     def front(i, _):
@@ -739,6 +740,8 @@
         stage_a4(i, x, wm, bm, fm, g2, b2, qkv, mixed, resid, vh2, r2, mask, plane, pmat)
         stage_a5(i, st1, cb1, act, slope, stat, mask, plane)
         stage_a6(i, edge, act, stat, mask)
+        for k, (a, b) in enumerate(away):
+            pltpu.make_async_copy(a.at[i], b.at[i], away_sems.at[k]).start()
         return 0
 
     lax.fori_loop(0, images, front, 0)
@@ -750,68 +753,95 @@
     pl.semaphore_wait(barrier, n - 1)
     push_all(place, lambda device: payload.at[0], gathered.at[0, me], push_sems.at[0])
     gathered[0, me] = payload[0]
-    for copy in later_copies:
+    for copy in in_copies[early:]:
         copy.wait()
     land_all(gathered.at[0, pl.ds(0, n - 1)], push_sems.at[0])
 
-    def sum_both(k, carry):
-        return carry + gathered[0, k]
-
-    summed = lax.fori_loop(0, n, sum_both, zeros(8, L))
+    parts = gathered[0]
+    summed = jnp.sum(parts, axis=0)
     count = summed[6:7, :]
-    mean = summed[0:3, :] / count
-
-    def sum_squares(k, carry):
-        part = gathered[0, k]
-        own = part[6:7, :]
-        gap = part[0:3, :] / own - mean
-        return carry + part[3:6, :] + own * gap * gap
-
-    square = lax.fori_loop(0, n, sum_squares, zeros(3, L))
+    average = summed / count
+    own = jnp.broadcast_to(parts[:, 6:7, :], parts.shape)
+    gap = parts / own - average
+    square = summed[3:6, :] + jnp.sum(own * gap * gap, axis=0)[0:3, :]
+    mean = average[0:3, :]
     inv = lax.rsqrt(square / count + EPS_BATCH)
     for c in range(3):
         stats[0:1, c * L : (c + 1) * L] = mean[c : c + 1, :]
         stats[1:2, c * L : (c + 1) * L] = inv[c : c + 1, :]
         stats[2:3, c * L : (c + 1) * L] = count
 
-    def middle(i, _):
+    streams = []
+    at, start = 0, 0
+    for k, ((size, x_first), received) in enumerate(zip(STREAMS, stream_rows(n))):
+        piece = recv.at[pl.ds(at, received), :]
+        steps = stream_steps(n, x_first)
+        streams.append(Stream(place, steps, grads, start, size, piece, group_sems.at[k], credits.at[k]))
+        at, start = at + received, start + size
+
+    def book(sets):
+        moves = []
+        for which in sets:
+            for k in which:
+                if streams[k].done <= streams[k].last:
+                    moves.append((k, streams[k].done))
+                    streams[k].done += 1
+        return moves
+
+    def move(moves):
+        for k, step in moves:
+            streams[k].advance(step)
+
+    def tick(*sets):
+        move(book(sets))
+
+    def image_loop(body, plan):
+        booked = {k: book(sets) for k, sets in sorted(plan.items())}
+
+        def step(i, _):
+            body(i)
+            for k, moves in booked.items():
+
+                @pl.when(i == k)
+                def _():
+                    move(moves)
+
+            return 0
+
+        lax.fori_loop(0, images, step, 0)
+
+    for k, (a, b) in enumerate(away):
+        pltpu.make_async_copy(a, b, away_sems.at[k]).wait()
+
+    def middle(i):
         write_mask(edges[i], mask)
         stage_b1(i, act, stats, bg, bo, mask, plane)
         stage_b2(i, st2, cb2, fl, resid, mask, plane)
-        stage_b3(i, sens, g3, b3, fp, sm_b, mask, resid, vh3, r3, n3, f2)
-        stage_b4(w1, bb1, w2, smf, n3, f2, hl, e1, branch, back)
-        stage_b5(i, sens, bb2, fp, g3, fl, resid, sm_b, mask, vh3, r3, branch, back)
-        stage_b6(dw1, n3, e1)
-        stage_b7(dw2, hl, f2)
-        return 0
-
-    lax.fori_loop(0, images, middle, 0)
-
-    streams = []
-    at, start = 0, 0
-    for k, (size, received) in enumerate(zip(STREAMS, stream_rows(n, STREAMS))):
-        piece = recv.at[pl.ds(at, received), :]
-        steps = stream_steps(n, k % 2 == 0)
-        streams.append(Stream(place, steps, grads, start, size, piece, group_sems.at[k], credits.at[k]))
-        at, start = at + received, start + size
-
-    def tick(*which):
-        for k in which:
-            if streams[k].done <= streams[k].last:
-                streams[k].advance()
-
-    tick(4, 5, 2, 3)
+        stage_b3(i, sens, g3, b3, fp, resid, sm_b, mask, n3, f2)
+
+    image_loop(middle, {})
+    for part in range(FF // FP):
+
+        def feed(i):
+            stage_b4(i, part, w1, bb1, w2, smf, n3, f2, hl, e1, branch, rear)
+
+        image_loop(feed, PLAN[f"mlp{part}"] if part else {})
+        stage_b6(second[part], hl, f2)
+        stage_b6(first[part], e1, n3)
+        tick(*(PLAN[f"part{part}"] if part else (PART0,)))
+    home = [pltpu.make_async_copy(b, a, away_sems.at[k]) for k, (a, b) in enumerate(away)]
+    for copy in home[:2]:
+        copy.start()
+
+    def conv_back(i):
+        write_mask(edges[i], mask)
+        stage_b5(i, sens, bb2, fp, g3, fl, resid, sm_b, mask, branch, rear)
+        stage_b8(i, act, stats, bg, bo, fl, st2, resid, vh3, sm_b, mask, plane, plane2)
+
+    image_loop(conv_back, PLAN["conv_back"])
+    home[2].start()
     out_copies = [pltpu.make_async_copy(sens, lout, out_sems.at[0])]
     out_copies[0].start()
-
-    def conv_back(i, _):
-        write_mask(edges[i], mask)
-        stage_b8(i, act, stats, bg, bo, fl, st2, resid, vh3, sm_b, mask, plane, plane2)
-        return 0
-
-    lax.fori_loop(0, images // 2, conv_back, 0)
-    tick(4, 5)
-    lax.fori_loop(images // 2, images, conv_back, 0)
     for k in range(15):
         put_small(small, k, total(sm_b[k]))
     for j in range(4):
@@ -822,44 +852,43 @@
     push_all(place, lambda device: payload.at[1], gathered.at[1, me], push_sems.at[1])
     gathered[1, me] = payload[1]
     land_all(gathered.at[1, pl.ds(0, n - 1)], push_sems.at[1])
-    summed = lax.fori_loop(0, n, lambda k, carry: carry + gathered[1, k], zeros(8, L))
+    tick(*PLAN["exchange"])
+    for copy in home:
+        copy.wait()
+    summed = jnp.sum(gathered[1], axis=0)
     for k in range(2):
         bsums[k : k + 1, :] = jnp.concatenate([summed[3 * k + c : 3 * k + c + 1] for c in range(3)], axis=1)
 
-    def rear1(i, _):
+    def rear1(i):
         write_mask(edges[i], mask)
         stage_c1(i, act, slope, vh3, stats, bsums, bg, sm_c, mask, plane2)
         stage_c2(i, vh2, g2, b2, st1, sm_c, mask, plane2, back)
         stage_c3(i, resid, vh2, r2, fm, g2, sm_c, mask, back, slope)
-        return 0
-
-    tick(4, 5)
-    lax.fori_loop(0, images // 2, rear1, 0)
-    tick(4, 5, 2, 3)
-    lax.fori_loop(images // 2, images, rear1, 0)
+
+    image_loop(rear1, PLAN["rear1"])
+
+    def rear2(i):
+        stage_c5a(i, wm, qkv, score, smq, sharp_mask, slope, pmat, vh3)
+
+    image_loop(rear2, PLAN["rear2"])
     stage_c4(mixed, dwm, slope)
-
-    def rear2(i, _):
-        stage_c4b(i, wm, slope)
-        stage_c5(i, qkv, score, sqk, srow, sharp_mask, slope, pmat, alow, cqk)
-        stage_c6(i, qkv, smq, slope, pmat, alow, cqk)
-        return 0
-
-    lax.fori_loop(0, images // 4, rear2, 0)
-    tick(4, 5, 2, 3)
-    lax.fori_loop(images // 4, images // 2, rear2, 0)
-    tick(2, 3)
-    lax.fori_loop(images // 2, images, rear2, 0)
-    tick(4, 5)
-    stage_c7(n1, qkv, dwq, dwk, dwv)
-    tick(4, 5, 2, 3, 0, 1)
-
-    def rear3(i, _):
+    stage_c7(2, n1, qkv, dwv)
+    tick(*PLAN["value"])
+
+    def rear3(i):
+        stage_c5b(i, score, sqk, srow, sharp_mask, vh3, alow, cqk)
+        stage_c6(i, qkv, smq, pmat, alow, cqk)
+
+    image_loop(rear3, PLAN["rear3"])
+    stage_c7(0, n1, qkv, dwq)
+    stage_c7(1, n1, qkv, dwk)
+    tick(*PLAN["query"])
+
+    def rear4(i):
         write_mask(edges[i], mask)
         stage_c8(i, x, g1, wqkv, resid, sm_c, mask, qkv)
-        return 0
-
-    lax.fori_loop(0, images, rear3, 0)
+
+    image_loop(rear4, PLAN["rear4"])
     out_copies.append(pltpu.make_async_copy(x, gin, out_sems.at[1]))
     out_copies[1].start()
     for k in range(15):
@@ -868,25 +897,42 @@
         put_small(small, 34 + p, total(smq[:, p * D : (p + 1) * D]))
     put_small(small, 37, srow[...])
 
+    weights = [(grads.at[p * D : (p + 1) * D, :], dwqkv_out.at[:, p * D : (p + 1) * D]) for p in range(3)]
+    weights.append((dwm, dwm_out))
+    weights += [(act.at[j, 0:D, :], dw1_out.at[:, j * D : (j + 1) * D]) for j in range(4)]
+    weights += [(second[part], dw2_out.at[part * FP : (part + 1) * FP, :]) for part in range(FF // FP)]
+    weights = [pltpu.make_async_copy(a, b, out_sems.at[2 + k]) for k, (a, b) in enumerate(weights)]
+    out_copies += weights
+    later_weights = weights[:4]
+
+    def complete(which):
+        return all(streams[k].done > streams[k].last for k in which)
+
     push_all(place, lambda device: small.at[rows(device * 8, 8), :], gathered.at[0, me], push_sems.at[2])
     gathered[0, me] = small[rows(me * 8, 8), :]
-    tick(0, 1, 4, 5, 2, 3)
-    land_all(gathered.at[0, pl.ds(0, n - 1)], push_sems.at[2])
-    gathered[1, me] = lax.fori_loop(0, n, lambda k, carry: carry + gathered[0, k], zeros(8, L))
-    push_all(place, lambda device: gathered.at[1, me], gathered.at[1, me], push_sems.at[3])
-    for k in range(streams[0].last):
-        tick(0, 1, 4, 5, 2, 3)
+    tick(*PLAN["small"])
+    fed = False
+    rounds = 0
+    while not complete(range(len(streams))):
+        if not fed and complete(PART0 + PART1 + PART2):
+            fed = True
+            for u in range(FF // L):
+                block, col = divmod(u * L, D)
+                part, row = divmod(u * L, FP)
+                act[block, 0:D, col : col + L] = first[part][row : row + L, :].T
+            for copy in weights[4:]:
+                copy.start()
+        tick(*PLAN["end"])
+        rounds += 1
+        if rounds == 3:
+            land_all(gathered.at[0, pl.ds(0, n - 1)], push_sems.at[2])
+            gathered[1, me] = jnp.sum(gathered[0], axis=0)
+            push_all(place, lambda device: gathered.at[1, me], gathered.at[1, me], push_sems.at[3])
+    for copy in later_weights:
+        copy.start()
     land_all(gathered.at[1, pl.ds(0, n - 1)], push_sems.at[3])
     for k in range(16):
         small[8 * k : 8 * k + 8, :] = gathered[1, k]
-
-    weights = [(grads.at[p * D : (p + 1) * D, :], dwqkv_out.at[:, p * D : (p + 1) * D]) for p in range(3)]
-    weights.append((dwm, dwm_out))
-    weights += [(grads.at[(4 + j) * D : (5 + j) * D, :], dw1_out.at[:, j * D : (j + 1) * D]) for j in range(4)]
-    weights.append((dw2, dw2_out))
-    for k, (a, b) in enumerate(weights):
-        out_copies.append(pltpu.make_async_copy(a, b, out_sems.at[2 + k]))
-        out_copies[-1].start()
 
     def branch_factor(weight, grad, bias, bias_grad, factor):
         return (total(weight.astype(F32) * grad) + bias * bias_grad) / factor
@@ -895,7 +941,8 @@
     picked.append(branch_factor(wm[...], dwm[...], bm[...], picked[19 + 4], fm[...]))
     local = sum(st2[a, b : b + 1, :] * picked[4 + 3 * a + b] for a in range(3) for b in range(3))
     picked.append((local + cb2[...] * picked[3]) / fl[...])
-    picked.append(branch_factor(w2[...], dw2[...], bb2[...], picked[2], fp[...]))
+    mlp = sum(total(w2[part * FP : (part + 1) * FP, :].astype(F32) * second[part][...]) for part in range(FF // FP))
+    picked.append((mlp + bb2[...] * picked[2]) / fp[...])
     lane = lax.broadcasted_iota(jnp.int32, (1, D), 1)
     by_head = zeros(1, D)
     for h in range(HEADS):
@@ -913,25 +960,28 @@
 
 def deliver_kernel(*refs):
     small, outs, stage, sems = refs[6], refs[7:-7], refs[-7:-1], refs[-1]
-    loads = [pltpu.make_async_copy(refs[k], stage[k], sems.at[0, k]) for k in range(6)]
-    copies = [pltpu.make_async_copy(stage[k], outs[k], sems.at[1, k]) for k in range(6)]
+    parts = []
+    for k in range(6):
+        parts.append((k, pl.ds(0, refs[k].shape[0])))
+    loads = [pltpu.make_async_copy(refs[k].at[at], stage[k].at[at], sems.at[0, q]) for q, (k, at) in enumerate(parts)]
     for load in loads:
         load.start()
-    qkv_bias, hidden_bias, sharp_grad, conv1, conv2 = outs[6:11]
-    for p in range(3):
-        qkv_bias[p * D : (p + 1) * D] = small[34 + p : 35 + p, :].reshape(D)
-    for j in range(4):
-        hidden_bias[j * D : (j + 1) * D] = small[15 + j : 16 + j, :].reshape(D)
+    sharp_grad, conv1, conv2, qkv_bias, hidden_bias = outs[6:11]
     sharp_grad[...] = small[41:42, :].reshape(D)[0:HEADS]
     for a in range(3):
         for b in range(3):
             conv2[a, b : b + 1, :] = small[4 + 3 * a + b : 5 + 3 * a + b, :]
             conv1[a, b : b + 1, :] = small[24 + 3 * a + b : 25 + 3 * a + b, :]
-    for k, out in zip(SINGLES, outs[11:]):
-        out[...] = small[k : k + 1, :].reshape(D)
-    for load, copy in zip(loads, copies):
-        load.wait()
+    pairs = [(small.at[34 + p], qkv_bias.at[pl.ds(p * D, D)]) for p in range(3)]
+    pairs += [(small.at[15 + j], hidden_bias.at[pl.ds(j * D, D)]) for j in range(FF // D)]
+    pairs += [(small.at[k], out) for k, out in zip(SINGLES, outs[11:])]
+    copies = [pltpu.make_async_copy(a, b, sems.at[1, len(parts) + k]) for k, (a, b) in enumerate(pairs)]
+    for copy in copies:
         copy.start()
+    for q, (k, at) in enumerate(parts):
+        loads[q].wait()
+        copies.append(pltpu.make_async_copy(stage[k].at[at], outs[k].at[at], sems.at[1, q]))
+        copies[-1].start()
     for copy in copies:
         copy.wait()
 
@@ -945,27 +995,27 @@
     sm = pl.BlockSpec(memory_space=pltpu.SMEM)
     hbm = pl.BlockSpec(memory_space=pl.ANY)
     full = (images, T, D)
-    small_rows = max(16 * 8, 8 * n)
     dma = pltpu.SemaphoreType.DMA
     copies = stream_shape(n, stream_steps(n, True), FF)[1]
-    lout, gin, dwqkv, dwm, dw1, dw2, small = pl.pallas_call(
+    lout, gin, dwqkv, dwm, dw1, dw2, small, *_ = pl.pallas_call(
         lambda *refs: mega_kernel(n, images, refs),
-        in_specs=[sm, sm, hbm, hbm, vm, vm, hbm, hbm, vm, vm] + [vm] * 17,
-        out_specs=[hbm] * 6 + [vm],
+        in_specs=[sm, sm] + [hbm] * 25,
+        out_specs=[hbm] * 6 + [vm] + [hbm] * 3,
         out_shape=[S(full, BF16), S(full, BF16), S((D, 3 * D), F32), S((D, D), F32), S((D, FF), F32), S((FF, D), F32),
-                   S((48, D), F32)],
+                   S((48, D), F32), S(full, BF16), S(full, BF16), S(full, F32)],
         scratch_shapes=[
-            V((24, FF), F32), V(full, BF16), V(full, BF16), V((D, FF), BF16), V((FF, D), BF16),
+            V((24, FF), F32), V(full, BF16), V(full, BF16), V((D, 3 * D), BF16), V((D, D), BF16),
+            V((D, FF), BF16), V((FF, D), BF16), V((3, 3, D), F32), V((3, 3, D), F32),
             V(full, BF16), V((images, T, 3 * D), BF16), V(full, BF16),
             V((images, D, D), F32), V((images, 2, 8, D), F32),
             V((images, T, L), F32), V(full, F32), V(full, F32), V(full, F32), V(full, F32),
             V(full, BF16), V((images, 8, D), F32), V((8, D), F32), V((8, D), F32), V((8, D), F32),
             V((T, L), F32), V((D, D), F32), V((D, D), BF16), V((D, D), BF16), V((3, PLANE, L), F32), V((3, PLANE, L), F32),
-            V((T, L), F32), V((T, D), BF16), V((T, D), BF16), V((T, FF), BF16), V((T, FF), BF16),
+            V((images, T, FP), BF16), V((images, T, FP), BF16),
             V((15, 8, D), F32), V((8, FF), F32), V((15, 8, D), F32), V((8, 3 * D), F32), V((1, D), F32),
-            V((4 * D + 2 * FF, D), F32), V((sum(stream_rows(n, STREAMS)), D), F32),
-            V((small_rows, L), F32), V((2, 8, L), F32), V((2, n, 8, L), F32),
-            dma((images + 3,)), dma((11,)), dma((len(STREAMS), 4, copies)),
+            V((4 * D + 2 * FF, D), F32), V((sum(stream_rows(n)), D), F32),
+            V((8 * n, L), F32), V((2, 8, L), F32), V((2, n, 8, L), F32),
+            dma((images + 24,)), dma((13,)), dma((3,)), dma((len(STREAMS), 4, copies)),
             pltpu.SemaphoreType.REGULAR((len(STREAMS), 4)), dma((4, 2)),
         ],
         compiler_params=pltpu.CompilerParams(
@@ -975,14 +1025,14 @@
 
     vector = S((D,), F32)
     stencil_shape = S((3, 3, D), F32)
-    (lout, gin, dwqkv, dwm, dw1, dw2, qkv_bias, hidden_bias, sharp_grad, conv1, conv2, *singles) = pl.pallas_call(
+    (lout, gin, dwqkv, dwm, dw1, dw2, sharp_grad, conv1, conv2, qkv_bias, hidden_bias, *singles) = pl.pallas_call(
         deliver_kernel,
         in_specs=[hbm] * 6 + [vm],
-        out_specs=[hbm] * 6 + [vm] * (5 + len(SINGLES)),
+        out_specs=[hbm] * 6 + [vm] * 3 + [hbm] * (2 + len(SINGLES)),
         out_shape=[S(v.shape, v.dtype) for v in (lout, gin, dwqkv, dwm, dw1, dw2)]
-        + [S((3 * D,), F32), S((FF,), F32), S((HEADS,), F32), stencil_shape, stencil_shape]
+        + [S((HEADS,), F32), stencil_shape, stencil_shape, S((3 * D,), F32), S((FF,), F32)]
         + [vector] * len(SINGLES),
-        scratch_shapes=[V(v.shape, v.dtype) for v in (lout, gin, dwqkv, dwm, dw1, dw2)] + [dma((2, 6))],
+        scratch_shapes=[V(v.shape, v.dtype) for v in (lout, gin, dwqkv, dwm, dw1, dw2)] + [dma((2, 13 + len(SINGLES)))],
         compiler_params=pltpu.CompilerParams(vmem_limit_bytes=62 * 1024 * 1024),
     )(lout, gin, dwqkv, dwm, dw1, dw2, small)
     one = dict(zip(SINGLES, singles))

time: 175 us -> 171 us (0.977)
  Pallas kernels: 173 us -> 170 us
    pallas_call x1, Pallas kernels: 164 us -> 160 us  [on_device(): pl.pallas_call(lambda *refs: mega_kernel(n, images, refs), in_specs=[sm,...]
where the time goes in v4:
time: 171 us
  Pallas kernels  170 us (99%)
    pallas_call x1, Pallas kernels, on_device(): pl.pallas_call(lambda *refs: mega_kernel(n, images, refs), in_specs=[sm,...  160 us
    pallas_call x1, Pallas kernels, on_device(): pl.pallas_call(deliver_kernel, in_specs=[hbm] * 6 + [vm], out_specs=[hbm]...  9.8 us

profile of v4, /device:TPU:0, one launch (start us, length us, event | category | flops | bytes accessed | tf_op | source)
XLA Modules:
  0.0 170.7 jit_solution(14727681331192561376)
XLA Ops:
  0.7 160.0 %shard_map.458 = (bf16[4,576,384]{2,1,0:T(8,128)(2,1)}, bf16[4,576,384]{2,1,0:T(8,128)(2,1)}, f32[384,1152]{1,0:T(8,128)}, f32[384,384]{1,0:T(8,128)}, f32[384,1...) custom-call(s32[4]{0:T(128)} %refs_0_.1, ...), custom_call_target="tpu_custom_call" | custom-call | tf_op jit(solution)/shard_map/pallas_call | solution.py:1000
  160.7 9.8 %shard_map.459 = (bf16[4,576,384]{2,1,0:T(8,128)(2,1)}, bf16[4,576,384]{2,1,0:T(8,128)(2,1)}, f32[384,1152]{1,0:T(8,128)}, f32[384,384]{1,0:T(8,128)}, f32[384,1...) custom-call(bf16[4,576,384]{2,1,0:T(8,128)(2,1)} %get-tuple-element., ...), custom_call_target="tpu_custom_call" | custom-call | tf_op jit(solution)/shard_map/pallas_call | solution.py:1028

commit v5 on v4

--- a/solution.py
+++ b/solution.py
@@ -523,7 +523,7 @@
 
 
 STREAMS = ((512, True), (512, False), (512, True), (512, True), (512, True), (512, True), (512, False), (512, True), (512, True))
-TAIL, PART0, PART1, PART2 = (0, 1, 2), (3, 4), (5, 6), (7, 8)
+TAIL, LAST, PART0, PART1, PART2 = (0, 1), (2,), (3, 4), (5, 6), (7, 8)
 
 
 def stream_shape(n, steps, size):
@@ -549,12 +549,12 @@
     "exchange": (PART0, PART1, PART2,),
     "rear1": {},
     "rear2": {0: (PART2,), 1: (PART0,), 2: (PART1,)},
-    "value": (PART0, PART2,),
-    "rear3": {},
+    "value": (PART0, PART2, LAST),
+    "rear3": {2: (LAST,)},
     "query": (TAIL, PART1,),
-    "rear4": {0: (PART2,), 2: (TAIL,), 3: (PART1,)},
+    "rear4": {0: (PART2,), 1: (LAST,), 2: (TAIL,), 3: (PART1,)},
     "small": (PART2,),
-    "end": (PART0, PART1, PART2, TAIL),
+    "end": (TAIL, LAST, PART0, PART1, PART2),
 }
 
 

time: 171 us -> 173 us (1.012)
  Pallas kernels: 170 us -> 172 us
    pallas_call x1, Pallas kernels: 160 us -> 163 us  [on_device(): pl.pallas_call(lambda *refs: mega_kernel(n, images, refs), in_specs=[sm,...]
where the time goes in v5:
time: 173 us
  Pallas kernels  172 us (99%)
    pallas_call x1, Pallas kernels, on_device(): pl.pallas_call(lambda *refs: mega_kernel(n, images, refs), in_specs=[sm,...  163 us
    pallas_call x1, Pallas kernels, on_device(): pl.pallas_call(deliver_kernel, in_specs=[hbm] * 6 + [vm], out_specs=[hbm]...  9.8 us

profile of v5, /device:TPU:0, one launch (start us, length us, event | category | flops | bytes accessed | tf_op | source)
XLA Modules:
  0.0 173.3 jit_solution(2996093407743794238)
XLA Ops:
  0.7 162.6 %shard_map.458 = (bf16[4,576,384]{2,1,0:T(8,128)(2,1)}, bf16[4,576,384]{2,1,0:T(8,128)(2,1)}, f32[384,1152]{1,0:T(8,128)}, f32[384,384]{1,0:T(8,128)}, f32[384,1...) custom-call(s32[4]{0:T(128)} %refs_0_.1, ...), custom_call_target="tpu_custom_call" | custom-call | tf_op jit(solution)/shard_map/pallas_call | solution.py:1000
  163.3 9.8 %shard_map.459 = (bf16[4,576,384]{2,1,0:T(8,128)(2,1)}, bf16[4,576,384]{2,1,0:T(8,128)(2,1)}, f32[384,1152]{1,0:T(8,128)}, f32[384,384]{1,0:T(8,128)}, f32[384,1...) custom-call(bf16[4,576,384]{2,1,0:T(8,128)(2,1)} %get-tuple-element., ...), custom_call_target="tpu_custom_call" | custom-call | tf_op jit(solution)/shard_map/pallas_call | solution.py:1028
